TPU v7x, 512 devices: a whole 4x8x8 slice. The times are simulated.
512 devices in a mesh: dp: 8 (over x, core), ctx: 8 (over z), tp: 8 (over y).
Axes of the slice: x: 4, y: 8, z: 8, core: 2. Of those that a mesh axis runs over, the one named last changes fastest.
Arguments:
- tokens: bfloat16 [4096, 4096], P(('dp', 'ctx', 'tp')), may hold values from -6 to 6
- routes: int32 [4096, 2], P(('dp', 'ctx', 'tp')), may hold values from 0 to 63, all different within a row; in each aligned block of 64 rows (0 to 63, 64 to 127, ...) at most 2 rows name the same one
- gate_weights: float32 [4096, 2], P(('dp', 'ctx', 'tp')), may hold values from 0.2 to 1
- seq_ids: int32 [4096], P(('dp', 'ctx', 'tp')), may hold values from 0 to 127, never falling along the last dimension, each value on 1 to 64 neighbouring positions
- log_ratio: float32 [4096], P(('dp', 'ctx', 'tp')), may hold values from -0.5 to 0.9
- advantage: float32 [128], replicated, may hold values from -4 to 4
- upstream: bfloat16 [4096, 4096], P(('dp', 'ctx', 'tp')), may hold values from -6 to 6
- w_gate: bfloat16 [64, 4096, 1024], P(('dp', 'ctx'), None, 'tp'), may hold values from -0.09375 to 0.09375
- w_up: bfloat16 [64, 4096, 1024], P(('dp', 'ctx'), None, 'tp'), may hold values from -0.09375 to 0.09375
- w_down: bfloat16 [64, 1024, 4096], P(('dp', 'ctx'), 'tp'), may hold values from -0.1875 to 0.1875
Outputs:
- mixed: bfloat16 [4096, 4096], P(('dp', 'ctx', 'tp'))
- grad_tokens: bfloat16 [4096, 4096], P(('dp', 'ctx', 'tp'))
- grad_gates: float32 [4096, 2], P(('dp', 'ctx', 'tp'))
Inputs may be any that keep to these rules, and one draw needn't show every extreme that they name: `routes`: A row's 2 ids differ. In each aligned block of 64 rows no expert is named more than 2 times, a bound that some block reaches. `seq_ids`: never falling; every sequence has 1 to 64 tokens, one exactly 64.
All inputs are finite; a program needn't handle non-finite values.
Results may differ from a plain program's by a relative error of at most 0.025.
Values may be sent and summed in bfloat16 or wider, within the bound.
No kernel may reach another device: no remote copies, remote signals or barrier semaphores. Data moves between devices by JAX's collectives and lax.ppermute only.
A program may use at most 64 MiB of HBM per device.

v0:
```python
import jax
import jax.numpy as jnp
from jax import lax
from jax.sharding import PartitionSpec as P

CLIP_HIGH = 1.2
HIGHEST = lax.Precision.HIGHEST


def slot_layout(route_group, experts, capacity):
    flattened = route_group.reshape(-1)
    one_hot = (flattened[:, None] == jnp.arange(experts, dtype=jnp.int32)[None, :]).astype(
        jnp.int32
    )
    earlier = jnp.cumsum(one_hot, axis=0) - one_hot
    position = jnp.sum(earlier * one_hot, axis=1)
    return (flattened * capacity + position).reshape(route_group.shape)


def group_rows(local_rows):
    return lax.all_gather(local_rows, "tp", axis=0, tiled=True)


def send_slots(buffer):
    return lax.all_to_all(buffer, ("dp", "ctx"), split_axis=0, concat_axis=0, tiled=True)


def contract_last(left, right):
    return lax.dot_general(
        left, right, (((1,), (1,)), ((), ())), preferred_element_type=jnp.float32
    )


def per_device(
    tokens, routes, gate_weights, seq_ids, log_ratio, advantage, upstream, w_gate, w_up, w_down
):
    tok_local, model_width = tokens.shape
    top_count = routes.shape[1]
    experts = lax.axis_size("dp") * lax.axis_size("ctx")
    tok_group = tok_local * lax.axis_size("tp")
    capacity = max(2, 5 * tok_group * top_count // (4 * experts))
    slot_count = experts * capacity
    gate_local = w_gate[0]
    up_local = w_up[0]
    down_local = w_down[0]
    seq_count = advantage.shape[0]
    member = (seq_ids[:, None] == jnp.arange(seq_count, dtype=jnp.int32)[None, :]).astype(
        jnp.float32
    )
    seq_sums = jnp.dot(log_ratio, member, precision=HIGHEST)
    counts = jnp.sum(member, axis=0)
    seq_sums, counts = lax.psum((seq_sums, counts), ("dp", "ctx", "tp"))
    route_group, weight_group = (
        lax.all_gather(routes, "tp", axis=0, tiled=True),
        lax.all_gather(gate_weights, "tp", axis=0, tiled=True),
    )
    slot_index = slot_layout(route_group, experts, capacity)
    flat_index = slot_index.reshape(-1)
    selector = jnp.sum(
        (slot_index[None, :, :] == jnp.arange(slot_count, dtype=jnp.int32)[:, None, None]).astype(
            jnp.float32
        ),
        axis=2,
    ).astype(jnp.bfloat16)
    token_group = group_rows(tokens)
    token_slots = jnp.dot(selector, token_group, preferred_element_type=jnp.float32).astype(
        jnp.bfloat16
    )
    arrived_tokens = send_slots(token_slots.reshape(experts, capacity, -1)).reshape(slot_count, -1)
    gate_pre = jnp.dot(arrived_tokens, gate_local, preferred_element_type=jnp.float32)
    up_pre = jnp.dot(arrived_tokens, up_local, preferred_element_type=jnp.float32)
    squash = jax.nn.sigmoid(gate_pre)
    activated = gate_pre * squash
    hidden = (activated * up_pre).astype(jnp.bfloat16)
    expert_part = jnp.dot(hidden, down_local, preferred_element_type=jnp.float32).astype(
        jnp.bfloat16
    )
    part_back = lax.all_to_all(
        expert_part.reshape(experts, capacity, model_width),
        ("dp", "ctx"),
        split_axis=0,
        concat_axis=0,
        tiled=True,
    )
    gathered = jnp.take(part_back.reshape(slot_count, model_width), flat_index, axis=0).reshape(
        tok_group, top_count, model_width
    )
    output_group = jnp.sum(gathered.astype(jnp.float32) * weight_group[:, :, None], axis=1)
    mixed = lax.psum_scatter(output_group, "tp", scatter_dimension=0, tiled=True).astype(
        jnp.bfloat16
    )
    weight = advantage * jnp.minimum(jnp.exp(seq_sums / counts), CLIP_HIGH)
    token_weight = jnp.dot(member, weight, precision=HIGHEST)
    cotangent = (upstream.astype(jnp.float32) * token_weight[:, None]).astype(jnp.bfloat16)
    cotangent_group = group_rows(cotangent)
    cotangent_slots = jnp.dot(selector, cotangent_group, preferred_element_type=jnp.float32).astype(
        jnp.bfloat16
    )
    arrived_grads = send_slots(cotangent_slots.reshape(experts, capacity, -1)).reshape(
        slot_count, -1
    )
    d_hidden = contract_last(arrived_grads, down_local)
    gate_terms = jnp.einsum(
        "sd,sd->s", arrived_grads, expert_part, preferred_element_type=jnp.float32
    )
    grad_in_gate = (d_hidden * up_pre * squash * (1.0 + gate_pre * (1.0 - squash))).astype(
        jnp.bfloat16
    )
    grad_in_up = (d_hidden * activated).astype(jnp.bfloat16)
    input_part = (
        contract_last(grad_in_gate, gate_local) + contract_last(grad_in_up, up_local)
    ).astype(jnp.bfloat16)
    input_back, terms_back = (
        lax.all_to_all(
            input_part.reshape(experts, capacity, model_width),
            ("dp", "ctx"),
            split_axis=0,
            concat_axis=0,
            tiled=True,
        ),
        lax.all_to_all(
            gate_terms.astype(jnp.bfloat16).reshape(experts, capacity),
            ("dp", "ctx"),
            split_axis=0,
            concat_axis=0,
            tiled=True,
        ),
    )
    gathered_grad = jnp.take(
        input_back.reshape(slot_count, model_width), flat_index, axis=0
    ).reshape(tok_group, top_count, model_width)
    input_group = jnp.sum(gathered_grad.astype(jnp.float32) * weight_group[:, :, None], axis=1)
    gates_group = (
        jnp.take(terms_back.reshape(slot_count), flat_index, axis=0)
        .reshape(tok_group, top_count)
        .astype(jnp.float32)
    )
    grad_tokens = lax.psum_scatter(input_group, "tp", scatter_dimension=0, tiled=True)
    gates_total = lax.psum(gates_group, "tp")
    grad_gates = lax.dynamic_slice_in_dim(
        gates_total, lax.axis_index("tp") * tok_local, tok_local, 0
    )
    return (mixed, grad_tokens.astype(jnp.bfloat16), grad_gates)


def solution(mesh):
    in_specs = (
        P(("dp", "ctx", "tp"), None),
        P(("dp", "ctx", "tp"), None),
        P(("dp", "ctx", "tp"), None),
        P(("dp", "ctx", "tp")),
        P(("dp", "ctx", "tp")),
        P(),
        P(("dp", "ctx", "tp"), None),
        P(("dp", "ctx"), None, "tp"),
        P(("dp", "ctx"), None, "tp"),
        P(("dp", "ctx"), "tp", None),
    )
    out_specs = (
        P(("dp", "ctx", "tp"), None),
        P(("dp", "ctx", "tp"), None),
        P(("dp", "ctx", "tp"), None),
    )
    return jax.shard_map(
        per_device, mesh=mesh, in_specs=in_specs, out_specs=out_specs, check_vma=False
    )
```

profile of v0, /device:TPU:2, one launch (start us, length us, event | category | flops | bytes accessed | tf_op | source)
XLA Modules:
  0.0 430.4 jit_solution(14626573806312310017)
XLA Ops:
  7.2 17.1 %all-gather = s32[8,8,2]{1,2,0:T(2,128)S(1)} all-gather(s32[1,8,2]{1,2,0:T(2,128)} %bitcast.46), channel_id=1, replica_groups=mesh['dp'=8,'ctx'=8,'tp'=8] {'tp'}, dimensions={0}, use_global_device_ids=true | all-gather | bytes 576 | tf_op jit(solution)/shard_map/all_gather | solution.py:54
  25.4 25.8 %all_gather.13 = bf16[64,4096]{1,0:T(8,128)(2,1)S(1)} all-gather(bf16[8,4096]{1,0:T(8,128)(2,1)} %param.12), channel_id=1, replica_groups=mesh['dp'=8,'ctx'=8,'tp'=8] {'tp'}, dimensions={0}, use_global_device_ids=true | all-gather | bytes 589824 | tf_op jit(solution)/shard_map/all_gather | solution.py:21
  51.2 0.5 convolution_convert_fusion.2
  51.7 1.5 reshape.98
  53.2 13.9 %all-to-all-start = ((bf16[64,2,4096]{2,1,0:T(2,128)(2,1)}), bf16[64,2,4096]{2,1,0:T(2,128)(2,1)S(1)}, u32[]{:S(2)}, u32[]{:S(2)}) async-start(bf16[64,2,4096]{2,1,0:T(2,128)(2,1)} %reshape.98), calls=%async_computation | async-start | bytes 2097152 | tf_op jit(solution)/shard_map/all_to_all | solution.py:25
  67.4 113.7 %all-reduce = (f32[128]{0:T(128)S(1)}, f32[128]{0:T(128)S(1)}) all-reduce(f32[128]{0:T(128)S(1)} %convolution_bitcast_fusion.1, f32[128]{0:T(128)S(1)} %convert_reduce_fusion.1), channel_id=1, replica_groups=mesh['dp'=8,'ctx'=8,'tp'=8] {'dp','ctx','tp'}, use_global_device_ids=true, to_apply=%region_5.7 | all-reduce | flops 256 | bytes 2048 | tf_op jit(solution)/shard_map/psum | solution.py:52
  181.4 25.3 %all_gather.15 = bf16[64,4096]{1,0:T(8,128)(2,1)S(1)} all-gather(bf16[8,4096]{1,0:T(8,128)(2,1)S(1)} %multiply_convert_fusion), channel_id=1, replica_groups=mesh['dp'=8,'ctx'=8,'tp'=8] {'tp'}, dimensions={0}, use_global_device_ids=true | all-gather | bytes 589824 | tf_op jit(solution)/shard_map/all_gather | solution.py:21
  206.7 0.5 convolution_convert_fusion
  207.2 1.5 reshape.102
  208.7 1.0 copy-done.2
  209.7 8.9 %all-to-all-start.2 = ((bf16[64,2,4096]{2,1,0:T(2,128)(2,1)}), bf16[64,2,4096]{2,1,0:T(2,128)(2,1)}, u32[]{:S(2)}, u32[]{:S(2)}) async-start(bf16[64,2,4096]{2,1,0:T(2,128)(2,1)} %reshape.102), calls=%async_computation.3 | async-start | bytes 2097152 | tf_op jit(solution)/shard_map/all_to_all | solution.py:25
  218.6 1.5 reshape.99
  220.1 0.4 fusion.10
  220.6 0.8 copy-done.3
  221.4 0.4 fusion.6
  221.8 25.3 %all-to-all-done.2 = bf16[64,2,4096]{2,1,0:T(2,128)(2,1)} async-done(((bf16[64,2,4096]{2,1,0:T(2,128)(2,1)}), bf16[64,2,4096]{2,1,0:T(2,128)(2,1)}, u32[]{:S(2)}, u32[]{:S(2)}) %all-to-all-start.2) | async-done | bytes 1048608 | tf_op jit(solution)/shard_map/all_to_all | solution.py:25
  247.1 1.5 reshape.103
  248.6 1.4 fusion.1
  250.0 2.5 reshape.100
  252.5 6.6 %all-to-all-start.1 = ((bf16[64,2,4096]{2,1,0:T(2,128)(2,1)}), bf16[64,2,4096]{2,1,0:T(2,128)(2,1)}, u32[]{:S(2)}, u32[]{:S(2)}) async-start(bf16[64,2,4096]{2,1,0:T(2,128)(2,1)} %reshape.100), calls=%async_computation.1 | async-start | bytes 2097152 | tf_op jit(solution)/shard_map/all_to_all | solution.py:78
  259.1 0.4 fusion.2
  259.6 0.4 fusion.8
  260.0 0.8 copy-done.4
  260.8 0.4 fusion
  261.3 1.5 reshape.104
  262.8 24.8 %all-to-all-done.1 = bf16[64,2,4096]{2,1,0:T(2,128)(2,1)} async-done(((bf16[64,2,4096]{2,1,0:T(2,128)(2,1)}), bf16[64,2,4096]{2,1,0:T(2,128)(2,1)}, u32[]{:S(2)}, u32[]{:S(2)}) %all-to-all-start.1) | async-done | bytes 1048608 | tf_op jit(solution)/shard_map/all_to_all | solution.py:78
  287.6 6.6 %all-to-all-start.3 = ((bf16[64,2,4096]{2,1,0:T(2,128)(2,1)}), bf16[64,2,4096]{2,1,0:T(2,128)(2,1)}, u32[]{:S(2)}, u32[]{:S(2)}) async-start(bf16[64,2,4096]{2,1,0:T(2,128)(2,1)} %reshape.104), calls=%async_computation.4 | async-start | bytes 2097152 | tf_op jit(solution)/shard_map/all_to_all | solution.py:114
  294.2 14.1 %all-gather.1 = f32[8,8,2]{1,2,0:T(2,128)S(1)} all-gather(f32[1,8,2]{1,2,0:T(2,128)S(1)} %bitcast.47), channel_id=1, replica_groups=mesh['dp'=8,'ctx'=8,'tp'=8] {'tp'}, dimensions={0}, use_global_device_ids=true | all-gather | bytes 576 | tf_op jit(solution)/shard_map/all_gather | solution.py:55
  308.4 1.5 reshape.101
  309.9 1.2 gather_fusion.1
  311.1 11.5 %all-to-all-done.3 = bf16[64,2,4096]{2,1,0:T(2,128)(2,1)} async-done(((bf16[64,2,4096]{2,1,0:T(2,128)(2,1)}), bf16[64,2,4096]{2,1,0:T(2,128)(2,1)}, u32[]{:S(2)}, u32[]{:S(2)}) %all-to-all-start.3) | async-done | bytes 1048608 | tf_op jit(solution)/shard_map/all_to_all | solution.py:114
  322.6 1.5 reshape.105
  324.1 2.2 gather_fusion.2
  326.2 3.5 select_convert_fusion.1
  329.8 2.5 reshape.107
  332.3 3.5 reshape.108
  335.7 8.3 %multiply_reduce_fusion = (f32[64,4096]{1,0:T(8,128)}, f32[64,4096]{1,0:T(8,128)}) fusion(f32[64,2,4096]{2,1,0:T(2,128)} %reshape.108, f32[64,2]{1,0:T(8,128)S(1)} %bitcast.45, f32[64,2,4096]{2,1,0:T(2,128)S(1)} %reshape.107), kind=kLoop, calls=%fused_computation.10 | loop fusion | flops 1572864 | bytes 6291968 | tf_op jit(solution)/shard_map/reduce_sum | solution.py:132
  344.1 0.7 reduce-scatter.3.cloned.1.call-update
  345.1 0.8 all_to_all.24
  345.9 6.4 %all-to-all-start.4 = ((bf16[64,1,2]{2,1,0:T(2,128)(2,1)}), bf16[64,1,2]{2,1,0:T(2,128)(2,1)S(1)}, u32[]{:S(2)}, u32[]{:S(2)}) async-start(bf16[64,1,2]{2,1,0:T(2,128)(2,1)} %all_to_all.24), calls=%async_computation.6 | async-start | bytes 65536 | tf_op jit(solution)/shard_map/all_to_all | solution.py:121
  352.3 8.6 %all-to-all-done.4 = bf16[64,1,2]{2,1,0:T(2,128)(2,1)S(1)} async-done(((bf16[64,1,2]{2,1,0:T(2,128)(2,1)}), bf16[64,1,2]{2,1,0:T(2,128)(2,1)S(1)}, u32[]{:S(2)}, u32[]{:S(2)}) %all-to-all-start.4) | async-done | bytes 288 | tf_op jit(solution)/shard_map/all_to_all | solution.py:121
  361.1 1.2 gather_fusion
  362.6 14.7 %psum.23 = f32[64,2]{0,1:T(2,128)S(1)} all-reduce(f32[64,2]{0,1:T(2,128)S(1)} %fusion.24), channel_id=1, replica_groups=mesh['dp'=8,'ctx'=8,'tp'=8] {'tp'}, use_global_device_ids=true, to_apply=%region_10.12 | all-reduce | flops 128 | bytes 1024 | tf_op jit(solution)/shard_map/psum | solution.py:139
  377.4 0.6 constant_dynamic-slice_fusion
  378.0 1.1 reduce-scatter.5.cloned.1.call-done
  379.1 1.5 convert_element_type.81
  380.6 41.4 %reduce-scatter.3.cloned.1.call-done = f32[8,4096]{1,0:T(8,128)} async-done(((f32[64,4096]{1,0:T(8,128)}), f32[8,4096]{1,0:T(8,128)}) %reduce-scatter.3.cloned.1.call-update) | async-done | bytes 131088 | tf_op jit(solution)/shard_map/reduce_scatter | solution.py:89
  422.0 1.5 convert_element_type.71
  (48 shorter events, 2.7 us)
Async XLA Ops:
  7.2 241.4 %copy-start = (bf16[1,128,4096]{2,1,0:T(8,128)(2,1)S(1)}, bf16[1,128,4096]{2,1,0:T(8,128)(2,1)}, u32[]{:S(2)}) copy-start(bf16[1,128,4096]{2,1,0:T(8,128)(2,1)} %param.21) | copy-start | bytes 3145732
  51.7 15.5 %copy-start.8 = (s32[8]{0:T(128)S(1)}, s32[8]{0:T(128)}, u32[]{:S(2)}) copy-start(s32[8]{0:T(128)} %param.15) | copy-start | bytes 100
  51.7 15.5 %copy-start.7 = (f32[8]{0:T(128)S(1)}, f32[8]{0:T(128)}, u32[]{:S(2)}) copy-start(f32[8]{0:T(128)} %param.16) | copy-start | bytes 100
  51.7 129.4 %copy-start.9 = (f32[128]{0:T(128)S(1)}, f32[128]{0:T(128)}, u32[]{:S(2)}) copy-start(f32[128]{0:T(128)} %param.17) | copy-start | bytes 1540
  51.7 129.6 %copy-start.5 = (bf16[8,4096]{1,0:T(8,128)(2,1)S(1)}, bf16[8,4096]{1,0:T(8,128)(2,1)}, u32[]{:S(2)}) copy-start(bf16[8,4096]{1,0:T(8,128)(2,1)} %param.18) | copy-start | bytes 196612
  53.2 155.5 %all-to-all-start = ((bf16[64,2,4096]{2,1,0:T(2,128)(2,1)}), bf16[64,2,4096]{2,1,0:T(2,128)(2,1)S(1)}, u32[]{:S(2)}, u32[]{:S(2)}) async-start(bf16[64,2,4096]{2,1,0:T(2,128)(2,1)} %reshape.98), calls=%async_computation | async-start | bytes 2097152 | tf_op jit(solution)/shard_map/all_to_all | solution.py:25
  208.7 11.4 %copy-start.1 = (bf16[1,4096,128]{2,1,0:T(8,128)(2,1)S(1)}, bf16[1,4096,128]{2,1,0:T(8,128)(2,1)}, u32[]{:S(2)}) copy-start(bf16[1,4096,128]{2,1,0:T(8,128)(2,1)} %param.19) | copy-start | bytes 3145732
  208.7 1.0 copy-start.2
  209.7 37.4 %all-to-all-start.2 = ((bf16[64,2,4096]{2,1,0:T(2,128)(2,1)}), bf16[64,2,4096]{2,1,0:T(2,128)(2,1)}, u32[]{:S(2)}, u32[]{:S(2)}) async-start(bf16[64,2,4096]{2,1,0:T(2,128)(2,1)} %reshape.102), calls=%async_computation.3 | async-start | bytes 2097152 | tf_op jit(solution)/shard_map/all_to_all | solution.py:25
  220.1 1.2 copy-start.3
  252.5 35.0 %all-to-all-start.1 = ((bf16[64,2,4096]{2,1,0:T(2,128)(2,1)}), bf16[64,2,4096]{2,1,0:T(2,128)(2,1)}, u32[]{:S(2)}, u32[]{:S(2)}) async-start(bf16[64,2,4096]{2,1,0:T(2,128)(2,1)} %reshape.100), calls=%async_computation.1 | async-start | bytes 2097152 | tf_op jit(solution)/shard_map/all_to_all | solution.py:78
  259.6 1.2 copy-start.4
  261.2 33.0 %copy-start.6 = (f32[8,2]{0,1:T(2,128)S(1)}, f32[8,2]{0,1:T(2,128)}, u32[]{:S(2)}) copy-start(f32[8,2]{0,1:T(2,128)} %param.14) | copy-start | bytes 196
  287.6 35.0 %all-to-all-start.3 = ((bf16[64,2,4096]{2,1,0:T(2,128)(2,1)}), bf16[64,2,4096]{2,1,0:T(2,128)(2,1)}, u32[]{:S(2)}, u32[]{:S(2)}) async-start(bf16[64,2,4096]{2,1,0:T(2,128)(2,1)} %reshape.104), calls=%async_computation.4 | async-start | bytes 2097152 | tf_op jit(solution)/shard_map/all_to_all | solution.py:114
  294.2 84.9 %reduce-scatter.5.cloned.1.call-start = ((), (), s32[]{:S(2)}) async-start(), calls=%async_computation.8 | async-start | bytes 1179648 | tf_op jit(solution)/shard_map/reduce_scatter | solution.py:138
  344.0 77.9 %reduce-scatter.3.cloned.1.call-start = ((), (), s32[]{:S(2)}) async-start(), calls=%async_computation.7 | async-start | bytes 1179648 | tf_op jit(solution)/shard_map/reduce_scatter | solution.py:89
  345.9 15.0 %all-to-all-start.4 = ((bf16[64,1,2]{2,1,0:T(2,128)(2,1)}), bf16[64,1,2]{2,1,0:T(2,128)(2,1)S(1)}, u32[]{:S(2)}, u32[]{:S(2)}) async-start(bf16[64,1,2]{2,1,0:T(2,128)(2,1)} %all_to_all.24), calls=%async_computation.6 | async-start | bytes 65536 | tf_op jit(solution)/shard_map/all_to_all | solution.py:121
Sparse Core Ops, SparseCore 0:
  344.2 34.8 reduce-scatter.4
  381.9 40.0 reduce-scatter.2
where the time goes:
time: 431 us; the launch traced here: 430 us
  blocking collectives  211 us (49%)
  waiting for transfers between devices  113 us (26%)
  starting transfers between devices  42.5 us (10%)
  local copies, waits for them, and re-layouts  28.8 us (7%)
  other arithmetic  15.8 us (4%)
  between operations  14.4 us (3%)
  matrix products  4.87 us (1%)
    psum x1, blocking collectives, per_device(): seq_sums, counts = lax.psum((seq_sums, counts), ('dp', 'ctx', 'tp'))  114 us
    all_gather x2, blocking collectives, group_rows(): return lax.all_gather(local_rows, 'tp', axis=0, tiled=True)  51.1 us
    reduce_scatter x1, waiting for transfers between devices, per_device(): lax.psum_scatter(output_group, 'tp', scatter_dimension=0, tiled=True)  41.4 us
    all_to_all x2, waiting for transfers between devices, send_slots(): lax.all_to_all(buffer, ('dp', 'ctx'), split_axis=0, concat_axis=0, tiled=...  25.3 us
    all_to_all x1, waiting for transfers between devices, per_device(): lax.all_to_all(expert_part.reshape(experts, capacity, model_width), ('dp'...  24.8 us
    all_to_all x2, starting transfers between devices, send_slots(): lax.all_to_all(buffer, ('dp', 'ctx'), split_axis=0, concat_axis=0, tiled=...  22.8 us
    all_gather x1, blocking collectives, per_device(): lax.all_gather(routes, 'tp', axis=0, tiled=True)  17.1 us
    psum x1, blocking collectives, per_device(): gates_total = lax.psum(gates_group, 'tp')  14.7 us
  transfers between devices with their start and end apart: 7, of which 6 were waited for; matrix products, arithmetic and copies ran while one was open for 3% of the time, Pallas kernels for 0%

commit v1 on v0

v1 whole, which is shorter than its diff:
```python
import jax
import jax.numpy as jnp
from jax import lax
from jax.experimental import pallas as pl
from jax.experimental.pallas import tpu as pltpu
from jax.sharding import PartitionSpec as P

CLIP_HIGH = 1.2
GROUP_AXES = ("dp", "ctx")
META = 128
F32 = jnp.float32
BF16 = jnp.bfloat16


def split3(value):
    high = value.astype(BF16).astype(F32)
    rest = value - high
    middle = rest.astype(BF16).astype(F32)
    return high, middle, rest - middle


def lanes(rows, columns):
    lane = lax.broadcasted_iota(jnp.int32, (rows, META), 1)
    total = jnp.zeros((rows, META), F32)
    for place, column in enumerate(columns):
        total = total + jnp.where(lane == place, column, 0.0)
    return total


def pack_kernel(tokens, upstream, routes, gates, ids, ratio, out):
    parts, rows = out.shape[0], out.shape[1]
    width = tokens.shape[1] // parts
    gate_parts = split3(gates[...])
    columns = [routes[:, 0:1].astype(F32), routes[:, 1:2].astype(F32), ids[...].astype(F32)]
    columns += list(split3(ratio[...]))
    for k in range(2):
        columns += [piece[:, k : k + 1] for piece in gate_parts]
    meta = lanes(rows, columns).astype(BF16)
    for t in range(parts):
        out[t, :, 0:width] = tokens[:, t * width : (t + 1) * width]
        out[t, :, width : 2 * width] = upstream[:, t * width : (t + 1) * width]
        out[t, :, 2 * width : 2 * width + META] = meta


def slot_one_hots(meta, experts, capacity):
    count = meta.shape[0]
    expert = lax.broadcasted_iota(jnp.int32, (count, experts), 1).astype(F32)
    chosen = [(meta[:, k : k + 1] == expert).astype(F32) for k in range(2)]
    row = lax.broadcasted_iota(jnp.int32, (count, count), 0)
    column = lax.broadcasted_iota(jnp.int32, (count, count), 1)
    before = jnp.dot(
        (column < row).astype(BF16),
        (chosen[0] + chosen[1]).astype(BF16),
        preferred_element_type=F32,
    )
    slot = lax.broadcasted_iota(jnp.int32, (count, experts * capacity), 1).astype(F32)
    result = []
    for k in range(2):
        position = jnp.sum(before * chosen[k], axis=1, keepdims=True)
        result.append((meta[:, k : k + 1] * capacity + position == slot).astype(F32))
    return result


def dispatch_kernel(group, out):
    experts = out.shape[0] // 2
    width = out.shape[1]
    hots = slot_one_hots(group[:, width : width + META].astype(F32), experts, 2)
    out[...] = lax.dot_general(
        (hots[0] + hots[1]).astype(BF16),
        group[:, 0:width],
        (((0,), (0,)), ((), ())),
        preferred_element_type=F32,
    ).astype(BF16)


def expert_kernel(arrived, w_gate, w_up, w_down, out):
    parts = arrived.shape[0]
    width = arrived.shape[2] // 2
    gate_pre = up_pre = d_hidden = 0.0
    for t in range(parts):
        cut = slice(t * width, (t + 1) * width)
        rows = arrived[t, :, 0:width]
        gate_pre += jnp.dot(rows, w_gate[cut, :], preferred_element_type=F32)
        up_pre += jnp.dot(rows, w_up[cut, :], preferred_element_type=F32)
        d_hidden += lax.dot_general(
            arrived[t, :, width : 2 * width],
            w_down[:, cut],
            (((1,), (1,)), ((), ())),
            preferred_element_type=F32,
        )
    squash = jax.nn.sigmoid(gate_pre)
    activated = gate_pre * squash
    hidden = (activated * up_pre).astype(BF16)
    d_gate = (d_hidden * up_pre * squash * (1.0 + gate_pre * (1.0 - squash))).astype(BF16)
    d_up = (d_hidden * activated).astype(BF16)
    for t in range(parts):
        cut = slice(t * width, (t + 1) * width)
        out[t, :, 0:width] = jnp.dot(
            hidden, w_down[:, cut], preferred_element_type=F32
        ).astype(BF16)
        contract = (((1,), (1,)), ((), ()))
        out[t, :, width : 2 * width] = (
            lax.dot_general(d_gate, w_gate[cut, :], contract, preferred_element_type=F32)
            + lax.dot_general(d_up, w_up[cut, :], contract, preferred_element_type=F32)
        ).astype(BF16)


def combine_kernel(back, group, meta_before, meta_after, advantage, out):
    slots, both = back.shape
    width = both // 2
    count = group.shape[0]
    meta = group[:, both : both + META].astype(F32)
    hots = slot_one_hots(meta, slots // 2, 2)
    near = jnp.concatenate(
        [meta_before[...].astype(F32), meta, meta_after[...].astype(F32)], axis=0
    ).T
    same = (meta[:, 2:3] == near[2:3, :]).astype(F32)
    ratio_row = near[3:4, :] + near[4:5, :] + near[5:6, :]
    tally = jnp.sum(same, axis=1, keepdims=True)
    ratio = jnp.exp(jnp.sum(same * ratio_row, axis=1, keepdims=True) / tally)
    sequence = lax.broadcasted_iota(jnp.int32, (count, advantage.shape[1]), 1).astype(F32)
    own = jnp.sum(
        jnp.where(meta[:, 2:3] == sequence, advantage[...], 0.0), axis=1, keepdims=True
    )
    weight = own * jnp.minimum(ratio, CLIP_HIGH)
    upstream = group[:, width:both].astype(F32)
    total = 0.0
    columns = []
    for k in range(2):
        picked = jnp.dot(hots[k].astype(BF16), back[...], preferred_element_type=F32)
        first = 6 + 3 * k
        gate = meta[:, first : first + 1] + meta[:, first + 1 : first + 2]
        gate = gate + meta[:, first + 2 : first + 3]
        total = total + gate * picked
        term = weight * jnp.sum(upstream * picked[:, 0:width], axis=1, keepdims=True)
        columns += list(split3(term))
    out[:, 0:width] = total[:, 0:width].astype(BF16)
    out[:, width:both] = (weight * total[:, width:both]).astype(BF16)
    out[:, both : both + META] = lanes(count, columns).astype(BF16)


def unpack_kernel(arrived, mixed, grad_tokens, grad_gates):
    parts = arrived.shape[0]
    width = mixed.shape[1] // parts
    terms = jnp.zeros((arrived.shape[1], META), F32)
    for t in range(parts):
        cut = slice(t * width, (t + 1) * width)
        mixed[:, cut] = arrived[t, :, 0:width]
        grad_tokens[:, cut] = arrived[t, :, width : 2 * width]
        terms += arrived[t, :, 2 * width : 2 * width + META].astype(F32)
    for k in range(2):
        grad_gates[:, k : k + 1] = (
            terms[:, 3 * k : 3 * k + 1]
            + terms[:, 3 * k + 1 : 3 * k + 2]
            + terms[:, 3 * k + 2 : 3 * k + 3]
        )


def call(kernel, shapes, *operands):
    return pl.pallas_call(
        kernel,
        out_shape=shapes,
        compiler_params=pltpu.CompilerParams(vmem_limit_bytes=32 * 1024 * 1024),
    )(*operands)


def struct(*shape, dtype=BF16):
    return jax.ShapeDtypeStruct(shape, dtype)


def per_device(
    tokens, routes, gate_weights, seq_ids, log_ratio, advantage, upstream, w_gate, w_up, w_down
):
    count, model = tokens.shape
    parts = lax.axis_size("tp")
    groups = lax.axis_size("dp") * lax.axis_size("ctx")
    group_tokens = count * parts
    width = model // parts
    slots = 2 * groups

    packed = call(
        pack_kernel,
        struct(parts, count, 2 * width + META),
        tokens,
        upstream,
        routes,
        gate_weights,
        seq_ids.reshape(count, 1),
        log_ratio.reshape(count, 1),
    )
    group = lax.all_to_all(packed, "tp", 0, 0).reshape(group_tokens, 2 * width + META)
    sent = call(dispatch_kernel, struct(slots, 2 * width), group)
    slot_rows = lax.all_to_all(sent.reshape(groups, 2, 2 * width), GROUP_AXES, 0, 0)
    arrived = lax.all_gather(slot_rows.reshape(slots, 2 * width), "tp")

    meta = group[:, 2 * width :]
    meta_before = lax.ppermute(meta, GROUP_AXES, [(i, (i + 1) % groups) for i in range(groups)])
    meta_after = lax.ppermute(meta, GROUP_AXES, [((i + 1) % groups, i) for i in range(groups)])

    results = call(
        expert_kernel, struct(parts, slots, 2 * width), arrived, w_gate[0], w_up[0], w_down[0]
    )
    summed = lax.psum_scatter(results, "tp")
    back = lax.all_to_all(summed.reshape(groups, 2, 2 * width), GROUP_AXES, 0, 0)
    combined = call(
        combine_kernel,
        struct(group_tokens, 2 * width + META),
        back.reshape(slots, 2 * width),
        group,
        meta_before,
        meta_after,
        advantage.reshape(1, -1),
    )
    home = lax.all_to_all(combined.reshape(parts, count, 2 * width + META), "tp", 0, 0)
    return call(
        unpack_kernel,
        (struct(count, model), struct(count, model), struct(count, 2, dtype=F32)),
        home,
    )


def solution(mesh):
    rows = ("dp", "ctx", "tp")
    in_specs = (
        P(rows, None),
        P(rows, None),
        P(rows, None),
        P(rows),
        P(rows),
        P(),
        P(rows, None),
        P(GROUP_AXES, None, "tp"),
        P(GROUP_AXES, None, "tp"),
        P(GROUP_AXES, "tp", None),
    )
    out_specs = (P(rows, None), P(rows, None), P(rows, None))
    return jax.shard_map(
        per_device, mesh=mesh, in_specs=in_specs, out_specs=out_specs, check_vma=False
    )
```

time: 431 us -> 190 us (0.44)
  blocking collectives: 211 us -> 56.6 us
  waiting for transfers between devices: 113 us -> 83.4 us
  starting transfers between devices: 42.5 us -> 18.7 us
  local copies, waits for them, and re-layouts: 28.8 us -> 11 us
  other arithmetic: 15.8 us -> 0 us
  Pallas kernels: 0 us -> 5.3 us
  matrix products: 4.87 us -> 0 us
    psum x2 -> x0, blocking collectives: 128 us -> none  [the longest x1 114 us: per_device(): seq_sums, counts = lax.psum((seq_sums, counts), ('dp', 'ctx', 'tp'))]
    all_gather x4 -> x0, blocking collectives: 82.3 us -> none  [the longest x2 51.1 us: group_rows(): return lax.all_gather(local_rows, 'tp', axis=0, tiled=True)]
    all_to_all x5 -> x1, waiting for transfers between devices: 70.2 us -> 5.23 us  [per_device(): lax.all_to_all(summed.reshape(groups, 2, 2 * width), GROUP_AXES, 0, 0)]
    all_to_all x0 -> x3, blocking collectives: none -> 56.6 us  [the longest x1 26.4 us: per_device(): lax.all_to_all(sent.reshape(groups, 2, 2 * width), GROUP_AXES, 0, 0)]
    all_gather x0 -> x1, waiting for transfers between devices: none -> 34.5 us  [per_device(): arrived = lax.all_gather(slot_rows.reshape(slots, 2 * width), 'tp')]
    all_to_all x5 -> x1, starting transfers between devices: 42.4 us -> 11 us  [per_device(): lax.all_to_all(summed.reshape(groups, 2, 2 * width), GROUP_AXES, 0, 0)]
    reshape x9 -> x4, local copies, waits for them, and re-layouts: 13.1 us -> 1.66 us  [the longest x1 0.73 us: per_device(): log_ratio.reshape(count, 1)]
    reduce_sum x4 -> x0, other arithmetic: 8.64 us -> none  [the longest x1 8.28 us: per_device(): jnp.sum(gathered_grad.astype(jnp.float32) * weight_group[:, :, None], axi...]
  transfers between devices with their start and end apart: 7 -> 5, of which waited for: 6 -> 3; matrix products, arithmetic and copies ran while one was open for 3% -> 0% of each run, Pallas kernels for 0% -> 0%
where the time goes in v1:
time: 190 us; the launch traced here: 189 us
  waiting for transfers between devices  83.4 us (44%)
  blocking collectives  56.6 us (30%)
  starting transfers between devices  18.7 us (10%)
  between operations  14.2 us (7%)
  local copies, waits for them, and re-layouts  11 us (6%)
  Pallas kernels  5.3 us (3%)
    reduce_scatter x1, waiting for transfers between devices, per_device(): summed = lax.psum_scatter(results, 'tp')  43.7 us
    all_gather x1, waiting for transfers between devices, per_device(): arrived = lax.all_gather(slot_rows.reshape(slots, 2 * width), 'tp')  34.5 us
    all_to_all x1, blocking collectives, per_device(): lax.all_to_all(sent.reshape(groups, 2, 2 * width), GROUP_AXES, 0, 0)  26.4 us
    all_to_all x1, blocking collectives, per_device(): lax.all_to_all(packed, 'tp', 0, 0).reshape(group_tokens, 2 * width + META)  16.3 us
    all_to_all x1, blocking collectives, per_device(): lax.all_to_all(combined.reshape(parts, count, 2 * width + META), 'tp', 0, 0)  13.9 us
    all_to_all x1, starting transfers between devices, per_device(): lax.all_to_all(summed.reshape(groups, 2, 2 * width), GROUP_AXES, 0, 0)  11 us
    unnamed x16, local copies, waits for them, and re-layouts  6.15 us
    pallas_call x5, Pallas kernels, call(): pl.pallas_call(kernel, out_shape=shapes, compiler_params=pltpu.CompilerPa...  5.3 us
  transfers between devices with their start and end apart: 5, of which 3 were waited for; matrix products, arithmetic and copies ran while one was open for 0% of the time, Pallas kernels for 0%

profile of v1, /device:TPU:2, one launch (start us, length us, event | category | flops | bytes accessed | tf_op | source)
XLA Modules:
  0.0 189.2 jit_solution(7044663835187696965)
XLA Ops:
  7.2 0.0 copy-start.1
  7.2 0.0 copy-start.2
  7.2 0.0 all-gather.2.cloned.1.call-start
  7.2 0.9 copy.18.routes
  8.1 0.8 copy.19.gates
  8.9 0.7 copy.20.ids
  9.6 0.7 copy.21.ratio
  10.3 0.0 copy-start.4
  10.3 0.8 copy-done.4
  11.2 0.0 copy-start.5
  11.2 0.8 copy-done.5
  12.0 0.1 shard_map.121
  12.1 16.3 %all_to_all.20 = bf16[8,8,1152]{2,1,0:T(8,128)(2,1)S(1)} all-to-all(bf16[8,8,1152]{2,1,0:T(8,128)(2,1)S(1)} %shard_map.121), channel_id=1, replica_groups=mesh['dp'=8,'ctx'=8,'tp'=8] {'tp'}, dimensions={0} | all-to-all | bytes 294912 | tf_op jit(solution)/shard_map/all_to_all | solution.py:191
  28.4 0.6 shard_map.122
  29.1 0.1 reshape.30
  29.2 26.4 %all_to_all.21 = bf16[64,2,1024]{2,1,0:T(2,128)(2,1)S(1)} all-to-all(bf16[64,2,1024]{2,1,0:T(2,128)(2,1)S(1)} %reshape.30), channel_id=1, replica_groups=mesh['dp'=8,'ctx'=8,'tp'=8] {'dp','ctx'}, dimensions={0} | all-to-all | bytes 524288 | tf_op jit(solution)/shard_map/all_to_all | solution.py:193
  55.5 0.8 all_gather_reshape.3
  56.3 0.0 all-gather.2.cloned.1.call-update
  56.4 0.0 reduce-scatter.2.cloned.1.call-start
  56.4 34.5 %all-gather.2.cloned.1.call-done.arrived = bf16[8,128,1024]{2,1,0:T(8,128)(2,1)} async-done(((bf16[1,128,1024]{2,1,0:T(8,128)(2,1)}), bf16[8,128,1024]{2,1,0:T(8,128)(2,1)}) %all-gather.2.cloned.1.call-update) | async-done | bytes 2097168 | tf_op jit(solution)/shard_map/all_gather | solution.py:194
  90.9 0.0 copy-done.1
  90.9 0.0 copy-done.2
  90.9 0.0 copy-start
  90.9 1.6 copy-done
  92.5 0.0 copy-start.3
  92.5 1.2 copy-done.3
  93.7 3.2 %shard_map.123 = bf16[8,128,1024]{2,1,0:T(8,128)(2,1)} custom-call(bf16[8,128,1024]{2,1,0:T(8,128)(2,1)S(1)} %copy-done, bf16[4096,128]{1,0:T(8,128)(2,1)S(1)} %bitcast.11, bf16[4096,128]{1,0:T(8,128)(2,1)S(1)} %bitcast.12, bf16[128,4096]{1,0:T(8,128)(2,1)S(1)} %bitcast.13), custom_call_target="tpu_custom_call" | custom-call | tf_op jit(solution)/shard_map/pallas_call | solution.py:160
  96.9 0.0 copy-start.6
  97.0 0.0 reduce-scatter.2.cloned.1.call-update
  97.0 43.7 %reduce-scatter.2.cloned.1.call-done = bf16[1,128,1024]{2,1,0:T(8,128)(2,1)} async-done(((bf16[8,128,1024]{2,1,0:T(8,128)(2,1)}), bf16[1,128,1024]{2,1,0:T(8,128)(2,1)}) %reduce-scatter.2.cloned.1.call-update) | async-done | bytes 262160 | tf_op jit(solution)/shard_map/reduce_scatter | solution.py:203
  140.6 1.7 reshape_reduce_scatter.3
  142.4 11.0 %all-to-all-start.2 = ((bf16[64,2,1024]{2,1,0:T(2,128)(2,1)}), bf16[64,2,1024]{2,1,0:T(2,128)(2,1)S(1)}, u32[]{:S(2)}, u32[]{:S(2)}) async-start(bf16[64,2,1024]{2,1,0:T(2,128)(2,1)} %reshape_reduce_scatter.3), calls=%async_computation.3 | async-start | bytes 524288 | tf_op jit(solution)/shard_map/all_to_all | solution.py:204
  153.4 3.4 %collective-permute-start = (bf16[64,128]{1,0:T(8,128)(2,1)S(1)}, bf16[64,128]{1,0:T(8,128)(2,1)S(1)}, u32[]{:S(2)}, u32[]{:S(2)}) collective-permute-start(bf16[64,128]{1,0:T(8,128)(2,1)S(1)} %slice.4), channel_id=1, source_target_pairs={{0,8},{8,16},{16,24},{24,32},{32,40},{40,48},{48,56},{56,64},{64,7... | collective-permute-start | bytes 49160 | tf_op jit(solution)/shard_map/ppermute | solution.py:197
  156.7 4.3 %collective-permute-start.1 = (bf16[64,128]{1,0:T(8,128)(2,1)S(1)}, bf16[64,128]{1,0:T(8,128)(2,1)S(1)}, u32[]{:S(2)}, u32[]{:S(2)}) collective-permute-start(bf16[64,128]{1,0:T(8,128)(2,1)S(1)} %slice.4), channel_id=1, source_target_pairs={{8,0},{16,8},{24,16},{32,24},{40,32},{48,40},{56,48},{64,56},{72,6... | collective-permute-start | bytes 49160 | tf_op jit(solution)/shard_map/ppermute | solution.py:198
  161.1 5.2 %all-to-all-done.2 = bf16[64,2,1024]{2,1,0:T(2,128)(2,1)S(1)} async-done(((bf16[64,2,1024]{2,1,0:T(2,128)(2,1)}), bf16[64,2,1024]{2,1,0:T(2,128)(2,1)S(1)}, u32[]{:S(2)}, u32[]{:S(2)}) %all-to-all-start.2) | async-done | bytes 262176 | tf_op jit(solution)/shard_map/all_to_all | solution.py:204
  166.3 0.1 reshape.31.back
  166.4 0.0 collective-permute-done.meta_before
  166.4 0.0 collective-permute-done.1.meta_after
  166.4 0.0 copy-done.6
  166.4 0.7 shard_map.124
  167.2 13.9 %all_to_all.22.arrived = bf16[8,8,1152]{2,1,0:T(8,128)(2,1)S(1)} all-to-all(bf16[8,8,1152]{2,1,0:T(8,128)(2,1)S(1)} %bitcast.14), channel_id=1, replica_groups=mesh['dp'=8,'ctx'=8,'tp'=8] {'tp'}, dimensions={0} | all-to-all | bytes 294912 | tf_op jit(solution)/shard_map/all_to_all | solution.py:214
  181.1 0.7 shard_map.125
  181.7 0.6 copy.22
  (1 shorter events, 0.0 us)
Async XLA Ops:
  7.2 83.7 %copy-start.1 = (bf16[1,4096,128]{2,1,0:T(8,128)(2,1)S(1)}, bf16[1,4096,128]{2,1,0:T(8,128)(2,1)}, u32[]{:S(2)}) copy-start(bf16[1,4096,128]{2,1,0:T(8,128)(2,1)} %param.17) | copy-start | bytes 3145732
  7.2 83.7 %copy-start.2 = (bf16[1,4096,128]{2,1,0:T(8,128)(2,1)S(1)}, bf16[1,4096,128]{2,1,0:T(8,128)(2,1)}, u32[]{:S(2)}) copy-start(bf16[1,4096,128]{2,1,0:T(8,128)(2,1)} %param.18) | copy-start | bytes 3145732
  7.2 83.7 %all-gather.2.cloned.1.call-start = ((), (), s32[]{:S(2)}) async-start(), calls=%async_computation.5 | async-start | bytes 2359296 | tf_op jit(solution)/shard_map/all_gather | solution.py:194
  10.3 0.8 copy-start.4
  11.2 0.8 copy-start.5
  56.4 84.3 %reduce-scatter.2.cloned.1.call-start = ((), (), s32[]{:S(2)}) async-start(), calls=%async_computation.6 | async-start | bytes 2359296 | tf_op jit(solution)/shard_map/reduce_scatter | solution.py:203
  90.9 1.6 copy-start
  92.5 1.2 copy-start.3
  96.9 69.5 %copy-start.6 = (f32[128]{0:T(128)S(1)}, f32[128]{0:T(128)}, u32[]{:S(2)}) copy-start(f32[128]{0:T(128)} %param.15) | copy-start | bytes 1540
  142.4 23.9 %all-to-all-start.2 = ((bf16[64,2,1024]{2,1,0:T(2,128)(2,1)}), bf16[64,2,1024]{2,1,0:T(2,128)(2,1)S(1)}, u32[]{:S(2)}, u32[]{:S(2)}) async-start(bf16[64,2,1024]{2,1,0:T(2,128)(2,1)} %reshape_reduce_scatter.3), calls=%async_computation.3 | async-start | bytes 524288 | tf_op jit(solution)/shard_map/all_to_all | solution.py:204
  153.4 13.0 %collective-permute-start = (bf16[64,128]{1,0:T(8,128)(2,1)S(1)}, bf16[64,128]{1,0:T(8,128)(2,1)S(1)}, u32[]{:S(2)}, u32[]{:S(2)}) collective-permute-start(bf16[64,128]{1,0:T(8,128)(2,1)S(1)} %slice.4), channel_id=1, source_target_pairs={{0,8},{8,16},{16,24},{24,32},{32,40},{40,48},{48,56},{56,64},{64,7... | collective-permute-start | bytes 49160 | tf_op jit(solution)/shard_map/ppermute | solution.py:197
  156.7 9.7 %collective-permute-start.1 = (bf16[64,128]{1,0:T(8,128)(2,1)S(1)}, bf16[64,128]{1,0:T(8,128)(2,1)S(1)}, u32[]{:S(2)}, u32[]{:S(2)}) collective-permute-start(bf16[64,128]{1,0:T(8,128)(2,1)S(1)} %slice.4), channel_id=1, source_target_pairs={{8,0},{16,8},{24,16},{32,24},{40,32},{48,40},{56,48},{64,56},{72,6... | collective-permute-start | bytes 49160 | tf_op jit(solution)/shard_map/ppermute | solution.py:198
Sparse Core Ops, SparseCore 0:
  56.5 34.3 all-gather.1
  97.1 43.4 reduce-scatter.1

commit v2 on v1

v2 whole, which is shorter than its diff:
```python
import jax
import jax.numpy as jnp
from jax import lax
from jax.experimental import pallas as pl
from jax.experimental.pallas import tpu as pltpu
from jax.sharding import PartitionSpec as P

CLIP_HIGH = 1.2
GROUP_AXES = ("dp", "ctx")
META = 128
CUTS = 4
F32 = jnp.float32
BF16 = jnp.bfloat16


def split3(value):
    high = value.astype(BF16).astype(F32)
    rest = value - high
    middle = rest.astype(BF16).astype(F32)
    return high, middle, rest - middle


def columns_of(rows_by_one, count):
    eye = lax.broadcasted_iota(jnp.int32, (count, count), 0) == lax.broadcasted_iota(
        jnp.int32, (count, count), 1
    )
    return jnp.sum(jnp.where(eye, rows_by_one, 0.0), axis=1, keepdims=True)


def row_of(column, count):
    eye = lax.broadcasted_iota(jnp.int32, (count, count), 0) == lax.broadcasted_iota(
        jnp.int32, (count, count), 1
    )
    return jnp.sum(jnp.where(eye, column, 0.0), axis=0, keepdims=True)


def lanes(rows, columns):
    lane = lax.broadcasted_iota(jnp.int32, (rows, META), 1)
    total = jnp.zeros((rows, META), F32)
    for place, column in enumerate(columns):
        total = total + jnp.where(lane == place, column, 0.0)
    return total


def pack_kernel(tokens, upstream, routes, gates, ids, ratio, out):
    parts, rows = out.shape[0], out.shape[1]
    width = tokens.shape[1] // CUTS
    rows_in = [routes[0:1, :].astype(F32), routes[1:2, :].astype(F32), ids[...].astype(F32)]
    rows_in += list(split3(ratio[...]))
    gate_parts = split3(gates[...])
    for k in range(2):
        rows_in += [piece[k : k + 1, :] for piece in gate_parts]
    meta = lanes(rows, [columns_of(row, rows) for row in rows_in]).astype(BF16)
    for t in range(parts):
        cut = slice((t % CUTS) * width, (t % CUTS + 1) * width)
        out[t, :, 0:width] = tokens[:, cut]
        out[t, :, width : 2 * width] = upstream[:, cut]
        out[t, :, 2 * width : 2 * width + META] = meta


def slot_one_hots(meta, experts, capacity):
    count = meta.shape[0]
    expert = lax.broadcasted_iota(jnp.int32, (count, experts), 1).astype(F32)
    chosen = [(meta[:, k : k + 1] == expert).astype(F32) for k in range(2)]
    row = lax.broadcasted_iota(jnp.int32, (count, count), 0)
    column = lax.broadcasted_iota(jnp.int32, (count, count), 1)
    before = jnp.dot(
        (column < row).astype(BF16),
        (chosen[0] + chosen[1]).astype(BF16),
        preferred_element_type=F32,
    )
    slot = lax.broadcasted_iota(jnp.int32, (count, experts * capacity), 1).astype(F32)
    result = []
    for k in range(2):
        position = jnp.sum(before * chosen[k], axis=1, keepdims=True)
        result.append((meta[:, k : k + 1] * capacity + position == slot).astype(F32))
    return result


def dispatch_kernel(group, out):
    slots = out.shape[0]
    width = out.shape[1] - META
    meta = group[:, width : width + META].astype(F32)
    hots = slot_one_hots(meta, slots // 2, 2)
    out[:, 0:width] = lax.dot_general(
        (hots[0] + hots[1]).astype(BF16),
        group[:, 0:width],
        (((0,), (0,)), ((), ())),
        preferred_element_type=F32,
    ).astype(BF16)
    across = meta.T
    first = jnp.concatenate([across[2:3, :], across[3:4, :]], axis=1)
    second = jnp.concatenate([across[4:5, :], across[5:6, :]], axis=1)
    odd = lax.broadcasted_iota(jnp.int32, (slots, META), 0) % 2 == 1
    out[:, width : width + META] = jnp.where(odd, second, first).astype(BF16)


def weight_kernel(near, group, advantage, out):
    groups = near.shape[0] // 2
    count = group.shape[0]
    here = lax.axis_index("dp") * lax.axis_size("ctx") + lax.axis_index("ctx")
    wanted = lax.broadcasted_iota(jnp.int32, (8, 2 * groups), 0)
    target = 2 * ((here + wanted // 2 - 1 + groups) % groups) + wanted % 2
    row = lax.broadcasted_iota(jnp.int32, (8, 2 * groups), 1)
    rows = jnp.dot((row == target).astype(BF16), near[...], preferred_element_type=F32)
    own_id = group[:, 2:3].astype(F32)
    total = tally = 0.0
    for beside in range(3):
        ids = rows[2 * beside : 2 * beside + 1, 0:count]
        ratio = rows[2 * beside : 2 * beside + 1, count : 2 * count]
        ratio = ratio + rows[2 * beside + 1 : 2 * beside + 2, 0:count]
        ratio = ratio + rows[2 * beside + 1 : 2 * beside + 2, count : 2 * count]
        same = (own_id == ids).astype(F32)
        tally = tally + jnp.sum(same, axis=1, keepdims=True)
        total = total + jnp.sum(same * ratio, axis=1, keepdims=True)
    sequence = lax.broadcasted_iota(jnp.int32, (count, advantage.shape[1]), 1).astype(F32)
    own = jnp.sum(jnp.where(own_id == sequence, advantage[...], 0.0), axis=1, keepdims=True)
    weight = own * jnp.minimum(jnp.exp(total / tally), CLIP_HIGH)
    out[...] = jnp.broadcast_to(weight, out.shape)


def cut_of(offset, width):
    return pl.multiple_of((lax.axis_index("tp") + offset + CUTS) % CUTS * width, width)


def forward_kernel(x0, xm1, xp1, x2, w_gate, w_up, w_down, y0, ym1, yp1, y2, gate_out, up_out):
    width = x0.shape[1]
    gate_pre = up_pre = 0.0
    for rows, offset in ((x0, 0), (xm1, -1), (xp1, 1), (x2, 2)):
        cut = pl.ds(cut_of(offset, width), width)
        gate_pre += jnp.dot(rows[...], w_gate[cut, :], preferred_element_type=F32)
        up_pre += jnp.dot(rows[...], w_up[cut, :], preferred_element_type=F32)
    gate_out[...] = gate_pre
    up_out[...] = up_pre
    hidden = (gate_pre * jax.nn.sigmoid(gate_pre) * up_pre).astype(BF16)
    for rows, offset in ((y2, 2), (yp1, 1), (ym1, -1), (y0, 0)):
        cut = pl.ds(cut_of(offset, width), width)
        rows[...] = jnp.dot(hidden, w_down[:, cut], preferred_element_type=F32).astype(BF16)


def backward_kernel(d0, dm1, dp1, d2, gate, up, w_gate, w_up, w_down, g0, gm1, gp1, g2):
    width = d0.shape[1]
    contract = (((1,), (1,)), ((), ()))
    d_hidden = 0.0
    for rows, offset in ((d0, 0), (dm1, -1), (dp1, 1), (d2, 2)):
        cut = pl.ds(cut_of(offset, width), width)
        d_hidden += lax.dot_general(
            rows[...], w_down[:, cut], contract, preferred_element_type=F32
        )
    gate_pre = gate[...]
    squash = jax.nn.sigmoid(gate_pre)
    d_gate = (d_hidden * up[...] * squash * (1.0 + gate_pre * (1.0 - squash))).astype(BF16)
    d_up = (d_hidden * (gate_pre * squash)).astype(BF16)
    for rows, offset in ((g2, 2), (gp1, 1), (gm1, -1), (g0, 0)):
        cut = pl.ds(cut_of(offset, width), width)
        rows[...] = (
            lax.dot_general(d_gate, w_gate[cut, :], contract, preferred_element_type=F32)
            + lax.dot_general(d_up, w_up[cut, :], contract, preferred_element_type=F32)
        ).astype(BF16)


def sum_kernel(y0, y_right, y_left, g0, g_right, g_left, out):
    width = y0.shape[1]
    out[:, 0:width] = (
        y0[...].astype(F32) + y_right[...].astype(F32) + y_left[...].astype(F32)
    ).astype(BF16)
    out[:, width : 2 * width] = (
        g0[...].astype(F32) + g_right[...].astype(F32) + g_left[...].astype(F32)
    ).astype(BF16)


def combine_kernel(back, group, weights, out):
    slots, both = back.shape
    width = both // 2
    count = group.shape[0]
    meta = group[:, both : both + META].astype(F32)
    hots = slot_one_hots(meta, slots // 2, 2)
    weight = weights[:, 0:1]
    upstream = group[:, width:both].astype(F32)
    total = 0.0
    columns = []
    for k in range(2):
        picked = jnp.dot(hots[k].astype(BF16), back[...], preferred_element_type=F32)
        first = 6 + 3 * k
        gate = meta[:, first : first + 1] + meta[:, first + 1 : first + 2]
        gate = gate + meta[:, first + 2 : first + 3]
        total = total + gate * picked
        term = weight * jnp.sum(upstream * picked[:, 0:width], axis=1, keepdims=True)
        columns += list(split3(term))
    out[:, 0:width] = total[:, 0:width].astype(BF16)
    out[:, width:both] = (weight * total[:, width:both]).astype(BF16)
    out[:, both : both + META] = lanes(count, columns).astype(BF16)


def unpack_kernel(arrived, mixed, grad_tokens, grad_gates):
    parts, rows = arrived.shape[0], arrived.shape[1]
    width = mixed.shape[1] // CUTS
    terms = jnp.zeros((rows, META), F32)
    for t in range(parts):
        terms += arrived[t, :, 2 * width : 2 * width + META].astype(F32)
    for q in range(CUTS):
        total = 0.0
        for t in range(q, parts, CUTS):
            total = total + arrived[t, :, 0 : 2 * width].astype(F32)
        cut = slice(q * width, (q + 1) * width)
        mixed[:, cut] = total[:, 0:width].astype(BF16)
        grad_tokens[:, cut] = total[:, width : 2 * width].astype(BF16)
    for k in range(2):
        column = (
            terms[:, 3 * k : 3 * k + 1]
            + terms[:, 3 * k + 1 : 3 * k + 2]
            + terms[:, 3 * k + 2 : 3 * k + 3]
        )
        grad_gates[k : k + 1, :] = row_of(column, rows)


def call(kernel, shapes, *operands, mib=8):
    return pl.pallas_call(
        kernel,
        out_shape=shapes,
        compiler_params=pltpu.CompilerParams(vmem_limit_bytes=mib * 1024 * 1024),
    )(*operands)


def struct(*shape, dtype=BF16):
    return jax.ShapeDtypeStruct(shape, dtype)


def shift(rows, places):
    size = lax.axis_size("tp")
    return lax.ppermute(rows, "tp", [(i, (i + places) % size) for i in range(size)])


def add(left, right):
    return (left.astype(F32) + right.astype(F32)).astype(BF16)


def per_device(
    tokens, routes, gate_weights, seq_ids, log_ratio, advantage, upstream, w_gate, w_up, w_down
):
    count, model = tokens.shape
    parts = lax.axis_size("tp")
    groups = lax.axis_size("dp") * lax.axis_size("ctx")
    group_tokens = count * parts
    width = model // CUTS
    both = 2 * width
    slots = 2 * groups
    gate_local, up_local, down_local = w_gate[0], w_up[0], w_down[0]

    packed = call(
        pack_kernel,
        struct(parts, count, both + META),
        tokens,
        upstream,
        routes.T,
        gate_weights.T,
        seq_ids.reshape(1, count),
        log_ratio.reshape(1, count),
    )
    group = lax.all_to_all(packed, "tp", 0, 0).reshape(group_tokens, both + META)
    sent = call(dispatch_kernel, struct(slots, both + META), group)
    arrived = lax.all_to_all(
        sent.reshape(groups, 2, both + META), GROUP_AXES, 0, 0
    ).reshape(slots, both + META)

    x0, d0 = arrived[:, 0:width], arrived[:, width:both]
    xm1, dp1 = shift(x0, 1), shift(d0, -1)
    xp1, dm1 = shift(x0, -1), shift(d0, 1)
    x2, d2 = shift(xm1, 1), shift(dp1, -1)

    weights = call(
        weight_kernel,
        struct(group_tokens, META, dtype=F32),
        arrived[:, both:],
        group[:, both:],
        advantage.reshape(1, -1),
    )
    piece = struct(slots, width)
    inner = struct(slots, gate_local.shape[1], dtype=F32)
    y0, ym1, yp1, y2, gate_pre, up_pre = call(
        forward_kernel,
        (piece,) * 4 + (inner,) * 2,
        x0, xm1, xp1, x2, gate_local, up_local, down_local,
        mib=16,
    )
    g0, gm1, gp1, g2 = call(
        backward_kernel,
        (piece,) * 4,
        d0, dm1, dp1, d2, gate_pre, up_pre, gate_local, up_local, down_local,
        mib=16,
    )
    y_right = shift(yp1, 1)
    y_left = shift(add(ym1, shift(y2, -1)), -1)
    g_left = shift(gm1, -1)
    g_right = shift(add(gp1, shift(g2, 1)), 1)
    summed = call(sum_kernel, struct(slots, both), y0, y_right, y_left, g0, g_right, g_left)

    back = lax.all_to_all(summed.reshape(groups, 2, both), GROUP_AXES, 0, 0)
    combined = call(
        combine_kernel,
        struct(group_tokens, both + META),
        back.reshape(slots, both),
        group,
        weights,
    )
    home = lax.all_to_all(combined.reshape(parts, count, both + META), "tp", 0, 0)
    mixed, grad_tokens, grad_gates = call(
        unpack_kernel,
        (struct(count, model), struct(count, model), struct(2, count, dtype=F32)),
        home,
    )
    return mixed, grad_tokens, grad_gates.T


def solution(mesh):
    rows = ("dp", "ctx", "tp")
    in_specs = (
        P(rows, None),
        P(rows, None),
        P(rows, None),
        P(rows),
        P(rows),
        P(),
        P(rows, None),
        P(GROUP_AXES, None, "tp"),
        P(GROUP_AXES, None, "tp"),
        P(GROUP_AXES, "tp", None),
    )
    out_specs = (P(rows, None), P(rows, None), P(rows, None))
    return jax.shard_map(
        per_device, mesh=mesh, in_specs=in_specs, out_specs=out_specs, check_vma=False
    )
```

time: 190 us -> 157 us (0.83)
  waiting for transfers between devices: 83.4 us -> 25.4 us
  starting transfers between devices: 18.7 us -> 47.6 us
  between operations: 14.2 us -> 0.9 us
  blocking collectives: 56.6 us -> 67.4 us
  local copies, waits for them, and re-layouts: 11 us -> 8.66 us
    reduce_scatter x1 -> x0, waiting for transfers between devices: 43.7 us -> none  [per_device(): summed = lax.psum_scatter(results, 'tp')]
    all_gather x1 -> x0, waiting for transfers between devices: 34.5 us -> none  [per_device(): arrived = lax.all_gather(slot_rows.reshape(slots, 2 * width), 'tp')]
    ppermute x2 -> x12, starting transfers between devices: 7.67 us -> 38.7 us  [shift(): lax.ppermute(rows, 'tp', [(i, (i + places) % size) for i in range(size)])]
    all_to_all x1, waiting for transfers between devices: 5.23 us -> 16.2 us  [per_device(): back = lax.all_to_all(summed.reshape(groups, 2, both), GROUP_AXES, 0, 0)]
    all_to_all x3, blocking collectives: 56.6 us -> 67.4 us  [the longest x1 32.6 us: per_device(): lax.all_to_all(sent.reshape(groups, 2, both + META), GROUP_AXES, 0, 0)]
    ppermute x2 -> x12, waiting for transfers between devices: 0.01 us -> 9.16 us  [shift(): lax.ppermute(rows, 'tp', [(i, (i + places) % size) for i in range(size)])]
    unnamed x16 -> x20, local copies, waits for them, and re-layouts: 6.15 us -> 3.03 us
    another operation x2 -> x0, local copies, waits for them, and re-layouts: 2.55 us -> none  [the longest x1 1.75 us: per_device(): summed.reshape(groups, 2, 2 * width)]
  transfers between devices with their start and end apart: 5 -> 13, of which waited for: 3 -> 7; matrix products, arithmetic and copies ran while one was open for 0% -> 1% of each run, Pallas kernels for 0% -> 1%
where the time goes in v2:
time: 157 us; the launch traced here: 156 us
  blocking collectives  67.4 us (43%)
  starting transfers between devices  47.6 us (30%)
  waiting for transfers between devices  25.4 us (16%)
  local copies, waits for them, and re-layouts  8.66 us (6%)
  Pallas kernels  5.64 us (4%)
    ppermute x12, starting transfers between devices, shift(): lax.ppermute(rows, 'tp', [(i, (i + places) % size) for i in range(size)])  38.7 us
    all_to_all x1, blocking collectives, per_device(): lax.all_to_all(sent.reshape(groups, 2, both + META), GROUP_AXES, 0, 0)  32.6 us
    all_to_all x1, blocking collectives, per_device(): lax.all_to_all(packed, 'tp', 0, 0).reshape(group_tokens, both + META)  19.1 us
    all_to_all x1, waiting for transfers between devices, per_device(): back = lax.all_to_all(summed.reshape(groups, 2, both), GROUP_AXES, 0, 0)  16.2 us
    all_to_all x1, blocking collectives, per_device(): lax.all_to_all(combined.reshape(parts, count, both + META), 'tp', 0, 0)  15.7 us
    ppermute x12, waiting for transfers between devices, shift(): lax.ppermute(rows, 'tp', [(i, (i + places) % size) for i in range(size)])  9.16 us
    all_to_all x1, starting transfers between devices, per_device(): back = lax.all_to_all(summed.reshape(groups, 2, both), GROUP_AXES, 0, 0)  8.97 us
    pallas_call x8, Pallas kernels, call(): pl.pallas_call(kernel, out_shape=shapes, compiler_params=pltpu.CompilerPa...  5.64 us
  transfers between devices with their start and end apart: 13, of which 7 were waited for; matrix products, arithmetic and copies ran while one was open for 1% of the time, Pallas kernels for 1%

profile of v2, /device:TPU:2, one launch (start us, length us, event | category | flops | bytes accessed | tf_op | source)
XLA Modules:
  0.0 155.8 jit_solution(17692195569076349102)
XLA Ops:
  0.7 0.6 copy-done.6
  1.3 0.0 copy-done.5
  1.3 0.8 copy-done.3
  2.2 0.8 copy-done.4
  3.0 0.1 shard_map.121
  3.1 19.1 %all_to_all.20 = bf16[8,8,2176]{2,1,0:T(8,128)(2,1)S(1)} all-to-all(bf16[8,8,2176]{2,1,0:T(8,128)(2,1)S(1)} %shard_map.121), channel_id=1, replica_groups=mesh['dp'=8,'ctx'=8,'tp'=8] {'tp'}, dimensions={0} | all-to-all | bytes 557056 | tf_op jit(solution)/shard_map/all_to_all | solution.py:260
  22.3 0.7 shard_map.122
  22.9 0.2 reshape.36
  23.2 0.0 copy-start.2
  23.2 32.6 %all_to_all.21 = bf16[64,2,2176]{2,1,0:T(2,128)(2,1)} all-to-all(bf16[64,2,2176]{2,1,0:T(2,128)(2,1)S(1)} %reshape.36), channel_id=1, replica_groups=mesh['dp'=8,'ctx'=8,'tp'=8] {'dp','ctx'}, dimensions={0} | all-to-all | bytes 1114112 | tf_op jit(solution)/shard_map/all_to_all | solution.py:262
  55.8 2.2 %reshape.37 = bf16[128,2176]{1,0:T(8,128)(2,1)} reshape(bf16[64,2,2176]{2,1,0:T(2,128)(2,1)} %all_to_all.21) | data formatting | bytes 1114112 | tf_op jit(solution)/shard_map/reshape | solution.py:264
  58.0 1.1 fusion
  59.1 2.5 %collective-permute-start = (bf16[128,1024]{1,0:T(8,128)(2,1)S(1)}, bf16[128,1024]{1,0:T(8,128)(2,1)S(1)}, u32[]{:S(2)}, u32[]{:S(2)}) collective-permute-start(bf16[128,1024]{1,0:T(8,128)(2,1)S(1)} %get-tuple-element.30.x0), channel_id=1, source_target_pairs={{0,1},{1,2},{2,3},{3,4},{4,5},{5,6},{6,7},{7,0},{8,9},{9,10},{10,1... | collective-permute-start | bytes 786440 | tf_op jit(solution)/shard_map/ppermute | solution.py:231
  61.6 4.6 %collective-permute-start.7 = (bf16[128,1024]{1,0:T(8,128)(2,1)S(1)}, bf16[128,1024]{1,0:T(8,128)(2,1)S(1)}, u32[]{:S(2)}, u32[]{:S(2)}) collective-permute-start(bf16[128,1024]{1,0:T(8,128)(2,1)S(1)} %get-tuple-element.29.d0), channel_id=1, source_target_pairs={{0,7},{1,0},{2,1},{3,2},{4,3},{5,4},{6,5},{7,6},{8,15},{9,8},{10,9... | collective-permute-start | bytes 786440 | tf_op jit(solution)/shard_map/ppermute | solution.py:231
  66.2 1.9 %collective-permute-start.1 = (bf16[128,1024]{1,0:T(8,128)(2,1)S(1)}, bf16[128,1024]{1,0:T(8,128)(2,1)S(1)}, u32[]{:S(2)}, u32[]{:S(2)}) collective-permute-start(bf16[128,1024]{1,0:T(8,128)(2,1)S(1)} %get-tuple-element.30.x0), channel_id=1, source_target_pairs={{0,7},{1,0},{2,1},{3,2},{4,3},{5,4},{6,5},{7,6},{8,15},{9,8},{10,9... | collective-permute-start | bytes 786440 | tf_op jit(solution)/shard_map/ppermute | solution.py:231
  68.1 1.2 collective-permute-done.xm1
  69.4 2.7 %collective-permute-start.2 = (bf16[128,1024]{1,0:T(8,128)(2,1)S(1)}, bf16[128,1024]{1,0:T(8,128)(2,1)S(1)}, u32[]{:S(2)}, u32[]{:S(2)}) collective-permute-start(bf16[128,1024]{1,0:T(8,128)(2,1)S(1)} %collective-permute-done.xm1), channel_id=1, source_target_pairs={{0,1},{1,2},{2,3},{3,4},{4,5},{5,6},{6,7},{7,0},{8,9},{9,10},{10,1... | collective-permute-start | bytes 786440 | tf_op jit(solution)/shard_map/ppermute | solution.py:231
  72.0 1.9 %collective-permute-start.6 = (bf16[128,1024]{1,0:T(8,128)(2,1)S(1)}, bf16[128,1024]{1,0:T(8,128)(2,1)S(1)}, u32[]{:S(2)}, u32[]{:S(2)}) collective-permute-start(bf16[128,1024]{1,0:T(8,128)(2,1)S(1)} %get-tuple-element.29.d0), channel_id=1, source_target_pairs={{0,1},{1,2},{2,3},{3,4},{4,5},{5,6},{6,7},{7,0},{8,9},{9,10},{10,1... | collective-permute-start | bytes 786440 | tf_op jit(solution)/shard_map/ppermute | solution.py:231
  74.0 0.0 collective-permute-done.7.dp1
  74.0 5.1 %collective-permute-start.8 = (bf16[128,1024]{1,0:T(8,128)(2,1)S(1)}, bf16[128,1024]{1,0:T(8,128)(2,1)S(1)}, u32[]{:S(2)}, u32[]{:S(2)}) collective-permute-start(bf16[128,1024]{1,0:T(8,128)(2,1)S(1)} %collective-permute-done.7.dp1), channel_id=1, source_target_pairs={{0,7},{1,0},{2,1},{3,2},{4,3},{5,4},{6,5},{7,6},{8,15},{9,8},{10,9... | collective-permute-start | bytes 786440 | tf_op jit(solution)/shard_map/ppermute | solution.py:231
  79.1 0.0 collective-permute-done.1.xp1
  79.1 2.3 %collective-permute-done.2.x2 = bf16[128,1024]{1,0:T(8,128)(2,1)S(1)} collective-permute-done((bf16[128,1024]{1,0:T(8,128)(2,1)S(1)}, bf16[128,1024]{1,0:T(8,128)(2,1)S(1)}, u32[]{:S(2)}, u32[]{:S(2)}) %collective-permute-start.2) | collective-permute-done | bytes 262176 | tf_op jit(solution)/shard_map/ppermute | solution.py:231
  81.5 1.1 shard_map.123
  82.6 1.7 %collective-permute-done.6.dm1 = bf16[128,1024]{1,0:T(8,128)(2,1)S(1)} collective-permute-done((bf16[128,1024]{1,0:T(8,128)(2,1)S(1)}, bf16[128,1024]{1,0:T(8,128)(2,1)S(1)}, u32[]{:S(2)}, u32[]{:S(2)}) %collective-permute-start.6) | collective-permute-done | bytes 262176 | tf_op jit(solution)/shard_map/ppermute | solution.py:231
  84.3 0.0 collective-permute-done.8.d2
  84.3 1.6 %shard_map.124 = (bf16[128,1024]{1,0:T(8,128)(2,1)S(1)}, bf16[128,1024]{1,0:T(8,128)(2,1)S(1)}, bf16[128,1024]{1,0:T(8,128)(2,1)S(1)}, bf16[128,1024]{1,0:T(8,128)(2,1)S(1)}) custom-call(bf16[128,1024]{1,0:T(8,128)(2,1)S(1)} %get-tuple-element.29.d0, bf16[128,1024]{1,0:T(8,128)(2,1)S(1)} %collective-permute-done.6.dm1, ...), custom_call_target="tpu_custom_call" | custom-call | tf_op jit(solution)/shard_map/pallas_call | solution.py:218
  85.9 1.9 %collective-permute-start.9 = (bf16[128,1024]{1,0:T(8,128)(2,1)S(1)}, bf16[128,1024]{1,0:T(8,128)(2,1)S(1)}, u32[]{:S(2)}, u32[]{:S(2)}) collective-permute-start(bf16[128,1024]{1,0:T(8,128)(2,1)S(1)} %get-tuple-element.24), channel_id=1, source_target_pairs={{0,1},{1,2},{2,3},{3,4},{4,5},{5,6},{6,7},{7,0},{8,9},{9,10},{10,1... | collective-permute-start | bytes 786440 | tf_op jit(solution)/shard_map/ppermute | solution.py:231
  87.8 5.1 %collective-permute-start.4 = (bf16[128,1024]{1,0:T(8,128)(2,1)S(1)}, bf16[128,1024]{1,0:T(8,128)(2,1)S(1)}, u32[]{:S(2)}, u32[]{:S(2)}) collective-permute-start(bf16[128,1024]{1,0:T(8,128)(2,1)S(1)} %get-tuple-element.19), channel_id=1, source_target_pairs={{0,7},{1,0},{2,1},{3,2},{4,3},{5,4},{6,5},{7,6},{8,15},{9,8},{10,9... | collective-permute-start | bytes 786440 | tf_op jit(solution)/shard_map/ppermute | solution.py:231
  93.0 3.1 %collective-permute-start.11 = (bf16[128,1024]{1,0:T(8,128)(2,1)S(1)}, bf16[128,1024]{1,0:T(8,128)(2,1)S(1)}, u32[]{:S(2)}, u32[]{:S(2)}) collective-permute-start(bf16[128,1024]{1,0:T(8,128)(2,1)S(1)} %get-tuple-element.25), channel_id=1, source_target_pairs={{0,7},{1,0},{2,1},{3,2},{4,3},{5,4},{6,5},{7,6},{8,15},{9,8},{10,9... | collective-permute-start | bytes 786440 | tf_op jit(solution)/shard_map/ppermute | solution.py:231
  96.1 2.8 %collective-permute-start.3 = (bf16[128,1024]{1,0:T(8,128)(2,1)S(1)}, bf16[128,1024]{1,0:T(8,128)(2,1)S(1)}, u32[]{:S(2)}, u32[]{:S(2)}) collective-permute-start(bf16[128,1024]{1,0:T(8,128)(2,1)S(1)} %get-tuple-element.17), channel_id=1, source_target_pairs={{0,1},{1,2},{2,3},{3,4},{4,5},{5,6},{6,7},{7,0},{8,9},{9,10},{10,1... | collective-permute-start | bytes 786440 | tf_op jit(solution)/shard_map/ppermute | solution.py:231
  98.8 0.1 add_convert_fusion
  98.9 1.9 %collective-permute-start.10 = (bf16[128,1024]{1,0:T(8,128)(2,1)S(1)}, bf16[128,1024]{1,0:T(8,128)(2,1)S(1)}, u32[]{:S(2)}, u32[]{:S(2)}) collective-permute-start(bf16[128,1024]{1,0:T(8,128)(2,1)S(1)} %add_convert_fusion), channel_id=1, source_target_pairs={{0,1},{1,2},{2,3},{3,4},{4,5},{5,6},{6,7},{7,0},{8,9},{9,10},{10,1... | collective-permute-start | bytes 786440 | tf_op jit(solution)/shard_map/ppermute | solution.py:231
  100.9 0.1 add_convert_fusion.1
  100.9 5.1 %collective-permute-start.5 = (bf16[128,1024]{1,0:T(8,128)(2,1)S(1)}, bf16[128,1024]{1,0:T(8,128)(2,1)S(1)}, u32[]{:S(2)}, u32[]{:S(2)}) collective-permute-start(bf16[128,1024]{1,0:T(8,128)(2,1)S(1)} %add_convert_fusion.1), channel_id=1, source_target_pairs={{0,7},{1,0},{2,1},{3,2},{4,3},{5,4},{6,5},{7,6},{8,15},{9,8},{10,9... | collective-permute-start | bytes 786440 | tf_op jit(solution)/shard_map/ppermute | solution.py:231
  106.1 0.1 collective-permute-done.3.y_right
  106.2 2.8 %collective-permute-done.10.g_right = bf16[128,1024]{1,0:T(8,128)(2,1)S(1)} collective-permute-done((bf16[128,1024]{1,0:T(8,128)(2,1)S(1)}, bf16[128,1024]{1,0:T(8,128)(2,1)S(1)}, u32[]{:S(2)}, u32[]{:S(2)}) %collective-permute-start.10) | collective-permute-done | bytes 262176 | tf_op jit(solution)/shard_map/ppermute | solution.py:231
  109.0 0.9 collective-permute-done.5.y_left
  109.9 0.2 shard_map.125
  110.1 1.2 reshape.38
  111.3 9.0 %all-to-all-start.2 = ((bf16[64,2,2048]{2,1,0:T(2,128)(2,1)}), bf16[64,2,2048]{2,1,0:T(2,128)(2,1)S(1)}, u32[]{:S(2)}, u32[]{:S(2)}) async-start(bf16[64,2,2048]{2,1,0:T(2,128)(2,1)} %reshape.38), calls=%async_computation.2 | async-start | bytes 1048576 | tf_op jit(solution)/shard_map/all_to_all | solution.py:298
  120.3 0.8 slice.18.near
  121.1 0.7 copy-done.9
  121.7 0.4 shard_map.126.weights
  122.1 16.2 %all-to-all-done.2 = bf16[64,2,2048]{2,1,0:T(2,128)(2,1)S(1)} async-done(((bf16[64,2,2048]{2,1,0:T(2,128)(2,1)}), bf16[64,2,2048]{2,1,0:T(2,128)(2,1)S(1)}, u32[]{:S(2)}, u32[]{:S(2)}) %all-to-all-start.2) | async-done | bytes 524320 | tf_op jit(solution)/shard_map/all_to_all | solution.py:298
  138.3 0.2 reshape.39.back
  138.5 0.8 shard_map.127
  139.4 15.7 %all_to_all.22.arrived = bf16[8,8,2176]{2,1,0:T(8,128)(2,1)S(1)} all-to-all(bf16[8,8,2176]{2,1,0:T(8,128)(2,1)S(1)} %bitcast.20), channel_id=1, replica_groups=mesh['dp'=8,'ctx'=8,'tp'=8] {'tp'}, dimensions={0} | all-to-all | bytes 557056 | tf_op jit(solution)/shard_map/all_to_all | solution.py:306
  155.0 0.7 shard_map.128
  (18 shorter events, 0.0 us)
Async XLA Ops:
  0.6 0.7 copy-start.6
  0.6 0.7 copy-start.8
  0.7 0.7 copy-start.5
  0.7 0.7 copy-start.7
  1.3 0.8 copy-start.3
  2.2 0.8 copy-start.4
  23.2 58.3 %copy-start.2 = (bf16[1,128,4096]{2,1,0:T(8,128)(2,1)S(1)}, bf16[1,128,4096]{2,1,0:T(8,128)(2,1)}, u32[]{:S(2)}) copy-start(bf16[1,128,4096]{2,1,0:T(8,128)(2,1)} %param.19) | copy-start | bytes 3145732
  55.8 25.7 %copy-start = (bf16[1,4096,128]{2,1,0:T(8,128)(2,1)S(1)}, bf16[1,4096,128]{2,1,0:T(8,128)(2,1)}, u32[]{:S(2)}) copy-start(bf16[1,4096,128]{2,1,0:T(8,128)(2,1)} %param.17) | copy-start | bytes 3145732
  55.8 25.7 %copy-start.1 = (bf16[1,4096,128]{2,1,0:T(8,128)(2,1)S(1)}, bf16[1,4096,128]{2,1,0:T(8,128)(2,1)}, u32[]{:S(2)}) copy-start(bf16[1,4096,128]{2,1,0:T(8,128)(2,1)} %param.18) | copy-start | bytes 3145732
  59.1 10.2 %collective-permute-start = (bf16[128,1024]{1,0:T(8,128)(2,1)S(1)}, bf16[128,1024]{1,0:T(8,128)(2,1)S(1)}, u32[]{:S(2)}, u32[]{:S(2)}) collective-permute-start(bf16[128,1024]{1,0:T(8,128)(2,1)S(1)} %get-tuple-element.30.x0), channel_id=1, source_target_pairs={{0,1},{1,2},{2,3},{3,4},{4,5},{5,6},{6,7},{7,0},{8,9},{9,10},{10,1... | collective-permute-start | bytes 786440 | tf_op jit(solution)/shard_map/ppermute | solution.py:231
  61.6 12.4 %collective-permute-start.7 = (bf16[128,1024]{1,0:T(8,128)(2,1)S(1)}, bf16[128,1024]{1,0:T(8,128)(2,1)S(1)}, u32[]{:S(2)}, u32[]{:S(2)}) collective-permute-start(bf16[128,1024]{1,0:T(8,128)(2,1)S(1)} %get-tuple-element.29.d0), channel_id=1, source_target_pairs={{0,7},{1,0},{2,1},{3,2},{4,3},{5,4},{6,5},{7,6},{8,15},{9,8},{10,9... | collective-permute-start | bytes 786440 | tf_op jit(solution)/shard_map/ppermute | solution.py:231
  66.2 13.0 %collective-permute-start.1 = (bf16[128,1024]{1,0:T(8,128)(2,1)S(1)}, bf16[128,1024]{1,0:T(8,128)(2,1)S(1)}, u32[]{:S(2)}, u32[]{:S(2)}) collective-permute-start(bf16[128,1024]{1,0:T(8,128)(2,1)S(1)} %get-tuple-element.30.x0), channel_id=1, source_target_pairs={{0,7},{1,0},{2,1},{3,2},{4,3},{5,4},{6,5},{7,6},{8,15},{9,8},{10,9... | collective-permute-start | bytes 786440 | tf_op jit(solution)/shard_map/ppermute | solution.py:231
  69.4 12.1 %collective-permute-start.2 = (bf16[128,1024]{1,0:T(8,128)(2,1)S(1)}, bf16[128,1024]{1,0:T(8,128)(2,1)S(1)}, u32[]{:S(2)}, u32[]{:S(2)}) collective-permute-start(bf16[128,1024]{1,0:T(8,128)(2,1)S(1)} %collective-permute-done.xm1), channel_id=1, source_target_pairs={{0,1},{1,2},{2,3},{3,4},{4,5},{5,6},{6,7},{7,0},{8,9},{9,10},{10,1... | collective-permute-start | bytes 786440 | tf_op jit(solution)/shard_map/ppermute | solution.py:231
  72.0 12.2 %collective-permute-start.6 = (bf16[128,1024]{1,0:T(8,128)(2,1)S(1)}, bf16[128,1024]{1,0:T(8,128)(2,1)S(1)}, u32[]{:S(2)}, u32[]{:S(2)}) collective-permute-start(bf16[128,1024]{1,0:T(8,128)(2,1)S(1)} %get-tuple-element.29.d0), channel_id=1, source_target_pairs={{0,1},{1,2},{2,3},{3,4},{4,5},{5,6},{6,7},{7,0},{8,9},{9,10},{10,1... | collective-permute-start | bytes 786440 | tf_op jit(solution)/shard_map/ppermute | solution.py:231
  74.0 10.3 %collective-permute-start.8 = (bf16[128,1024]{1,0:T(8,128)(2,1)S(1)}, bf16[128,1024]{1,0:T(8,128)(2,1)S(1)}, u32[]{:S(2)}, u32[]{:S(2)}) collective-permute-start(bf16[128,1024]{1,0:T(8,128)(2,1)S(1)} %collective-permute-done.7.dp1), channel_id=1, source_target_pairs={{0,7},{1,0},{2,1},{3,2},{4,3},{5,4},{6,5},{7,6},{8,15},{9,8},{10,9... | collective-permute-start | bytes 786440 | tf_op jit(solution)/shard_map/ppermute | solution.py:231
  85.9 12.9 %collective-permute-start.9 = (bf16[128,1024]{1,0:T(8,128)(2,1)S(1)}, bf16[128,1024]{1,0:T(8,128)(2,1)S(1)}, u32[]{:S(2)}, u32[]{:S(2)}) collective-permute-start(bf16[128,1024]{1,0:T(8,128)(2,1)S(1)} %get-tuple-element.24), channel_id=1, source_target_pairs={{0,1},{1,2},{2,3},{3,4},{4,5},{5,6},{6,7},{7,0},{8,9},{9,10},{10,1... | collective-permute-start | bytes 786440 | tf_op jit(solution)/shard_map/ppermute | solution.py:231
  87.8 13.0 %collective-permute-start.4 = (bf16[128,1024]{1,0:T(8,128)(2,1)S(1)}, bf16[128,1024]{1,0:T(8,128)(2,1)S(1)}, u32[]{:S(2)}, u32[]{:S(2)}) collective-permute-start(bf16[128,1024]{1,0:T(8,128)(2,1)S(1)} %get-tuple-element.19), channel_id=1, source_target_pairs={{0,7},{1,0},{2,1},{3,2},{4,3},{5,4},{6,5},{7,6},{8,15},{9,8},{10,9... | collective-permute-start | bytes 786440 | tf_op jit(solution)/shard_map/ppermute | solution.py:231
  93.0 13.1 %collective-permute-start.11 = (bf16[128,1024]{1,0:T(8,128)(2,1)S(1)}, bf16[128,1024]{1,0:T(8,128)(2,1)S(1)}, u32[]{:S(2)}, u32[]{:S(2)}) collective-permute-start(bf16[128,1024]{1,0:T(8,128)(2,1)S(1)} %get-tuple-element.25), channel_id=1, source_target_pairs={{0,7},{1,0},{2,1},{3,2},{4,3},{5,4},{6,5},{7,6},{8,15},{9,8},{10,9... | collective-permute-start | bytes 786440 | tf_op jit(solution)/shard_map/ppermute | solution.py:231
  96.1 10.1 %collective-permute-start.3 = (bf16[128,1024]{1,0:T(8,128)(2,1)S(1)}, bf16[128,1024]{1,0:T(8,128)(2,1)S(1)}, u32[]{:S(2)}, u32[]{:S(2)}) collective-permute-start(bf16[128,1024]{1,0:T(8,128)(2,1)S(1)} %get-tuple-element.17), channel_id=1, source_target_pairs={{0,1},{1,2},{2,3},{3,4},{4,5},{5,6},{6,7},{7,0},{8,9},{9,10},{10,1... | collective-permute-start | bytes 786440 | tf_op jit(solution)/shard_map/ppermute | solution.py:231
  98.9 10.1 %collective-permute-start.10 = (bf16[128,1024]{1,0:T(8,128)(2,1)S(1)}, bf16[128,1024]{1,0:T(8,128)(2,1)S(1)}, u32[]{:S(2)}, u32[]{:S(2)}) collective-permute-start(bf16[128,1024]{1,0:T(8,128)(2,1)S(1)} %add_convert_fusion), channel_id=1, source_target_pairs={{0,1},{1,2},{2,3},{3,4},{4,5},{5,6},{6,7},{7,0},{8,9},{9,10},{10,1... | collective-permute-start | bytes 786440 | tf_op jit(solution)/shard_map/ppermute | solution.py:231
  100.9 9.0 %collective-permute-start.5 = (bf16[128,1024]{1,0:T(8,128)(2,1)S(1)}, bf16[128,1024]{1,0:T(8,128)(2,1)S(1)}, u32[]{:S(2)}, u32[]{:S(2)}) collective-permute-start(bf16[128,1024]{1,0:T(8,128)(2,1)S(1)} %add_convert_fusion.1), channel_id=1, source_target_pairs={{0,7},{1,0},{2,1},{3,2},{4,3},{5,4},{6,5},{7,6},{8,15},{9,8},{10,9... | collective-permute-start | bytes 786440 | tf_op jit(solution)/shard_map/ppermute | solution.py:231
  111.3 27.0 %all-to-all-start.2 = ((bf16[64,2,2048]{2,1,0:T(2,128)(2,1)}), bf16[64,2,2048]{2,1,0:T(2,128)(2,1)S(1)}, u32[]{:S(2)}, u32[]{:S(2)}) async-start(bf16[64,2,2048]{2,1,0:T(2,128)(2,1)} %reshape.38), calls=%async_computation.2 | async-start | bytes 1048576 | tf_op jit(solution)/shard_map/all_to_all | solution.py:298
  121.1 0.7 copy-start.9

commit v3 on v2

--- a/solution.py
+++ b/solution.py
@@ -93,6 +93,14 @@
     second = jnp.concatenate([across[4:5, :], across[5:6, :]], axis=1)
     odd = lax.broadcasted_iota(jnp.int32, (slots, META), 0) % 2 == 1
     out[:, width : width + META] = jnp.where(odd, second, first).astype(BF16)
+
+
+def arrive_kernel(arrived, x, dy, near):
+    rows = arrived.shape[0] * arrived.shape[1]
+    width = x.shape[1]
+    x[...] = arrived[:, :, 0:width].reshape(rows, width)
+    dy[...] = arrived[:, :, width : 2 * width].reshape(rows, width)
+    near[...] = arrived[:, :, 2 * width :].reshape(rows, META)
 
 
 def weight_kernel(near, group, advantage, out):
@@ -161,12 +169,17 @@
 
 def sum_kernel(y0, y_right, y_left, g0, g_right, g_left, out):
     width = y0.shape[1]
-    out[:, 0:width] = (
-        y0[...].astype(F32) + y_right[...].astype(F32) + y_left[...].astype(F32)
-    ).astype(BF16)
-    out[:, width : 2 * width] = (
-        g0[...].astype(F32) + g_right[...].astype(F32) + g_left[...].astype(F32)
-    ).astype(BF16)
+    shape = (out.shape[0], out.shape[1], width)
+    out[:, :, 0:width] = (
+        (y0[...].astype(F32) + y_right[...].astype(F32) + y_left[...].astype(F32))
+        .astype(BF16)
+        .reshape(shape)
+    )
+    out[:, :, width : 2 * width] = (
+        (g0[...].astype(F32) + g_right[...].astype(F32) + g_left[...].astype(F32))
+        .astype(BF16)
+        .reshape(shape)
+    )
 
 
 def combine_kernel(back, group, weights, out):
@@ -214,10 +227,11 @@
         grad_gates[k : k + 1, :] = row_of(column, rows)
 
 
-def call(kernel, shapes, *operands, mib=8):
+def call(kernel, shapes, *operands, mib=8, flops=0):
     return pl.pallas_call(
         kernel,
         out_shape=shapes,
+        cost_estimate=pl.CostEstimate(flops=flops, bytes_accessed=0, transcendentals=0),
         compiler_params=pltpu.CompilerParams(vmem_limit_bytes=mib * 1024 * 1024),
     )(*operands)
 
@@ -259,11 +273,10 @@
     )
     group = lax.all_to_all(packed, "tp", 0, 0).reshape(group_tokens, both + META)
     sent = call(dispatch_kernel, struct(slots, both + META), group)
-    arrived = lax.all_to_all(
-        sent.reshape(groups, 2, both + META), GROUP_AXES, 0, 0
-    ).reshape(slots, both + META)
-
-    x0, d0 = arrived[:, 0:width], arrived[:, width:both]
+    arrived = lax.all_to_all(sent.reshape(groups, 2, both + META), GROUP_AXES, 0, 0)
+    x0, d0, near = call(
+        arrive_kernel, (struct(slots, width), struct(slots, width), struct(slots, META)), arrived
+    )
     xm1, dp1 = shift(x0, 1), shift(d0, -1)
     xp1, dm1 = shift(x0, -1), shift(d0, 1)
     x2, d2 = shift(xm1, 1), shift(dp1, -1)
@@ -271,7 +284,7 @@
     weights = call(
         weight_kernel,
         struct(group_tokens, META, dtype=F32),
-        arrived[:, both:],
+        near,
         group[:, both:],
         advantage.reshape(1, -1),
     )
@@ -293,9 +306,9 @@
     y_left = shift(add(ym1, shift(y2, -1)), -1)
     g_left = shift(gm1, -1)
     g_right = shift(add(gp1, shift(g2, 1)), 1)
-    summed = call(sum_kernel, struct(slots, both), y0, y_right, y_left, g0, g_right, g_left)
-
-    back = lax.all_to_all(summed.reshape(groups, 2, both), GROUP_AXES, 0, 0)
+    summed = call(sum_kernel, struct(groups, 2, both), y0, y_right, y_left, g0, g_right, g_left)
+
+    back = lax.all_to_all(summed, GROUP_AXES, 0, 0)
     combined = call(
         combine_kernel,
         struct(group_tokens, both + META),

time: 157 us -> 149 us (0.949)
  local copies, waits for them, and re-layouts: 8.66 us -> 3.44 us
  starting transfers between devices: 47.6 us -> 43.6 us
  waiting for transfers between devices: 25.4 us -> 28.2 us
  blocking collectives: 67.4 us -> 65.8 us
    reshape x2 -> x0, local copies, waits for them, and re-layouts: 3.39 us -> none  [the longest x1 2.24 us: per_device(): arrived = lax.all_to_all(sent.reshape(groups, 2, both + META), GROUP_AXES...]
    ppermute x12, waiting for transfers between devices: 9.16 us -> 11.2 us  [shift(): lax.ppermute(rows, 'tp', [(i, (i + places) % size) for i in range(size)])]
    ppermute x12, starting transfers between devices: 38.7 us -> 36.7 us  [shift(): lax.ppermute(rows, 'tp', [(i, (i + places) % size) for i in range(size)])]
    all_to_all x1, starting transfers between devices: 8.97 us -> 6.99 us  [per_device(): back = lax.all_to_all(summed, GROUP_AXES, 0, 0)]
    slice x2 -> x0, local copies, waits for them, and re-layouts: 1.83 us -> none  [the longest x1 1.06 us: per_device(): x0, d0 = (arrived[:, 0:width], arrived[:, width:both])]
    pallas_call x8 -> x9, Pallas kernels: 5.64 us -> 6.6 us  [call(): pl.pallas_call(kernel, out_shape=shapes, cost_estimate=pl.CostEstimate(fl...]
  transfers between devices with their start and end apart: 13 -> 13, of which waited for: 7 -> 6; matrix products, arithmetic and copies ran while one was open for 1% -> 0% of each run, Pallas kernels for 1% -> 2%
where the time goes in v3:
time: 149 us
  blocking collectives  65.8 us (44%)
  starting transfers between devices  43.6 us (29%)
  waiting for transfers between devices  28.2 us (19%)
  Pallas kernels  6.6 us (4%)
  local copies, waits for them, and re-layouts  3.44 us (2%)
    ppermute x12, starting transfers between devices, shift(): lax.ppermute(rows, 'tp', [(i, (i + places) % size) for i in range(size)])  36.7 us
    all_to_all x1, blocking collectives, per_device(): lax.all_to_all(sent.reshape(groups, 2, both + META), GROUP_AXES, 0, 0)  32.5 us
    all_to_all x1, blocking collectives, per_device(): lax.all_to_all(packed, 'tp', 0, 0).reshape(group_tokens, both + META)  19.1 us
    all_to_all x1, waiting for transfers between devices, per_device(): back = lax.all_to_all(summed, GROUP_AXES, 0, 0)  17 us
    all_to_all x1, blocking collectives, per_device(): lax.all_to_all(combined.reshape(parts, count, both + META), 'tp', 0, 0)  14.1 us
    ppermute x12, waiting for transfers between devices, shift(): lax.ppermute(rows, 'tp', [(i, (i + places) % size) for i in range(size)])  11.2 us
    all_to_all x1, starting transfers between devices, per_device(): back = lax.all_to_all(summed, GROUP_AXES, 0, 0)  6.99 us
    pallas_call x9, Pallas kernels, call(): pl.pallas_call(kernel, out_shape=shapes, cost_estimate=pl.CostEstimate(fl...  6.6 us
  transfers between devices with their start and end apart: 13, of which 6 were waited for; matrix products, arithmetic and copies ran while one was open for 0% of the time, Pallas kernels for 2%

profile of v3, /device:TPU:2, one launch (start us, length us, event | category | flops | bytes accessed | tf_op | source)
XLA Modules:
  0.0 148.7 jit_solution(15868828906041234333)
XLA Ops:
  0.7 0.6 copy-done.6
  1.3 0.0 copy-done.5
  1.3 0.8 copy-done.3
  2.2 0.8 copy-done.4
  3.0 0.1 shard_map.121
  3.1 19.1 %all_to_all.20 = bf16[8,8,2176]{2,1,0:T(8,128)(2,1)S(1)} all-to-all(bf16[8,8,2176]{2,1,0:T(8,128)(2,1)S(1)} %shard_map.121), channel_id=1, replica_groups=mesh['dp'=8,'ctx'=8,'tp'=8] {'tp'}, dimensions={0} | all-to-all | bytes 557056 | tf_op jit(solution)/shard_map/all_to_all | solution.py:274
  22.3 0.7 shard_map.122
  22.9 0.0 copy-start.1
  23.0 0.2 reshape.30
  23.2 0.0 copy-start
  23.2 32.5 %all_to_all.21.arrived = bf16[64,2,2176]{2,1,0:T(2,128)(2,1)S(1)} all-to-all(bf16[64,2,2176]{2,1,0:T(2,128)(2,1)S(1)} %reshape.30), channel_id=1, replica_groups=mesh['dp'=8,'ctx'=8,'tp'=8] {'dp','ctx'}, dimensions={0} | all-to-all | bytes 1114112 | tf_op jit(solution)/shard_map/all_to_all | solution.py:276
  55.7 0.1 shard_map.123
  55.8 2.5 %collective-permute-start = (bf16[128,1024]{1,0:T(8,128)(2,1)S(1)}, bf16[128,1024]{1,0:T(8,128)(2,1)S(1)}, u32[]{:S(2)}, u32[]{:S(2)}) collective-permute-start(bf16[128,1024]{1,0:T(8,128)(2,1)S(1)} %get-tuple-element.19.x0), channel_id=1, source_target_pairs={{0,1},{1,2},{2,3},{3,4},{4,5},{5,6},{6,7},{7,0},{8,9},{9,10},{10,1... | collective-permute-start | bytes 786440 | tf_op jit(solution)/shard_map/ppermute | solution.py:245
  58.3 4.6 %collective-permute-start.7 = (bf16[128,1024]{1,0:T(8,128)(2,1)S(1)}, bf16[128,1024]{1,0:T(8,128)(2,1)S(1)}, u32[]{:S(2)}, u32[]{:S(2)}) collective-permute-start(bf16[128,1024]{1,0:T(8,128)(2,1)S(1)} %get-tuple-element.24.d0), channel_id=1, source_target_pairs={{0,7},{1,0},{2,1},{3,2},{4,3},{5,4},{6,5},{7,6},{8,15},{9,8},{10,9... | collective-permute-start | bytes 786440 | tf_op jit(solution)/shard_map/ppermute | solution.py:245
  62.8 1.9 %collective-permute-start.1 = (bf16[128,1024]{1,0:T(8,128)(2,1)S(1)}, bf16[128,1024]{1,0:T(8,128)(2,1)S(1)}, u32[]{:S(2)}, u32[]{:S(2)}) collective-permute-start(bf16[128,1024]{1,0:T(8,128)(2,1)S(1)} %get-tuple-element.19.x0), channel_id=1, source_target_pairs={{0,7},{1,0},{2,1},{3,2},{4,3},{5,4},{6,5},{7,6},{8,15},{9,8},{10,9... | collective-permute-start | bytes 786440 | tf_op jit(solution)/shard_map/ppermute | solution.py:245
  64.8 1.2 collective-permute-done.xm1
  66.0 2.7 %collective-permute-start.2 = (bf16[128,1024]{1,0:T(8,128)(2,1)S(1)}, bf16[128,1024]{1,0:T(8,128)(2,1)S(1)}, u32[]{:S(2)}, u32[]{:S(2)}) collective-permute-start(bf16[128,1024]{1,0:T(8,128)(2,1)S(1)} %collective-permute-done.xm1), channel_id=1, source_target_pairs={{0,1},{1,2},{2,3},{3,4},{4,5},{5,6},{6,7},{7,0},{8,9},{9,10},{10,1... | collective-permute-start | bytes 786440 | tf_op jit(solution)/shard_map/ppermute | solution.py:245
  68.7 1.9 %collective-permute-start.6 = (bf16[128,1024]{1,0:T(8,128)(2,1)S(1)}, bf16[128,1024]{1,0:T(8,128)(2,1)S(1)}, u32[]{:S(2)}, u32[]{:S(2)}) collective-permute-start(bf16[128,1024]{1,0:T(8,128)(2,1)S(1)} %get-tuple-element.24.d0), channel_id=1, source_target_pairs={{0,1},{1,2},{2,3},{3,4},{4,5},{5,6},{6,7},{7,0},{8,9},{9,10},{10,1... | collective-permute-start | bytes 786440 | tf_op jit(solution)/shard_map/ppermute | solution.py:245
  70.6 0.0 collective-permute-done.7.dp1
  70.7 5.1 %collective-permute-start.8 = (bf16[128,1024]{1,0:T(8,128)(2,1)S(1)}, bf16[128,1024]{1,0:T(8,128)(2,1)S(1)}, u32[]{:S(2)}, u32[]{:S(2)}) collective-permute-start(bf16[128,1024]{1,0:T(8,128)(2,1)S(1)} %collective-permute-done.7.dp1), channel_id=1, source_target_pairs={{0,7},{1,0},{2,1},{3,2},{4,3},{5,4},{6,5},{7,6},{8,15},{9,8},{10,9... | collective-permute-start | bytes 786440 | tf_op jit(solution)/shard_map/ppermute | solution.py:245
  75.8 0.0 collective-permute-done.1.xp1
  75.8 2.3 %collective-permute-done.2.x2 = bf16[128,1024]{1,0:T(8,128)(2,1)S(1)} collective-permute-done((bf16[128,1024]{1,0:T(8,128)(2,1)S(1)}, bf16[128,1024]{1,0:T(8,128)(2,1)S(1)}, u32[]{:S(2)}, u32[]{:S(2)}) %collective-permute-start.2) | collective-permute-done | bytes 262176 | tf_op jit(solution)/shard_map/ppermute | solution.py:245
  78.2 1.1 shard_map.124
  79.3 1.9 %collective-permute-start.4 = (bf16[128,1024]{1,0:T(8,128)(2,1)S(1)}, bf16[128,1024]{1,0:T(8,128)(2,1)S(1)}, u32[]{:S(2)}, u32[]{:S(2)}) collective-permute-start(bf16[128,1024]{1,0:T(8,128)(2,1)S(1)} %get-tuple-element.23), channel_id=1, source_target_pairs={{0,7},{1,0},{2,1},{3,2},{4,3},{5,4},{6,5},{7,6},{8,15},{9,8},{10,9... | collective-permute-start | bytes 786440 | tf_op jit(solution)/shard_map/ppermute | solution.py:245
  81.2 0.0 collective-permute-done.6.dm1
  81.2 0.8 collective-permute-done.8.d2
  82.0 1.6 %shard_map.125 = (bf16[128,1024]{1,0:T(8,128)(2,1)S(1)}, bf16[128,1024]{1,0:T(8,128)(2,1)S(1)}, bf16[128,1024]{1,0:T(8,128)(2,1)S(1)}, bf16[128,1024]{1,0:T(8,128)(2,1)S(1)}) custom-call(bf16[128,1024]{1,0:T(8,128)(2,1)S(1)} %get-tuple-element.24.d0, bf16[128,1024]{1,0:T(8,128)(2,1)S(1)} %collective-permute-done.6.dm1, ...), custom_call_target="tpu_custom_call" | custom-call | tf_op jit(solution)/shard_map/pallas_call | solution.py:231
  83.6 3.1 %collective-permute-start.9 = (bf16[128,1024]{1,0:T(8,128)(2,1)S(1)}, bf16[128,1024]{1,0:T(8,128)(2,1)S(1)}, u32[]{:S(2)}, u32[]{:S(2)}) collective-permute-start(bf16[128,1024]{1,0:T(8,128)(2,1)S(1)} %get-tuple-element.29), channel_id=1, source_target_pairs={{0,1},{1,2},{2,3},{3,4},{4,5},{5,6},{6,7},{7,0},{8,9},{9,10},{10,1... | collective-permute-start | bytes 786440 | tf_op jit(solution)/shard_map/ppermute | solution.py:245
  86.8 1.9 %collective-permute-start.3 = (bf16[128,1024]{1,0:T(8,128)(2,1)S(1)}, bf16[128,1024]{1,0:T(8,128)(2,1)S(1)}, u32[]{:S(2)}, u32[]{:S(2)}) collective-permute-start(bf16[128,1024]{1,0:T(8,128)(2,1)S(1)} %get-tuple-element.21), channel_id=1, source_target_pairs={{0,1},{1,2},{2,3},{3,4},{4,5},{5,6},{6,7},{7,0},{8,9},{9,10},{10,1... | collective-permute-start | bytes 786440 | tf_op jit(solution)/shard_map/ppermute | solution.py:245
  88.7 5.1 %collective-permute-start.11 = (bf16[128,1024]{1,0:T(8,128)(2,1)S(1)}, bf16[128,1024]{1,0:T(8,128)(2,1)S(1)}, u32[]{:S(2)}, u32[]{:S(2)}) collective-permute-start(bf16[128,1024]{1,0:T(8,128)(2,1)S(1)} %get-tuple-element.30), channel_id=1, source_target_pairs={{0,7},{1,0},{2,1},{3,2},{4,3},{5,4},{6,5},{7,6},{8,15},{9,8},{10,9... | collective-permute-start | bytes 786440 | tf_op jit(solution)/shard_map/ppermute | solution.py:245
  93.8 0.0 collective-permute-done.4
  93.9 0.1 add_convert_fusion.1
  93.9 3.2 %collective-permute-start.5 = (bf16[128,1024]{1,0:T(8,128)(2,1)S(1)}, bf16[128,1024]{1,0:T(8,128)(2,1)S(1)}, u32[]{:S(2)}, u32[]{:S(2)}) collective-permute-start(bf16[128,1024]{1,0:T(8,128)(2,1)S(1)} %add_convert_fusion.1), channel_id=1, source_target_pairs={{0,7},{1,0},{2,1},{3,2},{4,3},{5,4},{6,5},{7,6},{8,15},{9,8},{10,9... | collective-permute-start | bytes 786440 | tf_op jit(solution)/shard_map/ppermute | solution.py:245
  97.1 0.1 add_convert_fusion
  97.2 2.7 %collective-permute-start.10 = (bf16[128,1024]{1,0:T(8,128)(2,1)S(1)}, bf16[128,1024]{1,0:T(8,128)(2,1)S(1)}, u32[]{:S(2)}, u32[]{:S(2)}) collective-permute-start(bf16[128,1024]{1,0:T(8,128)(2,1)S(1)} %add_convert_fusion), channel_id=1, source_target_pairs={{0,1},{1,2},{2,3},{3,4},{4,5},{5,6},{6,7},{7,0},{8,9},{9,10},{10,1... | collective-permute-start | bytes 786440 | tf_op jit(solution)/shard_map/ppermute | solution.py:245
  99.9 0.0 collective-permute-done.11.g_left
  99.9 2.3 %collective-permute-done.5.y_left = bf16[128,1024]{1,0:T(8,128)(2,1)S(1)} collective-permute-done((bf16[128,1024]{1,0:T(8,128)(2,1)S(1)}, bf16[128,1024]{1,0:T(8,128)(2,1)S(1)}, u32[]{:S(2)}, u32[]{:S(2)}) %collective-permute-start.5) | collective-permute-done | bytes 262176 | tf_op jit(solution)/shard_map/ppermute | solution.py:245
  102.2 4.5 %collective-permute-done.10.g_right = bf16[128,1024]{1,0:T(8,128)(2,1)S(1)} collective-permute-done((bf16[128,1024]{1,0:T(8,128)(2,1)S(1)}, bf16[128,1024]{1,0:T(8,128)(2,1)S(1)}, u32[]{:S(2)}, u32[]{:S(2)}) %collective-permute-start.10) | collective-permute-done | bytes 262176 | tf_op jit(solution)/shard_map/ppermute | solution.py:245
  106.7 1.1 shard_map.126
  107.7 7.0 %all-to-all-start.2 = ((bf16[64,2,2048]{2,1,0:T(2,128)(2,1)}), bf16[64,2,2048]{2,1,0:T(2,128)(2,1)S(1)}, u32[]{:S(2)}, u32[]{:S(2)}) async-start(bf16[64,2,2048]{2,1,0:T(2,128)(2,1)} %shard_map.126), calls=%async_computation.2 | async-start | bytes 1048576 | tf_op jit(solution)/shard_map/all_to_all | solution.py:311
  114.8 0.0 copy-start.9
  114.8 0.6 copy-done.9
  115.4 0.4 shard_map.127.weights
  115.8 17.0 %all-to-all-done.2 = bf16[64,2,2048]{2,1,0:T(2,128)(2,1)S(1)} async-done(((bf16[64,2,2048]{2,1,0:T(2,128)(2,1)}), bf16[64,2,2048]{2,1,0:T(2,128)(2,1)S(1)}, u32[]{:S(2)}, u32[]{:S(2)}) %all-to-all-start.2) | async-done | bytes 524320 | tf_op jit(solution)/shard_map/all_to_all | solution.py:311
  132.8 0.2 reshape.31.back
  133.0 0.8 shard_map.128
  133.8 14.1 %all_to_all.22.arrived = bf16[8,8,2176]{2,1,0:T(8,128)(2,1)S(1)} all-to-all(bf16[8,8,2176]{2,1,0:T(8,128)(2,1)S(1)} %bitcast.20), channel_id=1, replica_groups=mesh['dp'=8,'ctx'=8,'tp'=8] {'tp'}, dimensions={0} | all-to-all | bytes 557056 | tf_op jit(solution)/shard_map/all_to_all | solution.py:319
  148.0 0.7 shard_map.129
  (15 shorter events, 0.0 us)
Async XLA Ops:
  0.6 0.7 copy-start.6
  0.6 0.7 copy-start.8
  0.7 0.7 copy-start.5
  0.7 0.7 copy-start.7
  1.3 0.8 copy-start.3
  2.2 0.8 copy-start.4
  22.3 55.9 %copy-start.2 = (bf16[1,128,4096]{2,1,0:T(8,128)(2,1)S(1)}, bf16[1,128,4096]{2,1,0:T(8,128)(2,1)}, u32[]{:S(2)}) copy-start(bf16[1,128,4096]{2,1,0:T(8,128)(2,1)} %param.19) | copy-start | bytes 3145732
  22.9 55.2 %copy-start.1 = (bf16[1,4096,128]{2,1,0:T(8,128)(2,1)S(1)}, bf16[1,4096,128]{2,1,0:T(8,128)(2,1)}, u32[]{:S(2)}) copy-start(bf16[1,4096,128]{2,1,0:T(8,128)(2,1)} %param.18) | copy-start | bytes 3145732
  23.2 55.0 %copy-start = (bf16[1,4096,128]{2,1,0:T(8,128)(2,1)S(1)}, bf16[1,4096,128]{2,1,0:T(8,128)(2,1)}, u32[]{:S(2)}) copy-start(bf16[1,4096,128]{2,1,0:T(8,128)(2,1)} %param.17) | copy-start | bytes 3145732
  55.8 10.2 %collective-permute-start = (bf16[128,1024]{1,0:T(8,128)(2,1)S(1)}, bf16[128,1024]{1,0:T(8,128)(2,1)S(1)}, u32[]{:S(2)}, u32[]{:S(2)}) collective-permute-start(bf16[128,1024]{1,0:T(8,128)(2,1)S(1)} %get-tuple-element.19.x0), channel_id=1, source_target_pairs={{0,1},{1,2},{2,3},{3,4},{4,5},{5,6},{6,7},{7,0},{8,9},{9,10},{10,1... | collective-permute-start | bytes 786440 | tf_op jit(solution)/shard_map/ppermute | solution.py:245
  58.3 12.4 %collective-permute-start.7 = (bf16[128,1024]{1,0:T(8,128)(2,1)S(1)}, bf16[128,1024]{1,0:T(8,128)(2,1)S(1)}, u32[]{:S(2)}, u32[]{:S(2)}) collective-permute-start(bf16[128,1024]{1,0:T(8,128)(2,1)S(1)} %get-tuple-element.24.d0), channel_id=1, source_target_pairs={{0,7},{1,0},{2,1},{3,2},{4,3},{5,4},{6,5},{7,6},{8,15},{9,8},{10,9... | collective-permute-start | bytes 786440 | tf_op jit(solution)/shard_map/ppermute | solution.py:245
  62.8 13.0 %collective-permute-start.1 = (bf16[128,1024]{1,0:T(8,128)(2,1)S(1)}, bf16[128,1024]{1,0:T(8,128)(2,1)S(1)}, u32[]{:S(2)}, u32[]{:S(2)}) collective-permute-start(bf16[128,1024]{1,0:T(8,128)(2,1)S(1)} %get-tuple-element.19.x0), channel_id=1, source_target_pairs={{0,7},{1,0},{2,1},{3,2},{4,3},{5,4},{6,5},{7,6},{8,15},{9,8},{10,9... | collective-permute-start | bytes 786440 | tf_op jit(solution)/shard_map/ppermute | solution.py:245
  66.0 12.1 %collective-permute-start.2 = (bf16[128,1024]{1,0:T(8,128)(2,1)S(1)}, bf16[128,1024]{1,0:T(8,128)(2,1)S(1)}, u32[]{:S(2)}, u32[]{:S(2)}) collective-permute-start(bf16[128,1024]{1,0:T(8,128)(2,1)S(1)} %collective-permute-done.xm1), channel_id=1, source_target_pairs={{0,1},{1,2},{2,3},{3,4},{4,5},{5,6},{6,7},{7,0},{8,9},{9,10},{10,1... | collective-permute-start | bytes 786440 | tf_op jit(solution)/shard_map/ppermute | solution.py:245
  68.7 12.5 %collective-permute-start.6 = (bf16[128,1024]{1,0:T(8,128)(2,1)S(1)}, bf16[128,1024]{1,0:T(8,128)(2,1)S(1)}, u32[]{:S(2)}, u32[]{:S(2)}) collective-permute-start(bf16[128,1024]{1,0:T(8,128)(2,1)S(1)} %get-tuple-element.24.d0), channel_id=1, source_target_pairs={{0,1},{1,2},{2,3},{3,4},{4,5},{5,6},{6,7},{7,0},{8,9},{9,10},{10,1... | collective-permute-start | bytes 786440 | tf_op jit(solution)/shard_map/ppermute | solution.py:245
  70.7 11.4 %collective-permute-start.8 = (bf16[128,1024]{1,0:T(8,128)(2,1)S(1)}, bf16[128,1024]{1,0:T(8,128)(2,1)S(1)}, u32[]{:S(2)}, u32[]{:S(2)}) collective-permute-start(bf16[128,1024]{1,0:T(8,128)(2,1)S(1)} %collective-permute-done.7.dp1), channel_id=1, source_target_pairs={{0,7},{1,0},{2,1},{3,2},{4,3},{5,4},{6,5},{7,6},{8,15},{9,8},{10,9... | collective-permute-start | bytes 786440 | tf_op jit(solution)/shard_map/ppermute | solution.py:245
  79.3 14.6 %collective-permute-start.4 = (bf16[128,1024]{1,0:T(8,128)(2,1)S(1)}, bf16[128,1024]{1,0:T(8,128)(2,1)S(1)}, u32[]{:S(2)}, u32[]{:S(2)}) collective-permute-start(bf16[128,1024]{1,0:T(8,128)(2,1)S(1)} %get-tuple-element.23), channel_id=1, source_target_pairs={{0,7},{1,0},{2,1},{3,2},{4,3},{5,4},{6,5},{7,6},{8,15},{9,8},{10,9... | collective-permute-start | bytes 786440 | tf_op jit(solution)/shard_map/ppermute | solution.py:245
  83.6 13.5 %collective-permute-start.9 = (bf16[128,1024]{1,0:T(8,128)(2,1)S(1)}, bf16[128,1024]{1,0:T(8,128)(2,1)S(1)}, u32[]{:S(2)}, u32[]{:S(2)}) collective-permute-start(bf16[128,1024]{1,0:T(8,128)(2,1)S(1)} %get-tuple-element.29), channel_id=1, source_target_pairs={{0,1},{1,2},{2,3},{3,4},{4,5},{5,6},{6,7},{7,0},{8,9},{9,10},{10,1... | collective-permute-start | bytes 786440 | tf_op jit(solution)/shard_map/ppermute | solution.py:245
  86.8 13.1 %collective-permute-start.3 = (bf16[128,1024]{1,0:T(8,128)(2,1)S(1)}, bf16[128,1024]{1,0:T(8,128)(2,1)S(1)}, u32[]{:S(2)}, u32[]{:S(2)}) collective-permute-start(bf16[128,1024]{1,0:T(8,128)(2,1)S(1)} %get-tuple-element.21), channel_id=1, source_target_pairs={{0,1},{1,2},{2,3},{3,4},{4,5},{5,6},{6,7},{7,0},{8,9},{9,10},{10,1... | collective-permute-start | bytes 786440 | tf_op jit(solution)/shard_map/ppermute | solution.py:245
  88.7 11.2 %collective-permute-start.11 = (bf16[128,1024]{1,0:T(8,128)(2,1)S(1)}, bf16[128,1024]{1,0:T(8,128)(2,1)S(1)}, u32[]{:S(2)}, u32[]{:S(2)}) collective-permute-start(bf16[128,1024]{1,0:T(8,128)(2,1)S(1)} %get-tuple-element.30), channel_id=1, source_target_pairs={{0,7},{1,0},{2,1},{3,2},{4,3},{5,4},{6,5},{7,6},{8,15},{9,8},{10,9... | collective-permute-start | bytes 786440 | tf_op jit(solution)/shard_map/ppermute | solution.py:245
  93.9 8.3 %collective-permute-start.5 = (bf16[128,1024]{1,0:T(8,128)(2,1)S(1)}, bf16[128,1024]{1,0:T(8,128)(2,1)S(1)}, u32[]{:S(2)}, u32[]{:S(2)}) collective-permute-start(bf16[128,1024]{1,0:T(8,128)(2,1)S(1)} %add_convert_fusion.1), channel_id=1, source_target_pairs={{0,7},{1,0},{2,1},{3,2},{4,3},{5,4},{6,5},{7,6},{8,15},{9,8},{10,9... | collective-permute-start | bytes 786440 | tf_op jit(solution)/shard_map/ppermute | solution.py:245
  97.2 9.5 %collective-permute-start.10 = (bf16[128,1024]{1,0:T(8,128)(2,1)S(1)}, bf16[128,1024]{1,0:T(8,128)(2,1)S(1)}, u32[]{:S(2)}, u32[]{:S(2)}) collective-permute-start(bf16[128,1024]{1,0:T(8,128)(2,1)S(1)} %add_convert_fusion), channel_id=1, source_target_pairs={{0,1},{1,2},{2,3},{3,4},{4,5},{5,6},{6,7},{7,0},{8,9},{9,10},{10,1... | collective-permute-start | bytes 786440 | tf_op jit(solution)/shard_map/ppermute | solution.py:245
  107.7 25.1 %all-to-all-start.2 = ((bf16[64,2,2048]{2,1,0:T(2,128)(2,1)}), bf16[64,2,2048]{2,1,0:T(2,128)(2,1)S(1)}, u32[]{:S(2)}, u32[]{:S(2)}) async-start(bf16[64,2,2048]{2,1,0:T(2,128)(2,1)} %shard_map.126), calls=%async_computation.2 | async-start | bytes 1048576 | tf_op jit(solution)/shard_map/all_to_all | solution.py:311
  114.8 0.7 copy-start.9

commit v4 on v3

--- a/solution.py
+++ b/solution.py
@@ -9,6 +9,7 @@
 GROUP_AXES = ("dp", "ctx")
 META = 128
 CUTS = 4
+PACK_MIB = 60
 F32 = jnp.float32
 BF16 = jnp.bfloat16
 
@@ -42,7 +43,22 @@
     return total
 
 
-def pack_kernel(tokens, upstream, routes, gates, ids, ratio, out):
+def pack_kernel(
+    tokens_in, upstream_in, routes_in, gates_in, ids_in, ratio_in, advantage_in,
+    out, tokens, upstream, routes, gates, ids, ratio, advantage, sems,
+):
+    pairs = (
+        (tokens_in, tokens), (upstream_in, upstream), (routes_in, routes),
+        (gates_in, gates), (ids_in, ids), (ratio_in, ratio), (advantage_in, advantage),
+    )
+    copies = [
+        pltpu.make_async_copy(source, target, sems.at[place])
+        for place, (source, target) in enumerate(pairs)
+    ]
+    for copy in copies:
+        copy.start()
+    for copy in copies[::-1]:
+        copy.wait()
     parts, rows = out.shape[0], out.shape[1]
     width = tokens.shape[1] // CUTS
     rows_in = [routes[0:1, :].astype(F32), routes[1:2, :].astype(F32), ids[...].astype(F32)]
@@ -50,7 +66,11 @@
     gate_parts = split3(gates[...])
     for k in range(2):
         rows_in += [piece[k : k + 1, :] for piece in gate_parts]
-    meta = lanes(rows, [columns_of(row, rows) for row in rows_in]).astype(BF16)
+    columns = [columns_of(row, rows) for row in rows_in]
+    sequence = lax.broadcasted_iota(jnp.int32, (rows, advantage.shape[1]), 1).astype(F32)
+    own = jnp.where(columns[2] == sequence, advantage[...], 0.0)
+    columns += list(split3(jnp.sum(own, axis=1, keepdims=True)))
+    meta = lanes(rows, columns).astype(BF16)
     for t in range(parts):
         cut = slice((t % CUTS) * width, (t % CUTS + 1) * width)
         out[t, :, 0:width] = tokens[:, cut]
@@ -77,11 +97,13 @@
     return result
 
 
-def dispatch_kernel(group, out):
+def dispatch_kernel(group, out, hot_out):
     slots = out.shape[0]
     width = out.shape[1] - META
     meta = group[:, width : width + META].astype(F32)
     hots = slot_one_hots(meta, slots // 2, 2)
+    for k in range(2):
+        hot_out[k] = hots[k].astype(BF16)
     out[:, 0:width] = lax.dot_general(
         (hots[0] + hots[1]).astype(BF16),
         group[:, 0:width],
@@ -103,15 +125,15 @@
     near[...] = arrived[:, :, 2 * width :].reshape(rows, META)
 
 
-def weight_kernel(near, group, advantage, out):
+def sequence_weights(near, meta):
     groups = near.shape[0] // 2
-    count = group.shape[0]
+    count = meta.shape[0]
     here = lax.axis_index("dp") * lax.axis_size("ctx") + lax.axis_index("ctx")
     wanted = lax.broadcasted_iota(jnp.int32, (8, 2 * groups), 0)
     target = 2 * ((here + wanted // 2 - 1 + groups) % groups) + wanted % 2
     row = lax.broadcasted_iota(jnp.int32, (8, 2 * groups), 1)
     rows = jnp.dot((row == target).astype(BF16), near[...], preferred_element_type=F32)
-    own_id = group[:, 2:3].astype(F32)
+    own_id = meta[:, 2:3].astype(F32)
     total = tally = 0.0
     for beside in range(3):
         ids = rows[2 * beside : 2 * beside + 1, 0:count]
@@ -121,18 +143,21 @@
         same = (own_id == ids).astype(F32)
         tally = tally + jnp.sum(same, axis=1, keepdims=True)
         total = total + jnp.sum(same * ratio, axis=1, keepdims=True)
-    sequence = lax.broadcasted_iota(jnp.int32, (count, advantage.shape[1]), 1).astype(F32)
-    own = jnp.sum(jnp.where(own_id == sequence, advantage[...], 0.0), axis=1, keepdims=True)
-    weight = own * jnp.minimum(jnp.exp(total / tally), CLIP_HIGH)
-    out[...] = jnp.broadcast_to(weight, out.shape)
+    own = meta[:, 12:13].astype(F32) + meta[:, 13:14].astype(F32) + meta[:, 14:15].astype(F32)
+    return own * jnp.minimum(jnp.exp(total / tally), CLIP_HIGH)
 
 
 def cut_of(offset, width):
     return pl.multiple_of((lax.axis_index("tp") + offset + CUTS) % CUTS * width, width)
 
 
-def forward_kernel(x0, xm1, xp1, x2, w_gate, w_up, w_down, y0, ym1, yp1, y2, gate_out, up_out):
+def forward_kernel(
+    x0, xm1, xp1, x2, near, group, w_gate, w_up, w_down,
+    y0, ym1, yp1, y2, gate_out, up_out, weights,
+):
     width = x0.shape[1]
+    weight = sequence_weights(near, group[:, group.shape[1] - META :])
+    weights[...] = jnp.broadcast_to(weight, weights.shape)
     gate_pre = up_pre = 0.0
     for rows, offset in ((x0, 0), (xm1, -1), (xp1, 1), (x2, 2)):
         cut = pl.ds(cut_of(offset, width), width)
@@ -167,33 +192,27 @@
         ).astype(BF16)
 
 
-def sum_kernel(y0, y_right, y_left, g0, g_right, g_left, out):
-    width = y0.shape[1]
+def sum_kernel(y0, g0, left, y_right, g_right, out):
+    slots, width = y0.shape
     shape = (out.shape[0], out.shape[1], width)
-    out[:, :, 0:width] = (
-        (y0[...].astype(F32) + y_right[...].astype(F32) + y_left[...].astype(F32))
-        .astype(BF16)
-        .reshape(shape)
-    )
-    out[:, :, width : 2 * width] = (
-        (g0[...].astype(F32) + g_right[...].astype(F32) + g_left[...].astype(F32))
-        .astype(BF16)
-        .reshape(shape)
-    )
-
-
-def combine_kernel(back, group, weights, out):
-    slots, both = back.shape
+    for own, right, half in ((y0, y_right, 0), (g0, g_right, 1)):
+        total = own[...].astype(F32) + right[...].astype(F32)
+        total = total + left[half * slots : (half + 1) * slots, :].astype(F32)
+        out[:, :, half * width : (half + 1) * width] = total.astype(BF16).reshape(shape)
+
+
+def combine_kernel(back, group, weights, hots, out):
+    slots, both = back.shape[0] * back.shape[1], back.shape[2]
     width = both // 2
     count = group.shape[0]
+    returned = back[...].reshape(slots, both)
     meta = group[:, both : both + META].astype(F32)
-    hots = slot_one_hots(meta, slots // 2, 2)
     weight = weights[:, 0:1]
     upstream = group[:, width:both].astype(F32)
     total = 0.0
     columns = []
     for k in range(2):
-        picked = jnp.dot(hots[k].astype(BF16), back[...], preferred_element_type=F32)
+        picked = jnp.dot(hots[k], returned, preferred_element_type=F32)
         first = 6 + 3 * k
         gate = meta[:, first : first + 1] + meta[:, first + 1 : first + 2]
         gate = gate + meta[:, first + 2 : first + 3]
@@ -261,18 +280,27 @@
     slots = 2 * groups
     gate_local, up_local, down_local = w_gate[0], w_up[0], w_down[0]
 
-    packed = call(
-        pack_kernel,
-        struct(parts, count, both + META),
+    local = (
         tokens,
         upstream,
         routes.T,
         gate_weights.T,
         seq_ids.reshape(1, count),
         log_ratio.reshape(1, count),
-    )
+        advantage.reshape(1, -1),
+    )
+    packed = pl.pallas_call(
+        pack_kernel,
+        out_shape=struct(parts, count, both + META),
+        in_specs=[pl.BlockSpec(memory_space=pltpu.HBM)] * len(local),
+        scratch_shapes=[pltpu.VMEM(array.shape, array.dtype) for array in local]
+        + [pltpu.SemaphoreType.DMA((len(local),))],
+        compiler_params=pltpu.CompilerParams(vmem_limit_bytes=PACK_MIB * 1024 * 1024),
+    )(*local)
     group = lax.all_to_all(packed, "tp", 0, 0).reshape(group_tokens, both + META)
-    sent = call(dispatch_kernel, struct(slots, both + META), group)
+    sent, hots = call(
+        dispatch_kernel, (struct(slots, both + META), struct(2, group_tokens, slots)), group
+    )
     arrived = lax.all_to_all(sent.reshape(groups, 2, both + META), GROUP_AXES, 0, 0)
     x0, d0, near = call(
         arrive_kernel, (struct(slots, width), struct(slots, width), struct(slots, META)), arrived
@@ -281,19 +309,12 @@
     xp1, dm1 = shift(x0, -1), shift(d0, 1)
     x2, d2 = shift(xm1, 1), shift(dp1, -1)
 
-    weights = call(
-        weight_kernel,
-        struct(group_tokens, META, dtype=F32),
-        near,
-        group[:, both:],
-        advantage.reshape(1, -1),
-    )
     piece = struct(slots, width)
     inner = struct(slots, gate_local.shape[1], dtype=F32)
-    y0, ym1, yp1, y2, gate_pre, up_pre = call(
+    y0, ym1, yp1, y2, gate_pre, up_pre, weights = call(
         forward_kernel,
-        (piece,) * 4 + (inner,) * 2,
-        x0, xm1, xp1, x2, gate_local, up_local, down_local,
+        (piece,) * 4 + (inner,) * 2 + (struct(group_tokens, META, dtype=F32),),
+        x0, xm1, xp1, x2, near, group, gate_local, up_local, down_local,
         mib=16,
     )
     g0, gm1, gp1, g2 = call(
@@ -302,19 +323,19 @@
         d0, dm1, dp1, d2, gate_pre, up_pre, gate_local, up_local, down_local,
         mib=16,
     )
-    y_right = shift(yp1, 1)
-    y_left = shift(add(ym1, shift(y2, -1)), -1)
-    g_left = shift(gm1, -1)
-    g_right = shift(add(gp1, shift(g2, 1)), 1)
-    summed = call(sum_kernel, struct(groups, 2, both), y0, y_right, y_left, g0, g_right, g_left)
+    y_far, y_right, g_far = shift(y2, -1), shift(yp1, 1), shift(g2, 1)
+    left = shift(jnp.concatenate([add(ym1, y_far), gm1], axis=0), -1)
+    g_right = shift(add(gp1, g_far), 1)
+    summed = call(sum_kernel, struct(groups, 2, both), y0, g0, left, y_right, g_right)
 
     back = lax.all_to_all(summed, GROUP_AXES, 0, 0)
     combined = call(
         combine_kernel,
         struct(group_tokens, both + META),
-        back.reshape(slots, both),
+        back,
         group,
         weights,
+        hots,
     )
     home = lax.all_to_all(combined.reshape(parts, count, both + META), "tp", 0, 0)
     mixed, grad_tokens, grad_gates = call(

time: 149 us -> 148 us (level)
  blocking collectives: 65.8 us -> 92.5 us
  waiting for transfers between devices: 28.2 us -> 14.5 us
  starting transfers between devices: 43.6 us -> 31.8 us
  local copies, waits for them, and re-layouts: 3.44 us -> 0.23 us
    all_to_all x0 -> x1, blocking collectives: none -> 26.5 us  [per_device(): back = lax.all_to_all(summed, GROUP_AXES, 0, 0)]
    all_to_all x1 -> x0, waiting for transfers between devices: 17 us -> none  [per_device(): back = lax.all_to_all(summed, GROUP_AXES, 0, 0)]
    all_to_all x1 -> x0, starting transfers between devices: 6.99 us -> none  [per_device(): back = lax.all_to_all(summed, GROUP_AXES, 0, 0)]
    ppermute x12 -> x11, starting transfers between devices: 36.7 us -> 31.8 us  [shift(): lax.ppermute(rows, 'tp', [(i, (i + places) % size) for i in range(size)])]
    ppermute x12 -> x11, waiting for transfers between devices: 11.2 us -> 14.5 us  [shift(): lax.ppermute(rows, 'tp', [(i, (i + places) % size) for i in range(size)])]
    unnamed x20 -> x6, local copies, waits for them, and re-layouts: 3.03 us -> 0.02 us
    pallas_call x0 -> x1, Pallas kernels: none -> 1.81 us  [per_device(): pl.pallas_call(pack_kernel, out_shape=struct(parts, count, both + META),...]
    pallas_call x9 -> x7, Pallas kernels: 6.6 us -> 4.99 us  [call(): pl.pallas_call(kernel, out_shape=shapes, cost_estimate=pl.CostEstimate(fl...]
  transfers between devices with their start and end apart: 13 -> 11, of which waited for: 6 -> 6; matrix products, arithmetic and copies ran while one was open for 0% -> 0% of each run, Pallas kernels for 2% -> 2%
where the time goes in v4:
time: 148 us; the launch traced here: 147 us
  blocking collectives  92.5 us (62%)
  starting transfers between devices  31.8 us (21%)
  waiting for transfers between devices  14.5 us (10%)
  Pallas kernels  6.79 us (5%)
    all_to_all x1, blocking collectives, per_device(): lax.all_to_all(sent.reshape(groups, 2, both + META), GROUP_AXES, 0, 0)  32.5 us
    ppermute x11, starting transfers between devices, shift(): lax.ppermute(rows, 'tp', [(i, (i + places) % size) for i in range(size)])  31.8 us
    all_to_all x1, blocking collectives, per_device(): back = lax.all_to_all(summed, GROUP_AXES, 0, 0)  26.5 us
    all_to_all x1, blocking collectives, per_device(): lax.all_to_all(packed, 'tp', 0, 0).reshape(group_tokens, both + META)  19.5 us
    ppermute x11, waiting for transfers between devices, shift(): lax.ppermute(rows, 'tp', [(i, (i + places) % size) for i in range(size)])  14.5 us
    all_to_all x1, blocking collectives, per_device(): lax.all_to_all(combined.reshape(parts, count, both + META), 'tp', 0, 0)  14 us
    pallas_call x7, Pallas kernels, call(): pl.pallas_call(kernel, out_shape=shapes, cost_estimate=pl.CostEstimate(fl...  4.99 us
  transfers between devices with their start and end apart: 11, of which 6 were waited for; matrix products, arithmetic and copies ran while one was open for 0% of the time, Pallas kernels for 2%

profile of v4, /device:TPU:2, one launch (start us, length us, event | category | flops | bytes accessed | tf_op | source)
XLA Modules:
  0.0 146.9 jit_solution(15149483506124097406)
XLA Ops:
  0.6 1.8 %shard_map.121 = bf16[8,8,2176]{2,1,0:T(8,128)(2,1)} custom-call(bf16[8,4096]{1,0:T(8,128)(2,1)} %tokens_in.1, bf16[8,4096]{1,0:T(8,128)(2,1)} %upstream_in.1, s32[2,8]{1,0:T(2,128)} %bitcast.21, f32[2,8]{1,0:T(2,128)} %bitcast.22, s32[1,8]{1,0:T(1,128)} %bitcast.23, f32[1,8]{1,0:T(1,128)} %bitcast.24, f32[1,128]{1,0:T(1,128)} %bitcast.25), custom_call_target="tpu_custom_call" | custom-call | tf_op jit(solution)/shard_map/pallas_call | solution.py:292
  2.4 0.0 copy-start.2
  2.5 19.5 %all_to_all.20 = bf16[8,8,2176]{2,1,0:T(8,128)(2,1)S(1)} all-to-all(bf16[8,8,2176]{2,1,0:T(8,128)(2,1)} %shard_map.121), channel_id=1, replica_groups=mesh['dp'=8,'ctx'=8,'tp'=8] {'tp'}, dimensions={0} | all-to-all | bytes 557056 | tf_op jit(solution)/shard_map/all_to_all | solution.py:300
  21.9 0.7 shard_map.122
  22.6 0.0 copy-start.1
  22.6 0.2 reshape.28
  22.8 0.0 copy-start
  22.9 32.5 %all_to_all.21.arrived = bf16[64,2,2176]{2,1,0:T(2,128)(2,1)S(1)} all-to-all(bf16[64,2,2176]{2,1,0:T(2,128)(2,1)S(1)} %reshape.28), channel_id=1, replica_groups=mesh['dp'=8,'ctx'=8,'tp'=8] {'dp','ctx'}, dimensions={0} | all-to-all | bytes 1114112 | tf_op jit(solution)/shard_map/all_to_all | solution.py:304
  55.4 0.1 shard_map.123
  55.4 2.5 %collective-permute-start = (bf16[128,1024]{1,0:T(8,128)(2,1)S(1)}, bf16[128,1024]{1,0:T(8,128)(2,1)S(1)}, u32[]{:S(2)}, u32[]{:S(2)}) collective-permute-start(bf16[128,1024]{1,0:T(8,128)(2,1)S(1)} %get-tuple-element.23.x0), channel_id=1, source_target_pairs={{0,1},{1,2},{2,3},{3,4},{4,5},{5,6},{6,7},{7,0},{8,9},{9,10},{10,1... | collective-permute-start | bytes 786440 | tf_op jit(solution)/shard_map/ppermute | solution.py:264
  57.9 4.6 %collective-permute-start.4 = (bf16[128,1024]{1,0:T(8,128)(2,1)S(1)}, bf16[128,1024]{1,0:T(8,128)(2,1)S(1)}, u32[]{:S(2)}, u32[]{:S(2)}) collective-permute-start(bf16[128,1024]{1,0:T(8,128)(2,1)S(1)} %get-tuple-element.26.d0), channel_id=1, source_target_pairs={{0,7},{1,0},{2,1},{3,2},{4,3},{5,4},{6,5},{7,6},{8,15},{9,8},{10,9... | collective-permute-start | bytes 786440 | tf_op jit(solution)/shard_map/ppermute | solution.py:264
  62.5 1.9 %collective-permute-start.1 = (bf16[128,1024]{1,0:T(8,128)(2,1)S(1)}, bf16[128,1024]{1,0:T(8,128)(2,1)S(1)}, u32[]{:S(2)}, u32[]{:S(2)}) collective-permute-start(bf16[128,1024]{1,0:T(8,128)(2,1)S(1)} %get-tuple-element.23.x0), channel_id=1, source_target_pairs={{0,7},{1,0},{2,1},{3,2},{4,3},{5,4},{6,5},{7,6},{8,15},{9,8},{10,9... | collective-permute-start | bytes 786440 | tf_op jit(solution)/shard_map/ppermute | solution.py:264
  64.4 1.2 collective-permute-done.xm1
  65.7 2.7 %collective-permute-start.2 = (bf16[128,1024]{1,0:T(8,128)(2,1)S(1)}, bf16[128,1024]{1,0:T(8,128)(2,1)S(1)}, u32[]{:S(2)}, u32[]{:S(2)}) collective-permute-start(bf16[128,1024]{1,0:T(8,128)(2,1)S(1)} %collective-permute-done.xm1), channel_id=1, source_target_pairs={{0,1},{1,2},{2,3},{3,4},{4,5},{5,6},{6,7},{7,0},{8,9},{9,10},{10,1... | collective-permute-start | bytes 786440 | tf_op jit(solution)/shard_map/ppermute | solution.py:264
  68.4 1.9 %collective-permute-start.3 = (bf16[128,1024]{1,0:T(8,128)(2,1)S(1)}, bf16[128,1024]{1,0:T(8,128)(2,1)S(1)}, u32[]{:S(2)}, u32[]{:S(2)}) collective-permute-start(bf16[128,1024]{1,0:T(8,128)(2,1)S(1)} %get-tuple-element.26.d0), channel_id=1, source_target_pairs={{0,1},{1,2},{2,3},{3,4},{4,5},{5,6},{6,7},{7,0},{8,9},{9,10},{10,1... | collective-permute-start | bytes 786440 | tf_op jit(solution)/shard_map/ppermute | solution.py:264
  70.3 0.0 collective-permute-done.4.dp1
  70.3 5.1 %collective-permute-start.5 = (bf16[128,1024]{1,0:T(8,128)(2,1)S(1)}, bf16[128,1024]{1,0:T(8,128)(2,1)S(1)}, u32[]{:S(2)}, u32[]{:S(2)}) collective-permute-start(bf16[128,1024]{1,0:T(8,128)(2,1)S(1)} %collective-permute-done.4.dp1), channel_id=1, source_target_pairs={{0,7},{1,0},{2,1},{3,2},{4,3},{5,4},{6,5},{7,6},{8,15},{9,8},{10,9... | collective-permute-start | bytes 786440 | tf_op jit(solution)/shard_map/ppermute | solution.py:264
  75.5 0.0 collective-permute-done.1.xp1
  75.5 2.3 %collective-permute-done.2.x2 = bf16[128,1024]{1,0:T(8,128)(2,1)S(1)} collective-permute-done((bf16[128,1024]{1,0:T(8,128)(2,1)S(1)}, bf16[128,1024]{1,0:T(8,128)(2,1)S(1)}, u32[]{:S(2)}, u32[]{:S(2)}) %collective-permute-start.2) | collective-permute-done | bytes 262176 | tf_op jit(solution)/shard_map/ppermute | solution.py:264
  77.8 0.0 copy-done.2
  77.8 0.0 copy-done.1
  77.8 0.0 copy-done
  77.8 1.1 shard_map.124
  78.9 1.9 %collective-permute-start.6 = (bf16[128,1024]{1,0:T(8,128)(2,1)S(1)}, bf16[128,1024]{1,0:T(8,128)(2,1)S(1)}, u32[]{:S(2)}, u32[]{:S(2)}) collective-permute-start(bf16[128,1024]{1,0:T(8,128)(2,1)S(1)} %get-tuple-element.31), channel_id=1, source_target_pairs={{0,7},{1,0},{2,1},{3,2},{4,3},{5,4},{6,5},{7,6},{8,15},{9,8},{10,9... | collective-permute-start | bytes 786440 | tf_op jit(solution)/shard_map/ppermute | solution.py:264
  80.9 0.0 collective-permute-done.3.dm1
  80.9 0.8 collective-permute-done.5.d2
  81.7 1.6 %shard_map.125 = (bf16[128,1024]{1,0:T(8,128)(2,1)S(1)}, bf16[128,1024]{1,0:T(8,128)(2,1)S(1)}, bf16[128,1024]{1,0:T(8,128)(2,1)S(1)}, bf16[128,1024]{1,0:T(8,128)(2,1)S(1)}) custom-call(bf16[128,1024]{1,0:T(8,128)(2,1)S(1)} %get-tuple-element.26.d0, bf16[128,1024]{1,0:T(8,128)(2,1)S(1)} %collective-permute-done.3.dm1, ...), custom_call_target="tpu_custom_call" | custom-call | tf_op jit(solution)/shard_map/pallas_call | solution.py:250
  83.3 3.1 %collective-permute-start.9 = (bf16[128,1024]{1,0:T(8,128)(2,1)S(1)}, bf16[128,1024]{1,0:T(8,128)(2,1)S(1)}, u32[]{:S(2)}, u32[]{:S(2)}) collective-permute-start(bf16[128,1024]{1,0:T(8,128)(2,1)S(1)} %get-tuple-element.35), channel_id=1, source_target_pairs={{0,1},{1,2},{2,3},{3,4},{4,5},{5,6},{6,7},{7,0},{8,9},{9,10},{10,1... | collective-permute-start | bytes 786440 | tf_op jit(solution)/shard_map/ppermute | solution.py:264
  86.5 1.0 collective-permute-done.6
  87.5 0.1 add_convert_fusion.1
  87.6 3.4 %collective-permute-start.7 = (bf16[256,1024]{1,0:T(8,128)(2,1)S(1)}, bf16[256,1024]{1,0:T(8,128)(2,1)S(1)}, u32[]{:S(2)}, u32[]{:S(2)}) collective-permute-start(bf16[256,1024]{1,0:T(8,128)(2,1)S(1)} %pad_maximum_fusion), channel_id=1, source_target_pairs={{0,7},{1,0},{2,1},{3,2},{4,3},{5,4},{6,5},{7,6},{8,15},{9,8},{10,9... | collective-permute-start | bytes 1572872 | tf_op jit(solution)/shard_map/ppermute | solution.py:264
  91.0 2.5 %collective-permute-start.8 = (bf16[128,1024]{1,0:T(8,128)(2,1)S(1)}, bf16[128,1024]{1,0:T(8,128)(2,1)S(1)}, u32[]{:S(2)}, u32[]{:S(2)}) collective-permute-start(bf16[128,1024]{1,0:T(8,128)(2,1)S(1)} %get-tuple-element.33), channel_id=1, source_target_pairs={{0,1},{1,2},{2,3},{3,4},{4,5},{5,6},{6,7},{7,0},{8,9},{9,10},{10,1... | collective-permute-start | bytes 786440 | tf_op jit(solution)/shard_map/ppermute | solution.py:264
  93.5 0.0 collective-permute-done.9
  93.5 0.1 add_convert_fusion
  93.5 2.2 %collective-permute-start.10 = (bf16[128,1024]{1,0:T(8,128)(2,1)S(1)}, bf16[128,1024]{1,0:T(8,128)(2,1)S(1)}, u32[]{:S(2)}, u32[]{:S(2)}) collective-permute-start(bf16[128,1024]{1,0:T(8,128)(2,1)S(1)} %add_convert_fusion), channel_id=1, source_target_pairs={{0,1},{1,2},{2,3},{3,4},{4,5},{5,6},{6,7},{7,0},{8,9},{9,10},{10,1... | collective-permute-start | bytes 786440 | tf_op jit(solution)/shard_map/ppermute | solution.py:264
  95.7 6.2 %collective-permute-done.8.y_right = bf16[128,1024]{1,0:T(8,128)(2,1)S(1)} collective-permute-done((bf16[128,1024]{1,0:T(8,128)(2,1)S(1)}, bf16[128,1024]{1,0:T(8,128)(2,1)S(1)}, u32[]{:S(2)}, u32[]{:S(2)}) %collective-permute-start.8) | collective-permute-done | bytes 262176 | tf_op jit(solution)/shard_map/ppermute | solution.py:264
  102.0 2.8 %collective-permute-done.10.g_right = bf16[128,1024]{1,0:T(8,128)(2,1)S(1)} collective-permute-done((bf16[128,1024]{1,0:T(8,128)(2,1)S(1)}, bf16[128,1024]{1,0:T(8,128)(2,1)S(1)}, u32[]{:S(2)}, u32[]{:S(2)}) %collective-permute-start.10) | collective-permute-done | bytes 262176 | tf_op jit(solution)/shard_map/ppermute | solution.py:264
  104.8 0.0 collective-permute-done.7.left
  104.8 0.3 shard_map.126
  105.1 26.5 %all_to_all.22.back = bf16[64,2,2048]{2,1,0:T(2,128)(2,1)S(1)} all-to-all(bf16[64,2,2048]{2,1,0:T(2,128)(2,1)S(1)} %shard_map.126), channel_id=1, replica_groups=mesh['dp'=8,'ctx'=8,'tp'=8] {'dp','ctx'}, dimensions={0} | all-to-all | bytes 1048576 | tf_op jit(solution)/shard_map/all_to_all | solution.py:331
  131.6 0.5 shard_map.127
  132.1 14.0 %all_to_all.23.arrived = bf16[8,8,2176]{2,1,0:T(8,128)(2,1)S(1)} all-to-all(bf16[8,8,2176]{2,1,0:T(8,128)(2,1)S(1)} %bitcast.20), channel_id=1, replica_groups=mesh['dp'=8,'ctx'=8,'tp'=8] {'tp'}, dimensions={0} | all-to-all | bytes 557056 | tf_op jit(solution)/shard_map/all_to_all | solution.py:340
  146.1 0.7 shard_map.128
  (1 shorter events, 0.0 us)
Async XLA Ops:
  2.4 75.4 %copy-start.2 = (bf16[1,128,4096]{2,1,0:T(8,128)(2,1)S(1)}, bf16[1,128,4096]{2,1,0:T(8,128)(2,1)}, u32[]{:S(2)}) copy-start(bf16[1,128,4096]{2,1,0:T(8,128)(2,1)} %param.19) | copy-start | bytes 3145732
  22.6 55.2 %copy-start.1 = (bf16[1,4096,128]{2,1,0:T(8,128)(2,1)S(1)}, bf16[1,4096,128]{2,1,0:T(8,128)(2,1)}, u32[]{:S(2)}) copy-start(bf16[1,4096,128]{2,1,0:T(8,128)(2,1)} %param.18) | copy-start | bytes 3145732
  22.8 55.0 %copy-start = (bf16[1,4096,128]{2,1,0:T(8,128)(2,1)S(1)}, bf16[1,4096,128]{2,1,0:T(8,128)(2,1)}, u32[]{:S(2)}) copy-start(bf16[1,4096,128]{2,1,0:T(8,128)(2,1)} %param.17) | copy-start | bytes 3145732
  55.4 10.2 %collective-permute-start = (bf16[128,1024]{1,0:T(8,128)(2,1)S(1)}, bf16[128,1024]{1,0:T(8,128)(2,1)S(1)}, u32[]{:S(2)}, u32[]{:S(2)}) collective-permute-start(bf16[128,1024]{1,0:T(8,128)(2,1)S(1)} %get-tuple-element.23.x0), channel_id=1, source_target_pairs={{0,1},{1,2},{2,3},{3,4},{4,5},{5,6},{6,7},{7,0},{8,9},{9,10},{10,1... | collective-permute-start | bytes 786440 | tf_op jit(solution)/shard_map/ppermute | solution.py:264
  57.9 12.4 %collective-permute-start.4 = (bf16[128,1024]{1,0:T(8,128)(2,1)S(1)}, bf16[128,1024]{1,0:T(8,128)(2,1)S(1)}, u32[]{:S(2)}, u32[]{:S(2)}) collective-permute-start(bf16[128,1024]{1,0:T(8,128)(2,1)S(1)} %get-tuple-element.26.d0), channel_id=1, source_target_pairs={{0,7},{1,0},{2,1},{3,2},{4,3},{5,4},{6,5},{7,6},{8,15},{9,8},{10,9... | collective-permute-start | bytes 786440 | tf_op jit(solution)/shard_map/ppermute | solution.py:264
  62.5 13.0 %collective-permute-start.1 = (bf16[128,1024]{1,0:T(8,128)(2,1)S(1)}, bf16[128,1024]{1,0:T(8,128)(2,1)S(1)}, u32[]{:S(2)}, u32[]{:S(2)}) collective-permute-start(bf16[128,1024]{1,0:T(8,128)(2,1)S(1)} %get-tuple-element.23.x0), channel_id=1, source_target_pairs={{0,7},{1,0},{2,1},{3,2},{4,3},{5,4},{6,5},{7,6},{8,15},{9,8},{10,9... | collective-permute-start | bytes 786440 | tf_op jit(solution)/shard_map/ppermute | solution.py:264
  65.7 12.1 %collective-permute-start.2 = (bf16[128,1024]{1,0:T(8,128)(2,1)S(1)}, bf16[128,1024]{1,0:T(8,128)(2,1)S(1)}, u32[]{:S(2)}, u32[]{:S(2)}) collective-permute-start(bf16[128,1024]{1,0:T(8,128)(2,1)S(1)} %collective-permute-done.xm1), channel_id=1, source_target_pairs={{0,1},{1,2},{2,3},{3,4},{4,5},{5,6},{6,7},{7,0},{8,9},{9,10},{10,1... | collective-permute-start | bytes 786440 | tf_op jit(solution)/shard_map/ppermute | solution.py:264
  68.4 12.5 %collective-permute-start.3 = (bf16[128,1024]{1,0:T(8,128)(2,1)S(1)}, bf16[128,1024]{1,0:T(8,128)(2,1)S(1)}, u32[]{:S(2)}, u32[]{:S(2)}) collective-permute-start(bf16[128,1024]{1,0:T(8,128)(2,1)S(1)} %get-tuple-element.26.d0), channel_id=1, source_target_pairs={{0,1},{1,2},{2,3},{3,4},{4,5},{5,6},{6,7},{7,0},{8,9},{9,10},{10,1... | collective-permute-start | bytes 786440 | tf_op jit(solution)/shard_map/ppermute | solution.py:264
  70.3 11.4 %collective-permute-start.5 = (bf16[128,1024]{1,0:T(8,128)(2,1)S(1)}, bf16[128,1024]{1,0:T(8,128)(2,1)S(1)}, u32[]{:S(2)}, u32[]{:S(2)}) collective-permute-start(bf16[128,1024]{1,0:T(8,128)(2,1)S(1)} %collective-permute-done.4.dp1), channel_id=1, source_target_pairs={{0,7},{1,0},{2,1},{3,2},{4,3},{5,4},{6,5},{7,6},{8,15},{9,8},{10,9... | collective-permute-start | bytes 786440 | tf_op jit(solution)/shard_map/ppermute | solution.py:264
  78.9 8.5 %collective-permute-start.6 = (bf16[128,1024]{1,0:T(8,128)(2,1)S(1)}, bf16[128,1024]{1,0:T(8,128)(2,1)S(1)}, u32[]{:S(2)}, u32[]{:S(2)}) collective-permute-start(bf16[128,1024]{1,0:T(8,128)(2,1)S(1)} %get-tuple-element.31), channel_id=1, source_target_pairs={{0,7},{1,0},{2,1},{3,2},{4,3},{5,4},{6,5},{7,6},{8,15},{9,8},{10,9... | collective-permute-start | bytes 786440 | tf_op jit(solution)/shard_map/ppermute | solution.py:264
  83.3 10.2 %collective-permute-start.9 = (bf16[128,1024]{1,0:T(8,128)(2,1)S(1)}, bf16[128,1024]{1,0:T(8,128)(2,1)S(1)}, u32[]{:S(2)}, u32[]{:S(2)}) collective-permute-start(bf16[128,1024]{1,0:T(8,128)(2,1)S(1)} %get-tuple-element.35), channel_id=1, source_target_pairs={{0,1},{1,2},{2,3},{3,4},{4,5},{5,6},{6,7},{7,0},{8,9},{9,10},{10,1... | collective-permute-start | bytes 786440 | tf_op jit(solution)/shard_map/ppermute | solution.py:264
  87.6 17.2 %collective-permute-start.7 = (bf16[256,1024]{1,0:T(8,128)(2,1)S(1)}, bf16[256,1024]{1,0:T(8,128)(2,1)S(1)}, u32[]{:S(2)}, u32[]{:S(2)}) collective-permute-start(bf16[256,1024]{1,0:T(8,128)(2,1)S(1)} %pad_maximum_fusion), channel_id=1, source_target_pairs={{0,7},{1,0},{2,1},{3,2},{4,3},{5,4},{6,5},{7,6},{8,15},{9,8},{10,9... | collective-permute-start | bytes 1572872 | tf_op jit(solution)/shard_map/ppermute | solution.py:264
  91.0 11.0 %collective-permute-start.8 = (bf16[128,1024]{1,0:T(8,128)(2,1)S(1)}, bf16[128,1024]{1,0:T(8,128)(2,1)S(1)}, u32[]{:S(2)}, u32[]{:S(2)}) collective-permute-start(bf16[128,1024]{1,0:T(8,128)(2,1)S(1)} %get-tuple-element.33), channel_id=1, source_target_pairs={{0,1},{1,2},{2,3},{3,4},{4,5},{5,6},{6,7},{7,0},{8,9},{9,10},{10,1... | collective-permute-start | bytes 786440 | tf_op jit(solution)/shard_map/ppermute | solution.py:264
  93.5 11.2 %collective-permute-start.10 = (bf16[128,1024]{1,0:T(8,128)(2,1)S(1)}, bf16[128,1024]{1,0:T(8,128)(2,1)S(1)}, u32[]{:S(2)}, u32[]{:S(2)}) collective-permute-start(bf16[128,1024]{1,0:T(8,128)(2,1)S(1)} %add_convert_fusion), channel_id=1, source_target_pairs={{0,1},{1,2},{2,3},{3,4},{4,5},{5,6},{6,7},{7,0},{8,9},{9,10},{10,1... | collective-permute-start | bytes 786440 | tf_op jit(solution)/shard_map/ppermute | solution.py:264

commit v5 on v4

--- a/solution.py
+++ b/solution.py
@@ -43,22 +43,7 @@
     return total
 
 
-def pack_kernel(
-    tokens_in, upstream_in, routes_in, gates_in, ids_in, ratio_in, advantage_in,
-    out, tokens, upstream, routes, gates, ids, ratio, advantage, sems,
-):
-    pairs = (
-        (tokens_in, tokens), (upstream_in, upstream), (routes_in, routes),
-        (gates_in, gates), (ids_in, ids), (ratio_in, ratio), (advantage_in, advantage),
-    )
-    copies = [
-        pltpu.make_async_copy(source, target, sems.at[place])
-        for place, (source, target) in enumerate(pairs)
-    ]
-    for copy in copies:
-        copy.start()
-    for copy in copies[::-1]:
-        copy.wait()
+def pack_kernel(tokens, upstream, routes, gates, ids, ratio, advantage, out):
     parts, rows = out.shape[0], out.shape[1]
     width = tokens.shape[1] // CUTS
     rows_in = [routes[0:1, :].astype(F32), routes[1:2, :].astype(F32), ids[...].astype(F32)]
@@ -171,25 +156,37 @@
         rows[...] = jnp.dot(hidden, w_down[:, cut], preferred_element_type=F32).astype(BF16)
 
 
-def backward_kernel(d0, dm1, dp1, d2, gate, up, w_gate, w_up, w_down, g0, gm1, gp1, g2):
+CONTRACT_LAST = (((1,), (1,)), ((), ()))
+
+
+def input_grad(d_gate, d_up, w_gate, w_up, cut):
+    total = lax.dot_general(d_gate, w_gate[cut, :], CONTRACT_LAST, preferred_element_type=F32)
+    total += lax.dot_general(d_up, w_up[cut, :], CONTRACT_LAST, preferred_element_type=F32)
+    return total.astype(BF16)
+
+
+def backward_kernel(d0, dm1, dp1, d2, gate, up, w_gate, w_up, w_down, g2, gate_out, up_out):
     width = d0.shape[1]
-    contract = (((1,), (1,)), ((), ()))
     d_hidden = 0.0
     for rows, offset in ((d0, 0), (dm1, -1), (dp1, 1), (d2, 2)):
         cut = pl.ds(cut_of(offset, width), width)
         d_hidden += lax.dot_general(
-            rows[...], w_down[:, cut], contract, preferred_element_type=F32
+            rows[...], w_down[:, cut], CONTRACT_LAST, preferred_element_type=F32
         )
     gate_pre = gate[...]
     squash = jax.nn.sigmoid(gate_pre)
     d_gate = (d_hidden * up[...] * squash * (1.0 + gate_pre * (1.0 - squash))).astype(BF16)
     d_up = (d_hidden * (gate_pre * squash)).astype(BF16)
-    for rows, offset in ((g2, 2), (gp1, 1), (gm1, -1), (g0, 0)):
+    gate_out[...] = d_gate
+    up_out[...] = d_up
+    g2[...] = input_grad(d_gate, d_up, w_gate, w_up, pl.ds(cut_of(2, width), width))
+
+
+def rest_kernel(d_gate, d_up, w_gate, w_up, g0, gm1, gp1):
+    width = g0.shape[1]
+    for rows, offset in ((gm1, -1), (gp1, 1), (g0, 0)):
         cut = pl.ds(cut_of(offset, width), width)
-        rows[...] = (
-            lax.dot_general(d_gate, w_gate[cut, :], contract, preferred_element_type=F32)
-            + lax.dot_general(d_up, w_up[cut, :], contract, preferred_element_type=F32)
-        ).astype(BF16)
+        rows[...] = input_grad(d_gate[...], d_up[...], w_gate, w_up, cut)
 
 
 def sum_kernel(y0, g0, left, y_right, g_right, out):
@@ -246,11 +243,11 @@
         grad_gates[k : k + 1, :] = row_of(column, rows)
 
 
-def call(kernel, shapes, *operands, mib=8, flops=0):
+def call(kernel, shapes, *operands, mib=8):
     return pl.pallas_call(
         kernel,
         out_shape=shapes,
-        cost_estimate=pl.CostEstimate(flops=flops, bytes_accessed=0, transcendentals=0),
+        cost_estimate=pl.CostEstimate(flops=0, bytes_accessed=0, transcendentals=0),
         compiler_params=pltpu.CompilerParams(vmem_limit_bytes=mib * 1024 * 1024),
     )(*operands)
 
@@ -280,7 +277,9 @@
     slots = 2 * groups
     gate_local, up_local, down_local = w_gate[0], w_up[0], w_down[0]
 
-    local = (
+    packed = call(
+        pack_kernel,
+        struct(parts, count, both + META),
         tokens,
         upstream,
         routes.T,
@@ -288,15 +287,8 @@
         seq_ids.reshape(1, count),
         log_ratio.reshape(1, count),
         advantage.reshape(1, -1),
-    )
-    packed = pl.pallas_call(
-        pack_kernel,
-        out_shape=struct(parts, count, both + META),
-        in_specs=[pl.BlockSpec(memory_space=pltpu.HBM)] * len(local),
-        scratch_shapes=[pltpu.VMEM(array.shape, array.dtype) for array in local]
-        + [pltpu.SemaphoreType.DMA((len(local),))],
-        compiler_params=pltpu.CompilerParams(vmem_limit_bytes=PACK_MIB * 1024 * 1024),
-    )(*local)
+        mib=PACK_MIB,
+    )
     group = lax.all_to_all(packed, "tp", 0, 0).reshape(group_tokens, both + META)
     sent, hots = call(
         dispatch_kernel, (struct(slots, both + META), struct(2, group_tokens, slots)), group
@@ -317,11 +309,15 @@
         x0, xm1, xp1, x2, near, group, gate_local, up_local, down_local,
         mib=16,
     )
-    g0, gm1, gp1, g2 = call(
+    slope = struct(slots, gate_local.shape[1])
+    g2, d_gate, d_up = call(
         backward_kernel,
-        (piece,) * 4,
+        (piece, slope, slope),
         d0, dm1, dp1, d2, gate_pre, up_pre, gate_local, up_local, down_local,
         mib=16,
+    )
+    g0, gm1, gp1 = call(
+        rest_kernel, (piece,) * 3, d_gate, d_up, gate_local, up_local, mib=16
     )
     y_far, y_right, g_far = shift(y2, -1), shift(yp1, 1), shift(g2, 1)
     left = shift(jnp.concatenate([add(ym1, y_far), gm1], axis=0), -1)

time: 148 us -> 147 us (level)
    pallas_call x1 -> x0, Pallas kernels: 1.81 us -> none  [per_device(): pl.pallas_call(pack_kernel, out_shape=struct(parts, count, both + META),...]
    pallas_call x7 -> x9, Pallas kernels: 4.99 us -> 6.66 us  [call(): pl.pallas_call(kernel, out_shape=shapes, cost_estimate=pl.CostEstimate(fl...]
where the time goes in v5:
time: 147 us
  blocking collectives  92.4 us (63%)
  starting transfers between devices  31.9 us (22%)
  waiting for transfers between devices  14.5 us (10%)
  Pallas kernels  6.66 us (5%)
    all_to_all x1, blocking collectives, per_device(): lax.all_to_all(sent.reshape(groups, 2, both + META), GROUP_AXES, 0, 0)  32.5 us
    ppermute x11, starting transfers between devices, shift(): lax.ppermute(rows, 'tp', [(i, (i + places) % size) for i in range(size)])  31.9 us
    all_to_all x1, blocking collectives, per_device(): back = lax.all_to_all(summed, GROUP_AXES, 0, 0)  26.4 us
    all_to_all x1, blocking collectives, per_device(): lax.all_to_all(packed, 'tp', 0, 0).reshape(group_tokens, both + META)  19.5 us
    ppermute x11, waiting for transfers between devices, shift(): lax.ppermute(rows, 'tp', [(i, (i + places) % size) for i in range(size)])  14.5 us
    all_to_all x1, blocking collectives, per_device(): lax.all_to_all(combined.reshape(parts, count, both + META), 'tp', 0, 0)  14 us
    pallas_call x9, Pallas kernels, call(): pl.pallas_call(kernel, out_shape=shapes, cost_estimate=pl.CostEstimate(fl...  6.66 us
  transfers between devices with their start and end apart: 11, of which 6 were waited for; matrix products, arithmetic and copies ran while one was open for 0% of the time, Pallas kernels for 2%

profile of v5, /device:TPU:2, one launch (start us, length us, event | category | flops | bytes accessed | tf_op | source)
XLA Modules:
  0.0 146.7 jit_solution(2024899388621132918)
XLA Ops:
  0.6 1.8 %shard_map.121 = bf16[8,8,2176]{2,1,0:T(8,128)(2,1)} custom-call(bf16[8,4096]{1,0:T(8,128)(2,1)} %tokens.1, bf16[8,4096]{1,0:T(8,128)(2,1)} %upstream.1, s32[2,8]{1,0:T(2,128)} %bitcast.23, f32[2,8]{1,0:T(2,128)} %bitcast.24, s32[1,8]{1,0:T(1,128)} %bitcast.25, f32[1,8]{1,0:T(1,128)} %bitcast.26, f32[1,128]{1,0:T(1,128)} %bitcast.27), custom_call_target="tpu_custom_call" | custom-call | tf_op jit(solution)/shard_map/pallas_call | solution.py:247
  2.4 0.0 copy-start.2
  2.4 19.5 %all_to_all.20 = bf16[8,8,2176]{2,1,0:T(8,128)(2,1)S(1)} all-to-all(bf16[8,8,2176]{2,1,0:T(8,128)(2,1)} %shard_map.121), channel_id=1, replica_groups=mesh['dp'=8,'ctx'=8,'tp'=8] {'tp'}, dimensions={0} | all-to-all | bytes 557056 | tf_op jit(solution)/shard_map/all_to_all | solution.py:292
  21.9 0.7 shard_map.122
  22.6 0.0 copy-start.1
  22.6 0.2 reshape.28
  22.8 0.0 copy-start
  22.8 32.5 %all_to_all.21.arrived = bf16[64,2,2176]{2,1,0:T(2,128)(2,1)S(1)} all-to-all(bf16[64,2,2176]{2,1,0:T(2,128)(2,1)S(1)} %reshape.28), channel_id=1, replica_groups=mesh['dp'=8,'ctx'=8,'tp'=8] {'dp','ctx'}, dimensions={0} | all-to-all | bytes 1114112 | tf_op jit(solution)/shard_map/all_to_all | solution.py:296
  55.3 0.1 shard_map.123
  55.4 2.5 %collective-permute-start = (bf16[128,1024]{1,0:T(8,128)(2,1)S(1)}, bf16[128,1024]{1,0:T(8,128)(2,1)S(1)}, u32[]{:S(2)}, u32[]{:S(2)}) collective-permute-start(bf16[128,1024]{1,0:T(8,128)(2,1)S(1)} %get-tuple-element.25.x0), channel_id=1, source_target_pairs={{0,1},{1,2},{2,3},{3,4},{4,5},{5,6},{6,7},{7,0},{8,9},{9,10},{10,1... | collective-permute-start | bytes 786440 | tf_op jit(solution)/shard_map/ppermute | solution.py:261
  57.9 4.6 %collective-permute-start.4 = (bf16[128,1024]{1,0:T(8,128)(2,1)S(1)}, bf16[128,1024]{1,0:T(8,128)(2,1)S(1)}, u32[]{:S(2)}, u32[]{:S(2)}) collective-permute-start(bf16[128,1024]{1,0:T(8,128)(2,1)S(1)} %get-tuple-element.28.d0), channel_id=1, source_target_pairs={{0,7},{1,0},{2,1},{3,2},{4,3},{5,4},{6,5},{7,6},{8,15},{9,8},{10,9... | collective-permute-start | bytes 786440 | tf_op jit(solution)/shard_map/ppermute | solution.py:261
  62.5 1.9 %collective-permute-start.1 = (bf16[128,1024]{1,0:T(8,128)(2,1)S(1)}, bf16[128,1024]{1,0:T(8,128)(2,1)S(1)}, u32[]{:S(2)}, u32[]{:S(2)}) collective-permute-start(bf16[128,1024]{1,0:T(8,128)(2,1)S(1)} %get-tuple-element.25.x0), channel_id=1, source_target_pairs={{0,7},{1,0},{2,1},{3,2},{4,3},{5,4},{6,5},{7,6},{8,15},{9,8},{10,9... | collective-permute-start | bytes 786440 | tf_op jit(solution)/shard_map/ppermute | solution.py:261
  64.4 1.2 collective-permute-done.xm1
  65.6 2.7 %collective-permute-start.2 = (bf16[128,1024]{1,0:T(8,128)(2,1)S(1)}, bf16[128,1024]{1,0:T(8,128)(2,1)S(1)}, u32[]{:S(2)}, u32[]{:S(2)}) collective-permute-start(bf16[128,1024]{1,0:T(8,128)(2,1)S(1)} %collective-permute-done.xm1), channel_id=1, source_target_pairs={{0,1},{1,2},{2,3},{3,4},{4,5},{5,6},{6,7},{7,0},{8,9},{9,10},{10,1... | collective-permute-start | bytes 786440 | tf_op jit(solution)/shard_map/ppermute | solution.py:261
  68.3 1.9 %collective-permute-start.3 = (bf16[128,1024]{1,0:T(8,128)(2,1)S(1)}, bf16[128,1024]{1,0:T(8,128)(2,1)S(1)}, u32[]{:S(2)}, u32[]{:S(2)}) collective-permute-start(bf16[128,1024]{1,0:T(8,128)(2,1)S(1)} %get-tuple-element.28.d0), channel_id=1, source_target_pairs={{0,1},{1,2},{2,3},{3,4},{4,5},{5,6},{6,7},{7,0},{8,9},{9,10},{10,1... | collective-permute-start | bytes 786440 | tf_op jit(solution)/shard_map/ppermute | solution.py:261
  70.3 0.0 collective-permute-done.4.dp1
  70.3 5.1 %collective-permute-start.5 = (bf16[128,1024]{1,0:T(8,128)(2,1)S(1)}, bf16[128,1024]{1,0:T(8,128)(2,1)S(1)}, u32[]{:S(2)}, u32[]{:S(2)}) collective-permute-start(bf16[128,1024]{1,0:T(8,128)(2,1)S(1)} %collective-permute-done.4.dp1), channel_id=1, source_target_pairs={{0,7},{1,0},{2,1},{3,2},{4,3},{5,4},{6,5},{7,6},{8,15},{9,8},{10,9... | collective-permute-start | bytes 786440 | tf_op jit(solution)/shard_map/ppermute | solution.py:261
  75.4 0.0 collective-permute-done.1.xp1
  75.4 2.3 %collective-permute-done.2.x2 = bf16[128,1024]{1,0:T(8,128)(2,1)S(1)} collective-permute-done((bf16[128,1024]{1,0:T(8,128)(2,1)S(1)}, bf16[128,1024]{1,0:T(8,128)(2,1)S(1)}, u32[]{:S(2)}, u32[]{:S(2)}) %collective-permute-start.2) | collective-permute-done | bytes 262176 | tf_op jit(solution)/shard_map/ppermute | solution.py:261
  77.8 0.0 copy-done.2
  77.8 0.0 copy-done.1
  77.8 0.0 copy-done
  77.8 1.1 shard_map.124
  78.9 1.9 %collective-permute-start.6 = (bf16[128,1024]{1,0:T(8,128)(2,1)S(1)}, bf16[128,1024]{1,0:T(8,128)(2,1)S(1)}, u32[]{:S(2)}, u32[]{:S(2)}) collective-permute-start(bf16[128,1024]{1,0:T(8,128)(2,1)S(1)} %get-tuple-element.35), channel_id=1, source_target_pairs={{0,7},{1,0},{2,1},{3,2},{4,3},{5,4},{6,5},{7,6},{8,15},{9,8},{10,9... | collective-permute-start | bytes 786440 | tf_op jit(solution)/shard_map/ppermute | solution.py:261
  80.8 0.0 collective-permute-done.3.dm1
  80.8 0.8 collective-permute-done.5.d2
  81.6 0.9 shard_map.125
  82.5 3.1 %collective-permute-start.9 = (bf16[128,1024]{1,0:T(8,128)(2,1)S(1)}, bf16[128,1024]{1,0:T(8,128)(2,1)S(1)}, u32[]{:S(2)}, u32[]{:S(2)}) collective-permute-start(bf16[128,1024]{1,0:T(8,128)(2,1)S(1)} %get-tuple-element.39), channel_id=1, source_target_pairs={{0,1},{1,2},{2,3},{3,4},{4,5},{5,6},{6,7},{7,0},{8,9},{9,10},{10,1... | collective-permute-start | bytes 786440 | tf_op jit(solution)/shard_map/ppermute | solution.py:261
  85.7 0.6 shard_map.126
  86.3 1.1 collective-permute-done.6
  87.4 0.1 add_convert_fusion.1
  87.5 3.2 %collective-permute-start.7 = (bf16[256,1024]{1,0:T(8,128)(2,1)S(1)}, bf16[256,1024]{1,0:T(8,128)(2,1)S(1)}, u32[]{:S(2)}, u32[]{:S(2)}) collective-permute-start(bf16[256,1024]{1,0:T(8,128)(2,1)S(1)} %pad_maximum_fusion), channel_id=1, source_target_pairs={{0,7},{1,0},{2,1},{3,2},{4,3},{5,4},{6,5},{7,6},{8,15},{9,8},{10,9... | collective-permute-start | bytes 1572872 | tf_op jit(solution)/shard_map/ppermute | solution.py:261
  90.8 2.6 %collective-permute-start.8 = (bf16[128,1024]{1,0:T(8,128)(2,1)S(1)}, bf16[128,1024]{1,0:T(8,128)(2,1)S(1)}, u32[]{:S(2)}, u32[]{:S(2)}) collective-permute-start(bf16[128,1024]{1,0:T(8,128)(2,1)S(1)} %get-tuple-element.37), channel_id=1, source_target_pairs={{0,1},{1,2},{2,3},{3,4},{4,5},{5,6},{6,7},{7,0},{8,9},{9,10},{10,1... | collective-permute-start | bytes 786440 | tf_op jit(solution)/shard_map/ppermute | solution.py:261
  93.4 0.0 collective-permute-done.9
  93.4 0.1 add_convert_fusion
  93.5 2.3 %collective-permute-start.10 = (bf16[128,1024]{1,0:T(8,128)(2,1)S(1)}, bf16[128,1024]{1,0:T(8,128)(2,1)S(1)}, u32[]{:S(2)}, u32[]{:S(2)}) collective-permute-start(bf16[128,1024]{1,0:T(8,128)(2,1)S(1)} %add_convert_fusion), channel_id=1, source_target_pairs={{0,1},{1,2},{2,3},{3,4},{4,5},{5,6},{6,7},{7,0},{8,9},{9,10},{10,1... | collective-permute-start | bytes 786440 | tf_op jit(solution)/shard_map/ppermute | solution.py:261
  95.8 6.2 %collective-permute-done.8.y_right = bf16[128,1024]{1,0:T(8,128)(2,1)S(1)} collective-permute-done((bf16[128,1024]{1,0:T(8,128)(2,1)S(1)}, bf16[128,1024]{1,0:T(8,128)(2,1)S(1)}, u32[]{:S(2)}, u32[]{:S(2)}) %collective-permute-start.8) | collective-permute-done | bytes 262176 | tf_op jit(solution)/shard_map/ppermute | solution.py:261
  101.9 2.8 %collective-permute-done.10.g_right = bf16[128,1024]{1,0:T(8,128)(2,1)S(1)} collective-permute-done((bf16[128,1024]{1,0:T(8,128)(2,1)S(1)}, bf16[128,1024]{1,0:T(8,128)(2,1)S(1)}, u32[]{:S(2)}, u32[]{:S(2)}) %collective-permute-start.10) | collective-permute-done | bytes 262176 | tf_op jit(solution)/shard_map/ppermute | solution.py:261
  104.7 0.0 collective-permute-done.7.left
  104.7 0.3 shard_map.127
  105.0 26.4 %all_to_all.22.back = bf16[64,2,2048]{2,1,0:T(2,128)(2,1)S(1)} all-to-all(bf16[64,2,2048]{2,1,0:T(2,128)(2,1)S(1)} %shard_map.127), channel_id=1, replica_groups=mesh['dp'=8,'ctx'=8,'tp'=8] {'dp','ctx'}, dimensions={0} | all-to-all | bytes 1048576 | tf_op jit(solution)/shard_map/all_to_all | solution.py:327
  131.4 0.5 shard_map.128
  131.9 14.0 %all_to_all.23.arrived = bf16[8,8,2176]{2,1,0:T(8,128)(2,1)S(1)} all-to-all(bf16[8,8,2176]{2,1,0:T(8,128)(2,1)S(1)} %bitcast.22), channel_id=1, replica_groups=mesh['dp'=8,'ctx'=8,'tp'=8] {'tp'}, dimensions={0} | all-to-all | bytes 557056 | tf_op jit(solution)/shard_map/all_to_all | solution.py:336
  146.0 0.7 shard_map.129
  (1 shorter events, 0.0 us)
Async XLA Ops:
  2.4 75.4 %copy-start.2 = (bf16[1,128,4096]{2,1,0:T(8,128)(2,1)S(1)}, bf16[1,128,4096]{2,1,0:T(8,128)(2,1)}, u32[]{:S(2)}) copy-start(bf16[1,128,4096]{2,1,0:T(8,128)(2,1)} %param.19) | copy-start | bytes 3145732
  22.6 55.2 %copy-start.1 = (bf16[1,4096,128]{2,1,0:T(8,128)(2,1)S(1)}, bf16[1,4096,128]{2,1,0:T(8,128)(2,1)}, u32[]{:S(2)}) copy-start(bf16[1,4096,128]{2,1,0:T(8,128)(2,1)} %param.18) | copy-start | bytes 3145732
  22.8 55.0 %copy-start = (bf16[1,4096,128]{2,1,0:T(8,128)(2,1)S(1)}, bf16[1,4096,128]{2,1,0:T(8,128)(2,1)}, u32[]{:S(2)}) copy-start(bf16[1,4096,128]{2,1,0:T(8,128)(2,1)} %param.17) | copy-start | bytes 3145732
  55.4 10.2 %collective-permute-start = (bf16[128,1024]{1,0:T(8,128)(2,1)S(1)}, bf16[128,1024]{1,0:T(8,128)(2,1)S(1)}, u32[]{:S(2)}, u32[]{:S(2)}) collective-permute-start(bf16[128,1024]{1,0:T(8,128)(2,1)S(1)} %get-tuple-element.25.x0), channel_id=1, source_target_pairs={{0,1},{1,2},{2,3},{3,4},{4,5},{5,6},{6,7},{7,0},{8,9},{9,10},{10,1... | collective-permute-start | bytes 786440 | tf_op jit(solution)/shard_map/ppermute | solution.py:261
  57.9 12.4 %collective-permute-start.4 = (bf16[128,1024]{1,0:T(8,128)(2,1)S(1)}, bf16[128,1024]{1,0:T(8,128)(2,1)S(1)}, u32[]{:S(2)}, u32[]{:S(2)}) collective-permute-start(bf16[128,1024]{1,0:T(8,128)(2,1)S(1)} %get-tuple-element.28.d0), channel_id=1, source_target_pairs={{0,7},{1,0},{2,1},{3,2},{4,3},{5,4},{6,5},{7,6},{8,15},{9,8},{10,9... | collective-permute-start | bytes 786440 | tf_op jit(solution)/shard_map/ppermute | solution.py:261
  62.5 13.0 %collective-permute-start.1 = (bf16[128,1024]{1,0:T(8,128)(2,1)S(1)}, bf16[128,1024]{1,0:T(8,128)(2,1)S(1)}, u32[]{:S(2)}, u32[]{:S(2)}) collective-permute-start(bf16[128,1024]{1,0:T(8,128)(2,1)S(1)} %get-tuple-element.25.x0), channel_id=1, source_target_pairs={{0,7},{1,0},{2,1},{3,2},{4,3},{5,4},{6,5},{7,6},{8,15},{9,8},{10,9... | collective-permute-start | bytes 786440 | tf_op jit(solution)/shard_map/ppermute | solution.py:261
  65.6 12.1 %collective-permute-start.2 = (bf16[128,1024]{1,0:T(8,128)(2,1)S(1)}, bf16[128,1024]{1,0:T(8,128)(2,1)S(1)}, u32[]{:S(2)}, u32[]{:S(2)}) collective-permute-start(bf16[128,1024]{1,0:T(8,128)(2,1)S(1)} %collective-permute-done.xm1), channel_id=1, source_target_pairs={{0,1},{1,2},{2,3},{3,4},{4,5},{5,6},{6,7},{7,0},{8,9},{9,10},{10,1... | collective-permute-start | bytes 786440 | tf_op jit(solution)/shard_map/ppermute | solution.py:261
  68.3 12.5 %collective-permute-start.3 = (bf16[128,1024]{1,0:T(8,128)(2,1)S(1)}, bf16[128,1024]{1,0:T(8,128)(2,1)S(1)}, u32[]{:S(2)}, u32[]{:S(2)}) collective-permute-start(bf16[128,1024]{1,0:T(8,128)(2,1)S(1)} %get-tuple-element.28.d0), channel_id=1, source_target_pairs={{0,1},{1,2},{2,3},{3,4},{4,5},{5,6},{6,7},{7,0},{8,9},{9,10},{10,1... | collective-permute-start | bytes 786440 | tf_op jit(solution)/shard_map/ppermute | solution.py:261
  70.3 11.4 %collective-permute-start.5 = (bf16[128,1024]{1,0:T(8,128)(2,1)S(1)}, bf16[128,1024]{1,0:T(8,128)(2,1)S(1)}, u32[]{:S(2)}, u32[]{:S(2)}) collective-permute-start(bf16[128,1024]{1,0:T(8,128)(2,1)S(1)} %collective-permute-done.4.dp1), channel_id=1, source_target_pairs={{0,7},{1,0},{2,1},{3,2},{4,3},{5,4},{6,5},{7,6},{8,15},{9,8},{10,9... | collective-permute-start | bytes 786440 | tf_op jit(solution)/shard_map/ppermute | solution.py:261
  78.9 8.5 %collective-permute-start.6 = (bf16[128,1024]{1,0:T(8,128)(2,1)S(1)}, bf16[128,1024]{1,0:T(8,128)(2,1)S(1)}, u32[]{:S(2)}, u32[]{:S(2)}) collective-permute-start(bf16[128,1024]{1,0:T(8,128)(2,1)S(1)} %get-tuple-element.35), channel_id=1, source_target_pairs={{0,7},{1,0},{2,1},{3,2},{4,3},{5,4},{6,5},{7,6},{8,15},{9,8},{10,9... | collective-permute-start | bytes 786440 | tf_op jit(solution)/shard_map/ppermute | solution.py:261
  82.5 10.9 %collective-permute-start.9 = (bf16[128,1024]{1,0:T(8,128)(2,1)S(1)}, bf16[128,1024]{1,0:T(8,128)(2,1)S(1)}, u32[]{:S(2)}, u32[]{:S(2)}) collective-permute-start(bf16[128,1024]{1,0:T(8,128)(2,1)S(1)} %get-tuple-element.39), channel_id=1, source_target_pairs={{0,1},{1,2},{2,3},{3,4},{4,5},{5,6},{6,7},{7,0},{8,9},{9,10},{10,1... | collective-permute-start | bytes 786440 | tf_op jit(solution)/shard_map/ppermute | solution.py:261
  87.5 17.2 %collective-permute-start.7 = (bf16[256,1024]{1,0:T(8,128)(2,1)S(1)}, bf16[256,1024]{1,0:T(8,128)(2,1)S(1)}, u32[]{:S(2)}, u32[]{:S(2)}) collective-permute-start(bf16[256,1024]{1,0:T(8,128)(2,1)S(1)} %pad_maximum_fusion), channel_id=1, source_target_pairs={{0,7},{1,0},{2,1},{3,2},{4,3},{5,4},{6,5},{7,6},{8,15},{9,8},{10,9... | collective-permute-start | bytes 1572872 | tf_op jit(solution)/shard_map/ppermute | solution.py:261
  90.8 11.1 %collective-permute-start.8 = (bf16[128,1024]{1,0:T(8,128)(2,1)S(1)}, bf16[128,1024]{1,0:T(8,128)(2,1)S(1)}, u32[]{:S(2)}, u32[]{:S(2)}) collective-permute-start(bf16[128,1024]{1,0:T(8,128)(2,1)S(1)} %get-tuple-element.37), channel_id=1, source_target_pairs={{0,1},{1,2},{2,3},{3,4},{4,5},{5,6},{6,7},{7,0},{8,9},{9,10},{10,1... | collective-permute-start | bytes 786440 | tf_op jit(solution)/shard_map/ppermute | solution.py:261
  93.5 11.2 %collective-permute-start.10 = (bf16[128,1024]{1,0:T(8,128)(2,1)S(1)}, bf16[128,1024]{1,0:T(8,128)(2,1)S(1)}, u32[]{:S(2)}, u32[]{:S(2)}) collective-permute-start(bf16[128,1024]{1,0:T(8,128)(2,1)S(1)} %add_convert_fusion), channel_id=1, source_target_pairs={{0,1},{1,2},{2,3},{3,4},{4,5},{5,6},{6,7},{7,0},{8,9},{9,10},{10,1... | collective-permute-start | bytes 786440 | tf_op jit(solution)/shard_map/ppermute | solution.py:261

commit v6 on v5

--- a/solution.py
+++ b/solution.py
@@ -83,23 +83,25 @@
 
 
 def dispatch_kernel(group, out, hot_out):
-    slots = out.shape[0]
-    width = out.shape[1] - META
+    slots = out.shape[0] * out.shape[1]
+    width = out.shape[2] - META
     meta = group[:, width : width + META].astype(F32)
     hots = slot_one_hots(meta, slots // 2, 2)
     for k in range(2):
         hot_out[k] = hots[k].astype(BF16)
-    out[:, 0:width] = lax.dot_general(
+    rows = lax.dot_general(
         (hots[0] + hots[1]).astype(BF16),
         group[:, 0:width],
         (((0,), (0,)), ((), ())),
         preferred_element_type=F32,
     ).astype(BF16)
+    out[:, :, 0:width] = rows.reshape(out.shape[0], out.shape[1], width)
     across = meta.T
     first = jnp.concatenate([across[2:3, :], across[3:4, :]], axis=1)
     second = jnp.concatenate([across[4:5, :], across[5:6, :]], axis=1)
     odd = lax.broadcasted_iota(jnp.int32, (slots, META), 0) % 2 == 1
-    out[:, width : width + META] = jnp.where(odd, second, first).astype(BF16)
+    beside = jnp.where(odd, second, first).astype(BF16)
+    out[:, :, width : width + META] = beside.reshape(out.shape[0], out.shape[1], META)
 
 
 def arrive_kernel(arrived, x, dy, near):
@@ -291,9 +293,11 @@
     )
     group = lax.all_to_all(packed, "tp", 0, 0).reshape(group_tokens, both + META)
     sent, hots = call(
-        dispatch_kernel, (struct(slots, both + META), struct(2, group_tokens, slots)), group
-    )
-    arrived = lax.all_to_all(sent.reshape(groups, 2, both + META), GROUP_AXES, 0, 0)
+        dispatch_kernel,
+        (struct(groups, 2, both + META), struct(2, group_tokens, slots)),
+        group,
+    )
+    arrived = lax.all_to_all(sent, GROUP_AXES, 0, 0)
     x0, d0, near = call(
         arrive_kernel, (struct(slots, width), struct(slots, width), struct(slots, META)), arrived
     )

time: 147 us -> 147 us (level)
  transfers between devices with their start and end apart: 11 -> 11, of which waited for: 6 -> 5; matrix products, arithmetic and copies ran while one was open for 0% -> 0% of each run, Pallas kernels for 2% -> 2%
where the time goes in v6:
time: 147 us; the launch traced here: 146 us
  blocking collectives  91.6 us (62%)
  starting transfers between devices  32.3 us (22%)
  waiting for transfers between devices  13.5 us (9%)
  Pallas kernels  6.68 us (5%)
    all_to_all x1, blocking collectives, per_device(): arrived = lax.all_to_all(sent, GROUP_AXES, 0, 0)  32.4 us
    ppermute x11, starting transfers between devices, shift(): lax.ppermute(rows, 'tp', [(i, (i + places) % size) for i in range(size)])  32.3 us
    all_to_all x1, blocking collectives, per_device(): back = lax.all_to_all(summed, GROUP_AXES, 0, 0)  25.7 us
    all_to_all x1, blocking collectives, per_device(): lax.all_to_all(packed, 'tp', 0, 0).reshape(group_tokens, both + META)  19.5 us
    all_to_all x1, blocking collectives, per_device(): lax.all_to_all(combined.reshape(parts, count, both + META), 'tp', 0, 0)  14 us
    ppermute x11, waiting for transfers between devices, shift(): lax.ppermute(rows, 'tp', [(i, (i + places) % size) for i in range(size)])  13.5 us
    pallas_call x9, Pallas kernels, call(): pl.pallas_call(kernel, out_shape=shapes, cost_estimate=pl.CostEstimate(fl...  6.68 us
  transfers between devices with their start and end apart: 11, of which 5 were waited for; matrix products, arithmetic and copies ran while one was open for 0% of the time, Pallas kernels for 2%

profile of v6, /device:TPU:2, one launch (start us, length us, event | category | flops | bytes accessed | tf_op | source)
XLA Modules:
  0.0 146.4 jit_solution(5058740085949691650)
XLA Ops:
  0.6 1.8 %shard_map.121 = bf16[8,8,2176]{2,1,0:T(8,128)(2,1)} custom-call(bf16[8,4096]{1,0:T(8,128)(2,1)} %tokens.1, bf16[8,4096]{1,0:T(8,128)(2,1)} %upstream.1, s32[2,8]{1,0:T(2,128)} %bitcast.23, f32[2,8]{1,0:T(2,128)} %bitcast.24, s32[1,8]{1,0:T(1,128)} %bitcast.25, f32[1,8]{1,0:T(1,128)} %bitcast.26, f32[1,128]{1,0:T(1,128)} %bitcast.27), custom_call_target="tpu_custom_call" | custom-call | tf_op jit(solution)/shard_map/pallas_call | solution.py:249
  2.4 0.0 copy-start.1
  2.4 19.5 %all_to_all.20 = bf16[8,8,2176]{2,1,0:T(8,128)(2,1)S(1)} all-to-all(bf16[8,8,2176]{2,1,0:T(8,128)(2,1)} %shard_map.121), channel_id=1, replica_groups=mesh['dp'=8,'ctx'=8,'tp'=8] {'tp'}, dimensions={0} | all-to-all | bytes 557056 | tf_op jit(solution)/shard_map/all_to_all | solution.py:294
  21.9 0.0 copy-start
  21.9 0.7 shard_map.122
  22.6 32.4 %all_to_all.21.arrived = bf16[64,2,2176]{2,1,0:T(2,128)(2,1)S(1)} all-to-all(bf16[64,2,2176]{2,1,0:T(2,128)(2,1)S(1)} %get-tuple-element.24), channel_id=1, replica_groups=mesh['dp'=8,'ctx'=8,'tp'=8] {'dp','ctx'}, dimensions={0} | all-to-all | bytes 1114112 | tf_op jit(solution)/shard_map/all_to_all | solution.py:300
  55.0 0.1 shard_map.123
  55.0 2.5 %collective-permute-start = (bf16[128,1024]{1,0:T(8,128)(2,1)S(1)}, bf16[128,1024]{1,0:T(8,128)(2,1)S(1)}, u32[]{:S(2)}, u32[]{:S(2)}) collective-permute-start(bf16[128,1024]{1,0:T(8,128)(2,1)S(1)} %get-tuple-element.25.x0), channel_id=1, source_target_pairs={{0,1},{1,2},{2,3},{3,4},{4,5},{5,6},{6,7},{7,0},{8,9},{9,10},{10,1... | collective-permute-start | bytes 786440 | tf_op jit(solution)/shard_map/ppermute | solution.py:263
  57.5 4.6 %collective-permute-start.4 = (bf16[128,1024]{1,0:T(8,128)(2,1)S(1)}, bf16[128,1024]{1,0:T(8,128)(2,1)S(1)}, u32[]{:S(2)}, u32[]{:S(2)}) collective-permute-start(bf16[128,1024]{1,0:T(8,128)(2,1)S(1)} %get-tuple-element.28.d0), channel_id=1, source_target_pairs={{0,7},{1,0},{2,1},{3,2},{4,3},{5,4},{6,5},{7,6},{8,15},{9,8},{10,9... | collective-permute-start | bytes 786440 | tf_op jit(solution)/shard_map/ppermute | solution.py:263
  62.1 1.9 %collective-permute-start.1 = (bf16[128,1024]{1,0:T(8,128)(2,1)S(1)}, bf16[128,1024]{1,0:T(8,128)(2,1)S(1)}, u32[]{:S(2)}, u32[]{:S(2)}) collective-permute-start(bf16[128,1024]{1,0:T(8,128)(2,1)S(1)} %get-tuple-element.25.x0), channel_id=1, source_target_pairs={{0,7},{1,0},{2,1},{3,2},{4,3},{5,4},{6,5},{7,6},{8,15},{9,8},{10,9... | collective-permute-start | bytes 786440 | tf_op jit(solution)/shard_map/ppermute | solution.py:263
  64.0 1.2 collective-permute-done.xm1
  65.3 2.7 %collective-permute-start.2 = (bf16[128,1024]{1,0:T(8,128)(2,1)S(1)}, bf16[128,1024]{1,0:T(8,128)(2,1)S(1)}, u32[]{:S(2)}, u32[]{:S(2)}) collective-permute-start(bf16[128,1024]{1,0:T(8,128)(2,1)S(1)} %collective-permute-done.xm1), channel_id=1, source_target_pairs={{0,1},{1,2},{2,3},{3,4},{4,5},{5,6},{6,7},{7,0},{8,9},{9,10},{10,1... | collective-permute-start | bytes 786440 | tf_op jit(solution)/shard_map/ppermute | solution.py:263
  68.0 1.9 %collective-permute-start.3 = (bf16[128,1024]{1,0:T(8,128)(2,1)S(1)}, bf16[128,1024]{1,0:T(8,128)(2,1)S(1)}, u32[]{:S(2)}, u32[]{:S(2)}) collective-permute-start(bf16[128,1024]{1,0:T(8,128)(2,1)S(1)} %get-tuple-element.28.d0), channel_id=1, source_target_pairs={{0,1},{1,2},{2,3},{3,4},{4,5},{5,6},{6,7},{7,0},{8,9},{9,10},{10,1... | collective-permute-start | bytes 786440 | tf_op jit(solution)/shard_map/ppermute | solution.py:263
  69.9 0.0 collective-permute-done.4.dp1
  69.9 5.1 %collective-permute-start.5 = (bf16[128,1024]{1,0:T(8,128)(2,1)S(1)}, bf16[128,1024]{1,0:T(8,128)(2,1)S(1)}, u32[]{:S(2)}, u32[]{:S(2)}) collective-permute-start(bf16[128,1024]{1,0:T(8,128)(2,1)S(1)} %collective-permute-done.4.dp1), channel_id=1, source_target_pairs={{0,7},{1,0},{2,1},{3,2},{4,3},{5,4},{6,5},{7,6},{8,15},{9,8},{10,9... | collective-permute-start | bytes 786440 | tf_op jit(solution)/shard_map/ppermute | solution.py:263
  75.1 0.0 collective-permute-done.1.xp1
  75.1 2.3 %collective-permute-done.2.x2 = bf16[128,1024]{1,0:T(8,128)(2,1)S(1)} collective-permute-done((bf16[128,1024]{1,0:T(8,128)(2,1)S(1)}, bf16[128,1024]{1,0:T(8,128)(2,1)S(1)}, u32[]{:S(2)}, u32[]{:S(2)}) %collective-permute-start.2) | collective-permute-done | bytes 262176 | tf_op jit(solution)/shard_map/ppermute | solution.py:263
  77.4 0.0 copy-done.1
  77.4 0.0 copy-done
  77.4 0.0 copy-start.2
  77.4 1.2 copy-done.2
  78.6 1.1 shard_map.124
  79.7 1.9 %collective-permute-start.6 = (bf16[128,1024]{1,0:T(8,128)(2,1)S(1)}, bf16[128,1024]{1,0:T(8,128)(2,1)S(1)}, u32[]{:S(2)}, u32[]{:S(2)}) collective-permute-start(bf16[128,1024]{1,0:T(8,128)(2,1)S(1)} %get-tuple-element.35), channel_id=1, source_target_pairs={{0,7},{1,0},{2,1},{3,2},{4,3},{5,4},{6,5},{7,6},{8,15},{9,8},{10,9... | collective-permute-start | bytes 786440 | tf_op jit(solution)/shard_map/ppermute | solution.py:263
  81.7 0.0 collective-permute-done.3.dm1
  81.7 0.0 collective-permute-done.5.d2
  81.7 0.9 shard_map.125
  82.6 3.9 %collective-permute-start.9 = (bf16[128,1024]{1,0:T(8,128)(2,1)S(1)}, bf16[128,1024]{1,0:T(8,128)(2,1)S(1)}, u32[]{:S(2)}, u32[]{:S(2)}) collective-permute-start(bf16[128,1024]{1,0:T(8,128)(2,1)S(1)} %get-tuple-element.39), channel_id=1, source_target_pairs={{0,1},{1,2},{2,3},{3,4},{4,5},{5,6},{6,7},{7,0},{8,9},{9,10},{10,1... | collective-permute-start | bytes 786440 | tf_op jit(solution)/shard_map/ppermute | solution.py:263
  86.6 0.6 shard_map.126
  87.1 2.4 %collective-permute-done.6 = bf16[128,1024]{1,0:T(8,128)(2,1)S(1)} collective-permute-done((bf16[128,1024]{1,0:T(8,128)(2,1)S(1)}, bf16[128,1024]{1,0:T(8,128)(2,1)S(1)}, u32[]{:S(2)}, u32[]{:S(2)}) %collective-permute-start.6) | collective-permute-done | bytes 262176 | tf_op jit(solution)/shard_map/ppermute | solution.py:263
  89.5 0.1 add_convert_fusion.1
  89.7 1.9 %collective-permute-start.7 = (bf16[256,1024]{1,0:T(8,128)(2,1)S(1)}, bf16[256,1024]{1,0:T(8,128)(2,1)S(1)}, u32[]{:S(2)}, u32[]{:S(2)}) collective-permute-start(bf16[256,1024]{1,0:T(8,128)(2,1)S(1)} %pad_maximum_fusion), channel_id=1, source_target_pairs={{0,7},{1,0},{2,1},{3,2},{4,3},{5,4},{6,5},{7,6},{8,15},{9,8},{10,9... | collective-permute-start | bytes 1572872 | tf_op jit(solution)/shard_map/ppermute | solution.py:263
  91.6 3.9 %collective-permute-start.8 = (bf16[128,1024]{1,0:T(8,128)(2,1)S(1)}, bf16[128,1024]{1,0:T(8,128)(2,1)S(1)}, u32[]{:S(2)}, u32[]{:S(2)}) collective-permute-start(bf16[128,1024]{1,0:T(8,128)(2,1)S(1)} %get-tuple-element.37), channel_id=1, source_target_pairs={{0,1},{1,2},{2,3},{3,4},{4,5},{5,6},{6,7},{7,0},{8,9},{9,10},{10,1... | collective-permute-start | bytes 786440 | tf_op jit(solution)/shard_map/ppermute | solution.py:263
  95.5 0.0 collective-permute-done.9
  95.5 0.1 add_convert_fusion
  95.6 1.9 %collective-permute-start.10 = (bf16[128,1024]{1,0:T(8,128)(2,1)S(1)}, bf16[128,1024]{1,0:T(8,128)(2,1)S(1)}, u32[]{:S(2)}, u32[]{:S(2)}) collective-permute-start(bf16[128,1024]{1,0:T(8,128)(2,1)S(1)} %add_convert_fusion), channel_id=1, source_target_pairs={{0,1},{1,2},{2,3},{3,4},{4,5},{5,6},{6,7},{7,0},{8,9},{9,10},{10,1... | collective-permute-start | bytes 786440 | tf_op jit(solution)/shard_map/ppermute | solution.py:263
  97.5 3.6 %collective-permute-done.8.y_right = bf16[128,1024]{1,0:T(8,128)(2,1)S(1)} collective-permute-done((bf16[128,1024]{1,0:T(8,128)(2,1)S(1)}, bf16[128,1024]{1,0:T(8,128)(2,1)S(1)}, u32[]{:S(2)}, u32[]{:S(2)}) %collective-permute-start.8) | collective-permute-done | bytes 262176 | tf_op jit(solution)/shard_map/ppermute | solution.py:263
  101.1 4.0 %collective-permute-done.10.g_right = bf16[128,1024]{1,0:T(8,128)(2,1)S(1)} collective-permute-done((bf16[128,1024]{1,0:T(8,128)(2,1)S(1)}, bf16[128,1024]{1,0:T(8,128)(2,1)S(1)}, u32[]{:S(2)}, u32[]{:S(2)}) %collective-permute-start.10) | collective-permute-done | bytes 262176 | tf_op jit(solution)/shard_map/ppermute | solution.py:263
  105.1 0.0 collective-permute-done.7.left
  105.1 0.3 shard_map.127
  105.3 25.7 %all_to_all.22.back = bf16[64,2,2048]{2,1,0:T(2,128)(2,1)S(1)} all-to-all(bf16[64,2,2048]{2,1,0:T(2,128)(2,1)S(1)} %shard_map.127), channel_id=1, replica_groups=mesh['dp'=8,'ctx'=8,'tp'=8] {'dp','ctx'}, dimensions={0} | all-to-all | bytes 1048576 | tf_op jit(solution)/shard_map/all_to_all | solution.py:331
  131.1 0.5 shard_map.128
  131.6 14.0 %all_to_all.23.arrived = bf16[8,8,2176]{2,1,0:T(8,128)(2,1)S(1)} all-to-all(bf16[8,8,2176]{2,1,0:T(8,128)(2,1)S(1)} %bitcast.22), channel_id=1, replica_groups=mesh['dp'=8,'ctx'=8,'tp'=8] {'tp'}, dimensions={0} | all-to-all | bytes 557056 | tf_op jit(solution)/shard_map/all_to_all | solution.py:340
  145.6 0.7 shard_map.129
  (1 shorter events, 0.0 us)
Async XLA Ops:
  2.4 75.0 %copy-start.1 = (bf16[1,4096,128]{2,1,0:T(8,128)(2,1)S(1)}, bf16[1,4096,128]{2,1,0:T(8,128)(2,1)}, u32[]{:S(2)}) copy-start(bf16[1,4096,128]{2,1,0:T(8,128)(2,1)} %param.18) | copy-start | bytes 3145732
  21.9 55.5 %copy-start = (bf16[1,4096,128]{2,1,0:T(8,128)(2,1)S(1)}, bf16[1,4096,128]{2,1,0:T(8,128)(2,1)}, u32[]{:S(2)}) copy-start(bf16[1,4096,128]{2,1,0:T(8,128)(2,1)} %param.17) | copy-start | bytes 3145732
  55.0 10.2 %collective-permute-start = (bf16[128,1024]{1,0:T(8,128)(2,1)S(1)}, bf16[128,1024]{1,0:T(8,128)(2,1)S(1)}, u32[]{:S(2)}, u32[]{:S(2)}) collective-permute-start(bf16[128,1024]{1,0:T(8,128)(2,1)S(1)} %get-tuple-element.25.x0), channel_id=1, source_target_pairs={{0,1},{1,2},{2,3},{3,4},{4,5},{5,6},{6,7},{7,0},{8,9},{9,10},{10,1... | collective-permute-start | bytes 786440 | tf_op jit(solution)/shard_map/ppermute | solution.py:263
  57.5 12.4 %collective-permute-start.4 = (bf16[128,1024]{1,0:T(8,128)(2,1)S(1)}, bf16[128,1024]{1,0:T(8,128)(2,1)S(1)}, u32[]{:S(2)}, u32[]{:S(2)}) collective-permute-start(bf16[128,1024]{1,0:T(8,128)(2,1)S(1)} %get-tuple-element.28.d0), channel_id=1, source_target_pairs={{0,7},{1,0},{2,1},{3,2},{4,3},{5,4},{6,5},{7,6},{8,15},{9,8},{10,9... | collective-permute-start | bytes 786440 | tf_op jit(solution)/shard_map/ppermute | solution.py:263
  62.1 13.0 %collective-permute-start.1 = (bf16[128,1024]{1,0:T(8,128)(2,1)S(1)}, bf16[128,1024]{1,0:T(8,128)(2,1)S(1)}, u32[]{:S(2)}, u32[]{:S(2)}) collective-permute-start(bf16[128,1024]{1,0:T(8,128)(2,1)S(1)} %get-tuple-element.25.x0), channel_id=1, source_target_pairs={{0,7},{1,0},{2,1},{3,2},{4,3},{5,4},{6,5},{7,6},{8,15},{9,8},{10,9... | collective-permute-start | bytes 786440 | tf_op jit(solution)/shard_map/ppermute | solution.py:263
  65.3 12.1 %collective-permute-start.2 = (bf16[128,1024]{1,0:T(8,128)(2,1)S(1)}, bf16[128,1024]{1,0:T(8,128)(2,1)S(1)}, u32[]{:S(2)}, u32[]{:S(2)}) collective-permute-start(bf16[128,1024]{1,0:T(8,128)(2,1)S(1)} %collective-permute-done.xm1), channel_id=1, source_target_pairs={{0,1},{1,2},{2,3},{3,4},{4,5},{5,6},{6,7},{7,0},{8,9},{9,10},{10,1... | collective-permute-start | bytes 786440 | tf_op jit(solution)/shard_map/ppermute | solution.py:263
  68.0 13.7 %collective-permute-start.3 = (bf16[128,1024]{1,0:T(8,128)(2,1)S(1)}, bf16[128,1024]{1,0:T(8,128)(2,1)S(1)}, u32[]{:S(2)}, u32[]{:S(2)}) collective-permute-start(bf16[128,1024]{1,0:T(8,128)(2,1)S(1)} %get-tuple-element.28.d0), channel_id=1, source_target_pairs={{0,1},{1,2},{2,3},{3,4},{4,5},{5,6},{6,7},{7,0},{8,9},{9,10},{10,1... | collective-permute-start | bytes 786440 | tf_op jit(solution)/shard_map/ppermute | solution.py:263
  69.9 11.8 %collective-permute-start.5 = (bf16[128,1024]{1,0:T(8,128)(2,1)S(1)}, bf16[128,1024]{1,0:T(8,128)(2,1)S(1)}, u32[]{:S(2)}, u32[]{:S(2)}) collective-permute-start(bf16[128,1024]{1,0:T(8,128)(2,1)S(1)} %collective-permute-done.4.dp1), channel_id=1, source_target_pairs={{0,7},{1,0},{2,1},{3,2},{4,3},{5,4},{6,5},{7,6},{8,15},{9,8},{10,9... | collective-permute-start | bytes 786440 | tf_op jit(solution)/shard_map/ppermute | solution.py:263
  77.4 1.2 copy-start.2
  79.7 9.8 %collective-permute-start.6 = (bf16[128,1024]{1,0:T(8,128)(2,1)S(1)}, bf16[128,1024]{1,0:T(8,128)(2,1)S(1)}, u32[]{:S(2)}, u32[]{:S(2)}) collective-permute-start(bf16[128,1024]{1,0:T(8,128)(2,1)S(1)} %get-tuple-element.35), channel_id=1, source_target_pairs={{0,7},{1,0},{2,1},{3,2},{4,3},{5,4},{6,5},{7,6},{8,15},{9,8},{10,9... | collective-permute-start | bytes 786440 | tf_op jit(solution)/shard_map/ppermute | solution.py:263
  82.6 12.9 %collective-permute-start.9 = (bf16[128,1024]{1,0:T(8,128)(2,1)S(1)}, bf16[128,1024]{1,0:T(8,128)(2,1)S(1)}, u32[]{:S(2)}, u32[]{:S(2)}) collective-permute-start(bf16[128,1024]{1,0:T(8,128)(2,1)S(1)} %get-tuple-element.39), channel_id=1, source_target_pairs={{0,1},{1,2},{2,3},{3,4},{4,5},{5,6},{6,7},{7,0},{8,9},{9,10},{10,1... | collective-permute-start | bytes 786440 | tf_op jit(solution)/shard_map/ppermute | solution.py:263
  89.7 15.4 %collective-permute-start.7 = (bf16[256,1024]{1,0:T(8,128)(2,1)S(1)}, bf16[256,1024]{1,0:T(8,128)(2,1)S(1)}, u32[]{:S(2)}, u32[]{:S(2)}) collective-permute-start(bf16[256,1024]{1,0:T(8,128)(2,1)S(1)} %pad_maximum_fusion), channel_id=1, source_target_pairs={{0,7},{1,0},{2,1},{3,2},{4,3},{5,4},{6,5},{7,6},{8,15},{9,8},{10,9... | collective-permute-start | bytes 1572872 | tf_op jit(solution)/shard_map/ppermute | solution.py:263
  91.6 9.5 %collective-permute-start.8 = (bf16[128,1024]{1,0:T(8,128)(2,1)S(1)}, bf16[128,1024]{1,0:T(8,128)(2,1)S(1)}, u32[]{:S(2)}, u32[]{:S(2)}) collective-permute-start(bf16[128,1024]{1,0:T(8,128)(2,1)S(1)} %get-tuple-element.37), channel_id=1, source_target_pairs={{0,1},{1,2},{2,3},{3,4},{4,5},{5,6},{6,7},{7,0},{8,9},{9,10},{10,1... | collective-permute-start | bytes 786440 | tf_op jit(solution)/shard_map/ppermute | solution.py:263
  95.6 9.5 %collective-permute-start.10 = (bf16[128,1024]{1,0:T(8,128)(2,1)S(1)}, bf16[128,1024]{1,0:T(8,128)(2,1)S(1)}, u32[]{:S(2)}, u32[]{:S(2)}) collective-permute-start(bf16[128,1024]{1,0:T(8,128)(2,1)S(1)} %add_convert_fusion), channel_id=1, source_target_pairs={{0,1},{1,2},{2,3},{3,4},{4,5},{5,6},{6,7},{7,0},{8,9},{9,10},{10,1... | collective-permute-start | bytes 786440 | tf_op jit(solution)/shard_map/ppermute | solution.py:263

commit v7 on v6

--- a/solution.py
+++ b/solution.py
@@ -138,24 +138,47 @@
     return pl.multiple_of((lax.axis_index("tp") + offset + CUTS) % CUTS * width, width)
 
 
-def forward_kernel(
-    x0, xm1, xp1, x2, near, group, w_gate, w_up, w_down,
-    y0, ym1, yp1, y2, gate_out, up_out, weights,
-):
+def forward_first_kernel(x0, xm1, xp1, near, group, w_gate, w_up, gate, up, weights):
     width = x0.shape[1]
     weight = sequence_weights(near, group[:, group.shape[1] - META :])
     weights[...] = jnp.broadcast_to(weight, weights.shape)
     gate_pre = up_pre = 0.0
-    for rows, offset in ((x0, 0), (xm1, -1), (xp1, 1), (x2, 2)):
+    for rows, offset in ((x0, 0), (xm1, -1), (xp1, 1)):
         cut = pl.ds(cut_of(offset, width), width)
         gate_pre += jnp.dot(rows[...], w_gate[cut, :], preferred_element_type=F32)
         up_pre += jnp.dot(rows[...], w_up[cut, :], preferred_element_type=F32)
+    gate[...] = gate_pre
+    up[...] = up_pre
+
+
+def forward_kernel(x2, gate, up, w_gate, w_up, w_down, y2, hidden_out, gate_out, up_out):
+    width = x2.shape[1]
+    cut = pl.ds(cut_of(2, width), width)
+    gate_pre = gate[...] + jnp.dot(x2[...], w_gate[cut, :], preferred_element_type=F32)
+    up_pre = up[...] + jnp.dot(x2[...], w_up[cut, :], preferred_element_type=F32)
     gate_out[...] = gate_pre
     up_out[...] = up_pre
     hidden = (gate_pre * jax.nn.sigmoid(gate_pre) * up_pre).astype(BF16)
-    for rows, offset in ((y2, 2), (yp1, 1), (ym1, -1), (y0, 0)):
+    hidden_out[...] = hidden
+    y2[...] = jnp.dot(hidden, w_down[:, cut], preferred_element_type=F32).astype(BF16)
+
+
+def forward_rest_kernel(hidden, w_down, y0, ym1, yp1):
+    width = y0.shape[1]
+    for rows, offset in ((yp1, 1), (ym1, -1), (y0, 0)):
         cut = pl.ds(cut_of(offset, width), width)
-        rows[...] = jnp.dot(hidden, w_down[:, cut], preferred_element_type=F32).astype(BF16)
+        rows[...] = jnp.dot(hidden[...], w_down[:, cut], preferred_element_type=F32).astype(BF16)
+
+
+def backward_first_kernel(d0, dm1, dp1, w_down, out):
+    width = d0.shape[1]
+    d_hidden = 0.0
+    for rows, offset in ((d0, 0), (dm1, -1), (dp1, 1)):
+        cut = pl.ds(cut_of(offset, width), width)
+        d_hidden += lax.dot_general(
+            rows[...], w_down[:, cut], CONTRACT_LAST, preferred_element_type=F32
+        )
+    out[...] = d_hidden
 
 
 CONTRACT_LAST = (((1,), (1,)), ((), ()))
@@ -167,21 +190,19 @@
     return total.astype(BF16)
 
 
-def backward_kernel(d0, dm1, dp1, d2, gate, up, w_gate, w_up, w_down, g2, gate_out, up_out):
-    width = d0.shape[1]
-    d_hidden = 0.0
-    for rows, offset in ((d0, 0), (dm1, -1), (dp1, 1), (d2, 2)):
-        cut = pl.ds(cut_of(offset, width), width)
-        d_hidden += lax.dot_general(
-            rows[...], w_down[:, cut], CONTRACT_LAST, preferred_element_type=F32
-        )
+def backward_kernel(d2, first, gate, up, w_gate, w_up, w_down, g2, gate_out, up_out):
+    width = d2.shape[1]
+    cut = pl.ds(cut_of(2, width), width)
+    d_hidden = first[...] + lax.dot_general(
+        d2[...], w_down[:, cut], CONTRACT_LAST, preferred_element_type=F32
+    )
     gate_pre = gate[...]
     squash = jax.nn.sigmoid(gate_pre)
     d_gate = (d_hidden * up[...] * squash * (1.0 + gate_pre * (1.0 - squash))).astype(BF16)
     d_up = (d_hidden * (gate_pre * squash)).astype(BF16)
     gate_out[...] = d_gate
     up_out[...] = d_up
-    g2[...] = input_grad(d_gate, d_up, w_gate, w_up, pl.ds(cut_of(2, width), width))
+    g2[...] = input_grad(d_gate, d_up, w_gate, w_up, cut)
 
 
 def rest_kernel(d_gate, d_up, w_gate, w_up, g0, gm1, gp1):
@@ -307,17 +328,25 @@
 
     piece = struct(slots, width)
     inner = struct(slots, gate_local.shape[1], dtype=F32)
-    y0, ym1, yp1, y2, gate_pre, up_pre, weights = call(
+    gate_first, up_first, weights = call(
+        forward_first_kernel,
+        (inner, inner, struct(group_tokens, META, dtype=F32)),
+        x0, xm1, xp1, near, group, gate_local, up_local,
+        mib=16,
+    )
+    slope = struct(slots, gate_local.shape[1])
+    y2, hidden, gate_pre, up_pre = call(
         forward_kernel,
-        (piece,) * 4 + (inner,) * 2 + (struct(group_tokens, META, dtype=F32),),
-        x0, xm1, xp1, x2, near, group, gate_local, up_local, down_local,
+        (piece, slope, inner, inner),
+        x2, gate_first, up_first, gate_local, up_local, down_local,
         mib=16,
     )
-    slope = struct(slots, gate_local.shape[1])
+    y0, ym1, yp1 = call(forward_rest_kernel, (piece,) * 3, hidden, down_local, mib=16)
+    d_first = call(backward_first_kernel, inner, d0, dm1, dp1, down_local, mib=16)
     g2, d_gate, d_up = call(
         backward_kernel,
         (piece, slope, slope),
-        d0, dm1, dp1, d2, gate_pre, up_pre, gate_local, up_local, down_local,
+        d2, d_first, gate_pre, up_pre, gate_local, up_local, down_local,
         mib=16,
     )
     g0, gm1, gp1 = call(

time: 147 us -> 147 us (level)
    pallas_call x9 -> x12, Pallas kernels: 6.68 us -> 6.88 us  [call(): pl.pallas_call(kernel, out_shape=shapes, cost_estimate=pl.CostEstimate(fl...]
  transfers between devices with their start and end apart: 11 -> 11, of which waited for: 5 -> 6; matrix products, arithmetic and copies ran while one was open for 0% -> 0% of each run, Pallas kernels for 2% -> 2%
where the time goes in v7:
time: 147 us
  blocking collectives  92.1 us (63%)
  starting transfers between devices  32.1 us (22%)
  waiting for transfers between devices  14.5 us (10%)
  Pallas kernels  6.88 us (5%)
    all_to_all x1, blocking collectives, per_device(): arrived = lax.all_to_all(sent, GROUP_AXES, 0, 0)  32.4 us
    ppermute x11, starting transfers between devices, shift(): lax.ppermute(rows, 'tp', [(i, (i + places) % size) for i in range(size)])  32.1 us
    all_to_all x1, blocking collectives, per_device(): back = lax.all_to_all(summed, GROUP_AXES, 0, 0)  26.2 us
    all_to_all x1, blocking collectives, per_device(): lax.all_to_all(packed, 'tp', 0, 0).reshape(group_tokens, both + META)  19.5 us
    ppermute x11, waiting for transfers between devices, shift(): lax.ppermute(rows, 'tp', [(i, (i + places) % size) for i in range(size)])  14.5 us
    all_to_all x1, blocking collectives, per_device(): lax.all_to_all(combined.reshape(parts, count, both + META), 'tp', 0, 0)  14 us
    pallas_call x12, Pallas kernels, call(): pl.pallas_call(kernel, out_shape=shapes, cost_estimate=pl.CostEstimate(fl...  6.88 us
  transfers between devices with their start and end apart: 11, of which 6 were waited for; matrix products, arithmetic and copies ran while one was open for 0% of the time, Pallas kernels for 2%

profile of v7, /device:TPU:2, one launch (start us, length us, event | category | flops | bytes accessed | tf_op | source)
XLA Modules:
  0.0 146.7 jit_solution(1369633312846687638)
XLA Ops:
  0.6 1.8 %shard_map.121 = bf16[8,8,2176]{2,1,0:T(8,128)(2,1)} custom-call(bf16[8,4096]{1,0:T(8,128)(2,1)} %tokens.1, bf16[8,4096]{1,0:T(8,128)(2,1)} %upstream.1, s32[2,8]{1,0:T(2,128)} %bitcast.27, f32[2,8]{1,0:T(2,128)} %bitcast.28, s32[1,8]{1,0:T(1,128)} %bitcast.29, f32[1,8]{1,0:T(1,128)} %bitcast.30, f32[1,128]{1,0:T(1,128)} %bitcast.31), custom_call_target="tpu_custom_call" | custom-call | tf_op jit(solution)/shard_map/pallas_call | solution.py:270
  2.4 0.0 copy-start.1
  2.4 19.5 %all_to_all.20 = bf16[8,8,2176]{2,1,0:T(8,128)(2,1)S(1)} all-to-all(bf16[8,8,2176]{2,1,0:T(8,128)(2,1)} %shard_map.121), channel_id=1, replica_groups=mesh['dp'=8,'ctx'=8,'tp'=8] {'tp'}, dimensions={0} | all-to-all | bytes 557056 | tf_op jit(solution)/shard_map/all_to_all | solution.py:315
  21.9 0.0 copy-start
  21.9 0.7 shard_map.122
  22.6 32.4 %all_to_all.21.arrived = bf16[64,2,2176]{2,1,0:T(2,128)(2,1)S(1)} all-to-all(bf16[64,2,2176]{2,1,0:T(2,128)(2,1)S(1)} %get-tuple-element.27), channel_id=1, replica_groups=mesh['dp'=8,'ctx'=8,'tp'=8] {'dp','ctx'}, dimensions={0} | all-to-all | bytes 1114112 | tf_op jit(solution)/shard_map/all_to_all | solution.py:321
  54.9 0.1 shard_map.123
  55.0 2.5 %collective-permute-start = (bf16[128,1024]{1,0:T(8,128)(2,1)S(1)}, bf16[128,1024]{1,0:T(8,128)(2,1)S(1)}, u32[]{:S(2)}, u32[]{:S(2)}) collective-permute-start(bf16[128,1024]{1,0:T(8,128)(2,1)S(1)} %get-tuple-element.28.x0), channel_id=1, source_target_pairs={{0,1},{1,2},{2,3},{3,4},{4,5},{5,6},{6,7},{7,0},{8,9},{9,10},{10,1... | collective-permute-start | bytes 786440 | tf_op jit(solution)/shard_map/ppermute | solution.py:284
  57.5 4.6 %collective-permute-start.3 = (bf16[128,1024]{1,0:T(8,128)(2,1)S(1)}, bf16[128,1024]{1,0:T(8,128)(2,1)S(1)}, u32[]{:S(2)}, u32[]{:S(2)}) collective-permute-start(bf16[128,1024]{1,0:T(8,128)(2,1)S(1)} %get-tuple-element.34.d0), channel_id=1, source_target_pairs={{0,7},{1,0},{2,1},{3,2},{4,3},{5,4},{6,5},{7,6},{8,15},{9,8},{10,9... | collective-permute-start | bytes 786440 | tf_op jit(solution)/shard_map/ppermute | solution.py:284
  62.1 1.9 %collective-permute-start.2 = (bf16[128,1024]{1,0:T(8,128)(2,1)S(1)}, bf16[128,1024]{1,0:T(8,128)(2,1)S(1)}, u32[]{:S(2)}, u32[]{:S(2)}) collective-permute-start(bf16[128,1024]{1,0:T(8,128)(2,1)S(1)} %get-tuple-element.28.x0), channel_id=1, source_target_pairs={{0,7},{1,0},{2,1},{3,2},{4,3},{5,4},{6,5},{7,6},{8,15},{9,8},{10,9... | collective-permute-start | bytes 786440 | tf_op jit(solution)/shard_map/ppermute | solution.py:284
  64.0 1.2 collective-permute-done.xm1
  65.3 2.7 %collective-permute-start.1 = (bf16[128,1024]{1,0:T(8,128)(2,1)S(1)}, bf16[128,1024]{1,0:T(8,128)(2,1)S(1)}, u32[]{:S(2)}, u32[]{:S(2)}) collective-permute-start(bf16[128,1024]{1,0:T(8,128)(2,1)S(1)} %collective-permute-done.xm1), channel_id=1, source_target_pairs={{0,1},{1,2},{2,3},{3,4},{4,5},{5,6},{6,7},{7,0},{8,9},{9,10},{10,1... | collective-permute-start | bytes 786440 | tf_op jit(solution)/shard_map/ppermute | solution.py:284
  68.0 1.9 %collective-permute-start.5 = (bf16[128,1024]{1,0:T(8,128)(2,1)S(1)}, bf16[128,1024]{1,0:T(8,128)(2,1)S(1)}, u32[]{:S(2)}, u32[]{:S(2)}) collective-permute-start(bf16[128,1024]{1,0:T(8,128)(2,1)S(1)} %get-tuple-element.34.d0), channel_id=1, source_target_pairs={{0,1},{1,2},{2,3},{3,4},{4,5},{5,6},{6,7},{7,0},{8,9},{9,10},{10,1... | collective-permute-start | bytes 786440 | tf_op jit(solution)/shard_map/ppermute | solution.py:284
  69.9 0.0 collective-permute-done.3.dp1
  69.9 5.1 %collective-permute-start.4 = (bf16[128,1024]{1,0:T(8,128)(2,1)S(1)}, bf16[128,1024]{1,0:T(8,128)(2,1)S(1)}, u32[]{:S(2)}, u32[]{:S(2)}) collective-permute-start(bf16[128,1024]{1,0:T(8,128)(2,1)S(1)} %collective-permute-done.3.dp1), channel_id=1, source_target_pairs={{0,7},{1,0},{2,1},{3,2},{4,3},{5,4},{6,5},{7,6},{8,15},{9,8},{10,9... | collective-permute-start | bytes 786440 | tf_op jit(solution)/shard_map/ppermute | solution.py:284
  75.0 0.0 collective-permute-done.2.xp1
  75.1 0.0 copy-done.1
  75.1 0.0 copy-done
  75.1 0.0 copy-start.2
  75.1 0.6 shard_map.124
  75.7 1.7 %collective-permute-done.1.x2 = bf16[128,1024]{1,0:T(8,128)(2,1)S(1)} collective-permute-done((bf16[128,1024]{1,0:T(8,128)(2,1)S(1)}, bf16[128,1024]{1,0:T(8,128)(2,1)S(1)}, u32[]{:S(2)}, u32[]{:S(2)}) %collective-permute-start.1) | collective-permute-done | bytes 262176 | tf_op jit(solution)/shard_map/ppermute | solution.py:284
  77.4 0.0 copy-done.2
  77.4 0.5 shard_map.125
  77.9 2.1 %collective-permute-start.6 = (bf16[128,1024]{1,0:T(8,128)(2,1)S(1)}, bf16[128,1024]{1,0:T(8,128)(2,1)S(1)}, u32[]{:S(2)}, u32[]{:S(2)}) collective-permute-start(bf16[128,1024]{1,0:T(8,128)(2,1)S(1)} %get-tuple-element.41), channel_id=1, source_target_pairs={{0,7},{1,0},{2,1},{3,2},{4,3},{5,4},{6,5},{7,6},{8,15},{9,8},{10,9... | collective-permute-start | bytes 786440 | tf_op jit(solution)/shard_map/ppermute | solution.py:284
  79.9 0.3 collective-permute-done.5.dm1
  80.2 0.4 shard_map.127.first
  80.6 0.0 collective-permute-done.4.d2
  80.6 0.5 shard_map.128
  81.1 3.5 %collective-permute-start.9 = (bf16[128,1024]{1,0:T(8,128)(2,1)S(1)}, bf16[128,1024]{1,0:T(8,128)(2,1)S(1)}, u32[]{:S(2)}, u32[]{:S(2)}) collective-permute-start(bf16[128,1024]{1,0:T(8,128)(2,1)S(1)} %get-tuple-element.45), channel_id=1, source_target_pairs={{0,1},{1,2},{2,3},{3,4},{4,5},{5,6},{6,7},{7,0},{8,9},{9,10},{10,1... | collective-permute-start | bytes 786440 | tf_op jit(solution)/shard_map/ppermute | solution.py:284
  84.6 0.4 shard_map.126
  85.0 0.6 shard_map.129
  85.6 0.5 collective-permute-done.6
  86.1 0.1 add_convert_fusion.1
  86.2 4.0 %collective-permute-start.7 = (bf16[256,1024]{1,0:T(8,128)(2,1)S(1)}, bf16[256,1024]{1,0:T(8,128)(2,1)S(1)}, u32[]{:S(2)}, u32[]{:S(2)}) collective-permute-start(bf16[256,1024]{1,0:T(8,128)(2,1)S(1)} %pad_maximum_fusion), channel_id=1, source_target_pairs={{0,7},{1,0},{2,1},{3,2},{4,3},{5,4},{6,5},{7,6},{8,15},{9,8},{10,9... | collective-permute-start | bytes 1572872 | tf_op jit(solution)/shard_map/ppermute | solution.py:284
  90.3 1.9 %collective-permute-start.8 = (bf16[128,1024]{1,0:T(8,128)(2,1)S(1)}, bf16[128,1024]{1,0:T(8,128)(2,1)S(1)}, u32[]{:S(2)}, u32[]{:S(2)}) collective-permute-start(bf16[128,1024]{1,0:T(8,128)(2,1)S(1)} %get-tuple-element.43), channel_id=1, source_target_pairs={{0,1},{1,2},{2,3},{3,4},{4,5},{5,6},{6,7},{7,0},{8,9},{9,10},{10,1... | collective-permute-start | bytes 786440 | tf_op jit(solution)/shard_map/ppermute | solution.py:284
  92.2 0.0 collective-permute-done.9
  92.2 0.1 add_convert_fusion
  92.3 1.9 %collective-permute-start.10 = (bf16[128,1024]{1,0:T(8,128)(2,1)S(1)}, bf16[128,1024]{1,0:T(8,128)(2,1)S(1)}, u32[]{:S(2)}, u32[]{:S(2)}) collective-permute-start(bf16[128,1024]{1,0:T(8,128)(2,1)S(1)} %add_convert_fusion), channel_id=1, source_target_pairs={{0,1},{1,2},{2,3},{3,4},{4,5},{5,6},{6,7},{7,0},{8,9},{9,10},{10,1... | collective-permute-start | bytes 786440 | tf_op jit(solution)/shard_map/ppermute | solution.py:284
  94.2 7.9 %collective-permute-done.8.y_right = bf16[128,1024]{1,0:T(8,128)(2,1)S(1)} collective-permute-done((bf16[128,1024]{1,0:T(8,128)(2,1)S(1)}, bf16[128,1024]{1,0:T(8,128)(2,1)S(1)}, u32[]{:S(2)}, u32[]{:S(2)}) %collective-permute-start.8) | collective-permute-done | bytes 262176 | tf_op jit(solution)/shard_map/ppermute | solution.py:284
  102.1 2.8 %collective-permute-done.10.g_right = bf16[128,1024]{1,0:T(8,128)(2,1)S(1)} collective-permute-done((bf16[128,1024]{1,0:T(8,128)(2,1)S(1)}, bf16[128,1024]{1,0:T(8,128)(2,1)S(1)}, u32[]{:S(2)}, u32[]{:S(2)}) %collective-permute-start.10) | collective-permute-done | bytes 262176 | tf_op jit(solution)/shard_map/ppermute | solution.py:284
  104.9 0.0 collective-permute-done.7.left
  104.9 0.3 shard_map.130
  105.1 26.2 %all_to_all.22.back = bf16[64,2,2048]{2,1,0:T(2,128)(2,1)S(1)} all-to-all(bf16[64,2,2048]{2,1,0:T(2,128)(2,1)S(1)} %shard_map.130), channel_id=1, replica_groups=mesh['dp'=8,'ctx'=8,'tp'=8] {'dp','ctx'}, dimensions={0} | all-to-all | bytes 1048576 | tf_op jit(solution)/shard_map/all_to_all | solution.py:360
  131.4 0.5 shard_map.131
  131.9 14.0 %all_to_all.23.arrived = bf16[8,8,2176]{2,1,0:T(8,128)(2,1)S(1)} all-to-all(bf16[8,8,2176]{2,1,0:T(8,128)(2,1)S(1)} %bitcast.26), channel_id=1, replica_groups=mesh['dp'=8,'ctx'=8,'tp'=8] {'tp'}, dimensions={0} | all-to-all | bytes 557056 | tf_op jit(solution)/shard_map/all_to_all | solution.py:369
  145.9 0.7 shard_map.132
  (1 shorter events, 0.0 us)
Async XLA Ops:
  2.4 72.6 %copy-start.1 = (bf16[1,4096,128]{2,1,0:T(8,128)(2,1)S(1)}, bf16[1,4096,128]{2,1,0:T(8,128)(2,1)}, u32[]{:S(2)}) copy-start(bf16[1,4096,128]{2,1,0:T(8,128)(2,1)} %param.18) | copy-start | bytes 3145732
  21.9 53.2 %copy-start = (bf16[1,4096,128]{2,1,0:T(8,128)(2,1)S(1)}, bf16[1,4096,128]{2,1,0:T(8,128)(2,1)}, u32[]{:S(2)}) copy-start(bf16[1,4096,128]{2,1,0:T(8,128)(2,1)} %param.17) | copy-start | bytes 3145732
  55.0 10.2 %collective-permute-start = (bf16[128,1024]{1,0:T(8,128)(2,1)S(1)}, bf16[128,1024]{1,0:T(8,128)(2,1)S(1)}, u32[]{:S(2)}, u32[]{:S(2)}) collective-permute-start(bf16[128,1024]{1,0:T(8,128)(2,1)S(1)} %get-tuple-element.28.x0), channel_id=1, source_target_pairs={{0,1},{1,2},{2,3},{3,4},{4,5},{5,6},{6,7},{7,0},{8,9},{9,10},{10,1... | collective-permute-start | bytes 786440 | tf_op jit(solution)/shard_map/ppermute | solution.py:284
  57.5 12.4 %collective-permute-start.3 = (bf16[128,1024]{1,0:T(8,128)(2,1)S(1)}, bf16[128,1024]{1,0:T(8,128)(2,1)S(1)}, u32[]{:S(2)}, u32[]{:S(2)}) collective-permute-start(bf16[128,1024]{1,0:T(8,128)(2,1)S(1)} %get-tuple-element.34.d0), channel_id=1, source_target_pairs={{0,7},{1,0},{2,1},{3,2},{4,3},{5,4},{6,5},{7,6},{8,15},{9,8},{10,9... | collective-permute-start | bytes 786440 | tf_op jit(solution)/shard_map/ppermute | solution.py:284
  62.1 13.0 %collective-permute-start.2 = (bf16[128,1024]{1,0:T(8,128)(2,1)S(1)}, bf16[128,1024]{1,0:T(8,128)(2,1)S(1)}, u32[]{:S(2)}, u32[]{:S(2)}) collective-permute-start(bf16[128,1024]{1,0:T(8,128)(2,1)S(1)} %get-tuple-element.28.x0), channel_id=1, source_target_pairs={{0,7},{1,0},{2,1},{3,2},{4,3},{5,4},{6,5},{7,6},{8,15},{9,8},{10,9... | collective-permute-start | bytes 786440 | tf_op jit(solution)/shard_map/ppermute | solution.py:284
  65.3 12.1 %collective-permute-start.1 = (bf16[128,1024]{1,0:T(8,128)(2,1)S(1)}, bf16[128,1024]{1,0:T(8,128)(2,1)S(1)}, u32[]{:S(2)}, u32[]{:S(2)}) collective-permute-start(bf16[128,1024]{1,0:T(8,128)(2,1)S(1)} %collective-permute-done.xm1), channel_id=1, source_target_pairs={{0,1},{1,2},{2,3},{3,4},{4,5},{5,6},{6,7},{7,0},{8,9},{9,10},{10,1... | collective-permute-start | bytes 786440 | tf_op jit(solution)/shard_map/ppermute | solution.py:284
  68.0 12.2 %collective-permute-start.5 = (bf16[128,1024]{1,0:T(8,128)(2,1)S(1)}, bf16[128,1024]{1,0:T(8,128)(2,1)S(1)}, u32[]{:S(2)}, u32[]{:S(2)}) collective-permute-start(bf16[128,1024]{1,0:T(8,128)(2,1)S(1)} %get-tuple-element.34.d0), channel_id=1, source_target_pairs={{0,1},{1,2},{2,3},{3,4},{4,5},{5,6},{6,7},{7,0},{8,9},{9,10},{10,1... | collective-permute-start | bytes 786440 | tf_op jit(solution)/shard_map/ppermute | solution.py:284
  69.9 10.7 %collective-permute-start.4 = (bf16[128,1024]{1,0:T(8,128)(2,1)S(1)}, bf16[128,1024]{1,0:T(8,128)(2,1)S(1)}, u32[]{:S(2)}, u32[]{:S(2)}) collective-permute-start(bf16[128,1024]{1,0:T(8,128)(2,1)S(1)} %collective-permute-done.3.dp1), channel_id=1, source_target_pairs={{0,7},{1,0},{2,1},{3,2},{4,3},{5,4},{6,5},{7,6},{8,15},{9,8},{10,9... | collective-permute-start | bytes 786440 | tf_op jit(solution)/shard_map/ppermute | solution.py:284
  75.1 2.3 %copy-start.2 = (bf16[1,128,4096]{2,1,0:T(8,128)(2,1)S(1)}, bf16[1,128,4096]{2,1,0:T(8,128)(2,1)}, u32[]{:S(2)}) copy-start(bf16[1,128,4096]{2,1,0:T(8,128)(2,1)} %param.19) | copy-start | bytes 3145732
  77.9 8.3 %collective-permute-start.6 = (bf16[128,1024]{1,0:T(8,128)(2,1)S(1)}, bf16[128,1024]{1,0:T(8,128)(2,1)S(1)}, u32[]{:S(2)}, u32[]{:S(2)}) collective-permute-start(bf16[128,1024]{1,0:T(8,128)(2,1)S(1)} %get-tuple-element.41), channel_id=1, source_target_pairs={{0,7},{1,0},{2,1},{3,2},{4,3},{5,4},{6,5},{7,6},{8,15},{9,8},{10,9... | collective-permute-start | bytes 786440 | tf_op jit(solution)/shard_map/ppermute | solution.py:284
  81.1 11.1 %collective-permute-start.9 = (bf16[128,1024]{1,0:T(8,128)(2,1)S(1)}, bf16[128,1024]{1,0:T(8,128)(2,1)S(1)}, u32[]{:S(2)}, u32[]{:S(2)}) collective-permute-start(bf16[128,1024]{1,0:T(8,128)(2,1)S(1)} %get-tuple-element.45), channel_id=1, source_target_pairs={{0,1},{1,2},{2,3},{3,4},{4,5},{5,6},{6,7},{7,0},{8,9},{9,10},{10,1... | collective-permute-start | bytes 786440 | tf_op jit(solution)/shard_map/ppermute | solution.py:284
  86.2 18.6 %collective-permute-start.7 = (bf16[256,1024]{1,0:T(8,128)(2,1)S(1)}, bf16[256,1024]{1,0:T(8,128)(2,1)S(1)}, u32[]{:S(2)}, u32[]{:S(2)}) collective-permute-start(bf16[256,1024]{1,0:T(8,128)(2,1)S(1)} %pad_maximum_fusion), channel_id=1, source_target_pairs={{0,7},{1,0},{2,1},{3,2},{4,3},{5,4},{6,5},{7,6},{8,15},{9,8},{10,9... | collective-permute-start | bytes 1572872 | tf_op jit(solution)/shard_map/ppermute | solution.py:284
  90.3 11.8 %collective-permute-start.8 = (bf16[128,1024]{1,0:T(8,128)(2,1)S(1)}, bf16[128,1024]{1,0:T(8,128)(2,1)S(1)}, u32[]{:S(2)}, u32[]{:S(2)}) collective-permute-start(bf16[128,1024]{1,0:T(8,128)(2,1)S(1)} %get-tuple-element.43), channel_id=1, source_target_pairs={{0,1},{1,2},{2,3},{3,4},{4,5},{5,6},{6,7},{7,0},{8,9},{9,10},{10,1... | collective-permute-start | bytes 786440 | tf_op jit(solution)/shard_map/ppermute | solution.py:284
  92.3 12.6 %collective-permute-start.10 = (bf16[128,1024]{1,0:T(8,128)(2,1)S(1)}, bf16[128,1024]{1,0:T(8,128)(2,1)S(1)}, u32[]{:S(2)}, u32[]{:S(2)}) collective-permute-start(bf16[128,1024]{1,0:T(8,128)(2,1)S(1)} %add_convert_fusion), channel_id=1, source_target_pairs={{0,1},{1,2},{2,3},{3,4},{4,5},{5,6},{6,7},{7,0},{8,9},{9,10},{10,1... | collective-permute-start | bytes 786440 | tf_op jit(solution)/shard_map/ppermute | solution.py:284

commit v8 on v6

--- a/solution.py
+++ b/solution.py
@@ -134,6 +134,11 @@
     return own * jnp.minimum(jnp.exp(total / tally), CLIP_HIGH)
 
 
+def hold_kernel(rows, earlier, out):
+    del earlier
+    out[...] = rows[...]
+
+
 def cut_of(offset, width):
     return pl.multiple_of((lax.axis_index("tp") + offset + CUTS) % CUTS * width, width)
 
@@ -302,8 +307,9 @@
         arrive_kernel, (struct(slots, width), struct(slots, width), struct(slots, META)), arrived
     )
     xm1, dp1 = shift(x0, 1), shift(d0, -1)
-    xp1, dm1 = shift(x0, -1), shift(d0, 1)
+    xp1 = shift(x0, -1)
     x2, d2 = shift(xm1, 1), shift(dp1, -1)
+    dm1 = shift(call(hold_kernel, struct(slots, width), d0, dp1), 1)
 
     piece = struct(slots, width)
     inner = struct(slots, gate_local.shape[1], dtype=F32)

time: 147 us -> 147 us (level)
    pallas_call x9 -> x10, Pallas kernels: 6.68 us -> 6.68 us  [call(): pl.pallas_call(kernel, out_shape=shapes, cost_estimate=pl.CostEstimate(fl...]
  transfers between devices with their start and end apart: 11 -> 11, of which waited for: 5 -> 8; matrix products, arithmetic and copies ran while one was open for 0% -> 0% of each run, Pallas kernels for 2% -> 2%
where the time goes in v8:
time: 147 us
  blocking collectives  92.4 us (63%)
  starting transfers between devices  32.8 us (22%)
  waiting for transfers between devices  13.6 us (9%)
  Pallas kernels  6.68 us (5%)
    ppermute x11, starting transfers between devices, shift(): lax.ppermute(rows, 'tp', [(i, (i + places) % size) for i in range(size)])  32.8 us
    all_to_all x1, blocking collectives, per_device(): arrived = lax.all_to_all(sent, GROUP_AXES, 0, 0)  32.5 us
    all_to_all x1, blocking collectives, per_device(): back = lax.all_to_all(summed, GROUP_AXES, 0, 0)  26.4 us
    all_to_all x1, blocking collectives, per_device(): lax.all_to_all(packed, 'tp', 0, 0).reshape(group_tokens, both + META)  19.5 us
    all_to_all x1, blocking collectives, per_device(): lax.all_to_all(combined.reshape(parts, count, both + META), 'tp', 0, 0)  14 us
    ppermute x11, waiting for transfers between devices, shift(): lax.ppermute(rows, 'tp', [(i, (i + places) % size) for i in range(size)])  13.6 us
    pallas_call x10, Pallas kernels, call(): pl.pallas_call(kernel, out_shape=shapes, cost_estimate=pl.CostEstimate(fl...  6.68 us
  transfers between devices with their start and end apart: 11, of which 8 were waited for; matrix products, arithmetic and copies ran while one was open for 0% of the time, Pallas kernels for 2%

profile of v8, /device:TPU:2, one launch (start us, length us, event | category | flops | bytes accessed | tf_op | source)
XLA Modules:
  0.0 146.5 jit_solution(15709445311734949015)
XLA Ops:
  0.6 1.8 %shard_map.121 = bf16[8,8,2176]{2,1,0:T(8,128)(2,1)} custom-call(bf16[8,4096]{1,0:T(8,128)(2,1)} %tokens.1, bf16[8,4096]{1,0:T(8,128)(2,1)} %upstream.1, s32[2,8]{1,0:T(2,128)} %bitcast.23, f32[2,8]{1,0:T(2,128)} %bitcast.24, s32[1,8]{1,0:T(1,128)} %bitcast.25, f32[1,8]{1,0:T(1,128)} %bitcast.26, f32[1,128]{1,0:T(1,128)} %bitcast.27), custom_call_target="tpu_custom_call" | custom-call | tf_op jit(solution)/shard_map/pallas_call | solution.py:254
  2.4 0.0 copy-start.2
  2.4 19.5 %all_to_all.20 = bf16[8,8,2176]{2,1,0:T(8,128)(2,1)S(1)} all-to-all(bf16[8,8,2176]{2,1,0:T(8,128)(2,1)} %shard_map.121), channel_id=1, replica_groups=mesh['dp'=8,'ctx'=8,'tp'=8] {'tp'}, dimensions={0} | all-to-all | bytes 557056 | tf_op jit(solution)/shard_map/all_to_all | solution.py:299
  21.9 0.7 shard_map.122
  22.6 0.0 copy-start
  22.6 0.0 copy-start.1
  22.6 32.5 %all_to_all.21.arrived = bf16[64,2,2176]{2,1,0:T(2,128)(2,1)S(1)} all-to-all(bf16[64,2,2176]{2,1,0:T(2,128)(2,1)S(1)} %get-tuple-element.24), channel_id=1, replica_groups=mesh['dp'=8,'ctx'=8,'tp'=8] {'dp','ctx'}, dimensions={0} | all-to-all | bytes 1114112 | tf_op jit(solution)/shard_map/all_to_all | solution.py:305
  55.1 0.1 shard_map.123
  55.2 2.5 %collective-permute-start = (bf16[128,1024]{1,0:T(8,128)(2,1)S(1)}, bf16[128,1024]{1,0:T(8,128)(2,1)S(1)}, u32[]{:S(2)}, u32[]{:S(2)}) collective-permute-start(bf16[128,1024]{1,0:T(8,128)(2,1)S(1)} %get-tuple-element.25.x0), channel_id=1, source_target_pairs={{0,1},{1,2},{2,3},{3,4},{4,5},{5,6},{6,7},{7,0},{8,9},{9,10},{10,1... | collective-permute-start | bytes 786440 | tf_op jit(solution)/shard_map/ppermute | solution.py:268
  57.7 4.6 %collective-permute-start.3 = (bf16[128,1024]{1,0:T(8,128)(2,1)S(1)}, bf16[128,1024]{1,0:T(8,128)(2,1)S(1)}, u32[]{:S(2)}, u32[]{:S(2)}) collective-permute-start(bf16[128,1024]{1,0:T(8,128)(2,1)S(1)} %get-tuple-element.28.rows.d0), channel_id=1, source_target_pairs={{0,7},{1,0},{2,1},{3,2},{4,3},{5,4},{6,5},{7,6},{8,15},{9,8},{10,9... | collective-permute-start | bytes 786440 | tf_op jit(solution)/shard_map/ppermute | solution.py:268
  62.3 1.9 %collective-permute-start.1 = (bf16[128,1024]{1,0:T(8,128)(2,1)S(1)}, bf16[128,1024]{1,0:T(8,128)(2,1)S(1)}, u32[]{:S(2)}, u32[]{:S(2)}) collective-permute-start(bf16[128,1024]{1,0:T(8,128)(2,1)S(1)} %get-tuple-element.25.x0), channel_id=1, source_target_pairs={{0,7},{1,0},{2,1},{3,2},{4,3},{5,4},{6,5},{7,6},{8,15},{9,8},{10,9... | collective-permute-start | bytes 786440 | tf_op jit(solution)/shard_map/ppermute | solution.py:268
  64.2 1.2 collective-permute-done.xm1
  65.4 2.7 %collective-permute-start.2 = (bf16[128,1024]{1,0:T(8,128)(2,1)S(1)}, bf16[128,1024]{1,0:T(8,128)(2,1)S(1)}, u32[]{:S(2)}, u32[]{:S(2)}) collective-permute-start(bf16[128,1024]{1,0:T(8,128)(2,1)S(1)} %collective-permute-done.xm1), channel_id=1, source_target_pairs={{0,1},{1,2},{2,3},{3,4},{4,5},{5,6},{6,7},{7,0},{8,9},{9,10},{10,1... | collective-permute-start | bytes 786440 | tf_op jit(solution)/shard_map/ppermute | solution.py:268
  68.1 0.9 collective-permute-done.3.earlier.dp1
  69.0 2.3 %collective-permute-start.4 = (bf16[128,1024]{1,0:T(8,128)(2,1)S(1)}, bf16[128,1024]{1,0:T(8,128)(2,1)S(1)}, u32[]{:S(2)}, u32[]{:S(2)}) collective-permute-start(bf16[128,1024]{1,0:T(8,128)(2,1)S(1)} %shard_map.125), channel_id=1, source_target_pairs={{0,1},{1,2},{2,3},{3,4},{4,5},{5,6},{6,7},{7,0},{8,9},{9,10},{10,1... | collective-permute-start | bytes 786440 | tf_op jit(solution)/shard_map/ppermute | solution.py:268
  71.3 5.3 %collective-permute-start.5 = (bf16[128,1024]{1,0:T(8,128)(2,1)S(1)}, bf16[128,1024]{1,0:T(8,128)(2,1)S(1)}, u32[]{:S(2)}, u32[]{:S(2)}) collective-permute-start(bf16[128,1024]{1,0:T(8,128)(2,1)S(1)} %collective-permute-done.3.earlier.dp1), channel_id=1, source_target_pairs={{0,7},{1,0},{2,1},{3,2},{4,3},{5,4},{6,5},{7,6},{8,15},{9,8},{10,9... | collective-permute-start | bytes 786440 | tf_op jit(solution)/shard_map/ppermute | solution.py:268
  76.5 0.0 collective-permute-done.1.xp1
  76.6 1.0 collective-permute-done.2.x2
  77.6 0.0 copy-done.2
  77.6 0.0 copy-done
  77.6 0.0 copy-done.1
  77.6 1.1 shard_map.124
  78.7 3.0 %collective-permute-start.6 = (bf16[128,1024]{1,0:T(8,128)(2,1)S(1)}, bf16[128,1024]{1,0:T(8,128)(2,1)S(1)}, u32[]{:S(2)}, u32[]{:S(2)}) collective-permute-start(bf16[128,1024]{1,0:T(8,128)(2,1)S(1)} %get-tuple-element.35), channel_id=1, source_target_pairs={{0,7},{1,0},{2,1},{3,2},{4,3},{5,4},{6,5},{7,6},{8,15},{9,8},{10,9... | collective-permute-start | bytes 786440 | tf_op jit(solution)/shard_map/ppermute | solution.py:268
  81.6 0.0 collective-permute-done.4.dm1
  81.7 0.8 collective-permute-done.5.d2
  82.4 0.9 shard_map.126
  83.3 2.3 %collective-permute-start.9 = (bf16[128,1024]{1,0:T(8,128)(2,1)S(1)}, bf16[128,1024]{1,0:T(8,128)(2,1)S(1)}, u32[]{:S(2)}, u32[]{:S(2)}) collective-permute-start(bf16[128,1024]{1,0:T(8,128)(2,1)S(1)} %get-tuple-element.39), channel_id=1, source_target_pairs={{0,1},{1,2},{2,3},{3,4},{4,5},{5,6},{6,7},{7,0},{8,9},{9,10},{10,1... | collective-permute-start | bytes 786440 | tf_op jit(solution)/shard_map/ppermute | solution.py:268
  85.7 0.6 shard_map.127
  86.3 0.7 collective-permute-done.6
  87.0 0.1 add_convert_fusion.1
  87.1 4.5 %collective-permute-start.7 = (bf16[256,1024]{1,0:T(8,128)(2,1)S(1)}, bf16[256,1024]{1,0:T(8,128)(2,1)S(1)}, u32[]{:S(2)}, u32[]{:S(2)}) collective-permute-start(bf16[256,1024]{1,0:T(8,128)(2,1)S(1)} %pad_maximum_fusion), channel_id=1, source_target_pairs={{0,7},{1,0},{2,1},{3,2},{4,3},{5,4},{6,5},{7,6},{8,15},{9,8},{10,9... | collective-permute-start | bytes 1572872 | tf_op jit(solution)/shard_map/ppermute | solution.py:268
  91.6 1.9 %collective-permute-start.8 = (bf16[128,1024]{1,0:T(8,128)(2,1)S(1)}, bf16[128,1024]{1,0:T(8,128)(2,1)S(1)}, u32[]{:S(2)}, u32[]{:S(2)}) collective-permute-start(bf16[128,1024]{1,0:T(8,128)(2,1)S(1)} %get-tuple-element.37), channel_id=1, source_target_pairs={{0,1},{1,2},{2,3},{3,4},{4,5},{5,6},{6,7},{7,0},{8,9},{9,10},{10,1... | collective-permute-start | bytes 786440 | tf_op jit(solution)/shard_map/ppermute | solution.py:268
  93.5 0.1 collective-permute-done.9
  93.6 0.1 add_convert_fusion
  93.7 1.9 %collective-permute-start.10 = (bf16[128,1024]{1,0:T(8,128)(2,1)S(1)}, bf16[128,1024]{1,0:T(8,128)(2,1)S(1)}, u32[]{:S(2)}, u32[]{:S(2)}) collective-permute-start(bf16[128,1024]{1,0:T(8,128)(2,1)S(1)} %add_convert_fusion), channel_id=1, source_target_pairs={{0,1},{1,2},{2,3},{3,4},{4,5},{5,6},{6,7},{7,0},{8,9},{9,10},{10,1... | collective-permute-start | bytes 786440 | tf_op jit(solution)/shard_map/ppermute | solution.py:268
  95.6 6.1 %collective-permute-done.8.y_right = bf16[128,1024]{1,0:T(8,128)(2,1)S(1)} collective-permute-done((bf16[128,1024]{1,0:T(8,128)(2,1)S(1)}, bf16[128,1024]{1,0:T(8,128)(2,1)S(1)}, u32[]{:S(2)}, u32[]{:S(2)}) %collective-permute-start.8) | collective-permute-done | bytes 262176 | tf_op jit(solution)/shard_map/ppermute | solution.py:268
  101.7 2.8 %collective-permute-done.10.g_right = bf16[128,1024]{1,0:T(8,128)(2,1)S(1)} collective-permute-done((bf16[128,1024]{1,0:T(8,128)(2,1)S(1)}, bf16[128,1024]{1,0:T(8,128)(2,1)S(1)}, u32[]{:S(2)}, u32[]{:S(2)}) %collective-permute-start.10) | collective-permute-done | bytes 262176 | tf_op jit(solution)/shard_map/ppermute | solution.py:268
  104.5 0.0 collective-permute-done.7.left
  104.5 0.3 shard_map.128
  104.8 26.4 %all_to_all.22.back = bf16[64,2,2048]{2,1,0:T(2,128)(2,1)S(1)} all-to-all(bf16[64,2,2048]{2,1,0:T(2,128)(2,1)S(1)} %shard_map.128), channel_id=1, replica_groups=mesh['dp'=8,'ctx'=8,'tp'=8] {'dp','ctx'}, dimensions={0} | all-to-all | bytes 1048576 | tf_op jit(solution)/shard_map/all_to_all | solution.py:337
  131.2 0.5 shard_map.129
  131.7 14.0 %all_to_all.23.arrived = bf16[8,8,2176]{2,1,0:T(8,128)(2,1)S(1)} all-to-all(bf16[8,8,2176]{2,1,0:T(8,128)(2,1)S(1)} %bitcast.22), channel_id=1, replica_groups=mesh['dp'=8,'ctx'=8,'tp'=8] {'tp'}, dimensions={0} | all-to-all | bytes 557056 | tf_op jit(solution)/shard_map/all_to_all | solution.py:346
  145.8 0.7 shard_map.130
  (2 shorter events, 0.1 us)
Async XLA Ops:
  2.4 75.1 %copy-start.2 = (bf16[1,128,4096]{2,1,0:T(8,128)(2,1)S(1)}, bf16[1,128,4096]{2,1,0:T(8,128)(2,1)}, u32[]{:S(2)}) copy-start(bf16[1,128,4096]{2,1,0:T(8,128)(2,1)} %param.19) | copy-start | bytes 3145732
  22.6 55.0 %copy-start = (bf16[1,4096,128]{2,1,0:T(8,128)(2,1)S(1)}, bf16[1,4096,128]{2,1,0:T(8,128)(2,1)}, u32[]{:S(2)}) copy-start(bf16[1,4096,128]{2,1,0:T(8,128)(2,1)} %param.17) | copy-start | bytes 3145732
  22.6 55.0 %copy-start.1 = (bf16[1,4096,128]{2,1,0:T(8,128)(2,1)S(1)}, bf16[1,4096,128]{2,1,0:T(8,128)(2,1)}, u32[]{:S(2)}) copy-start(bf16[1,4096,128]{2,1,0:T(8,128)(2,1)} %param.18) | copy-start | bytes 3145732
  55.2 10.2 %collective-permute-start = (bf16[128,1024]{1,0:T(8,128)(2,1)S(1)}, bf16[128,1024]{1,0:T(8,128)(2,1)S(1)}, u32[]{:S(2)}, u32[]{:S(2)}) collective-permute-start(bf16[128,1024]{1,0:T(8,128)(2,1)S(1)} %get-tuple-element.25.x0), channel_id=1, source_target_pairs={{0,1},{1,2},{2,3},{3,4},{4,5},{5,6},{6,7},{7,0},{8,9},{9,10},{10,1... | collective-permute-start | bytes 786440 | tf_op jit(solution)/shard_map/ppermute | solution.py:268
  57.7 11.3 %collective-permute-start.3 = (bf16[128,1024]{1,0:T(8,128)(2,1)S(1)}, bf16[128,1024]{1,0:T(8,128)(2,1)S(1)}, u32[]{:S(2)}, u32[]{:S(2)}) collective-permute-start(bf16[128,1024]{1,0:T(8,128)(2,1)S(1)} %get-tuple-element.28.rows.d0), channel_id=1, source_target_pairs={{0,7},{1,0},{2,1},{3,2},{4,3},{5,4},{6,5},{7,6},{8,15},{9,8},{10,9... | collective-permute-start | bytes 786440 | tf_op jit(solution)/shard_map/ppermute | solution.py:268
  62.3 14.3 %collective-permute-start.1 = (bf16[128,1024]{1,0:T(8,128)(2,1)S(1)}, bf16[128,1024]{1,0:T(8,128)(2,1)S(1)}, u32[]{:S(2)}, u32[]{:S(2)}) collective-permute-start(bf16[128,1024]{1,0:T(8,128)(2,1)S(1)} %get-tuple-element.25.x0), channel_id=1, source_target_pairs={{0,7},{1,0},{2,1},{3,2},{4,3},{5,4},{6,5},{7,6},{8,15},{9,8},{10,9... | collective-permute-start | bytes 786440 | tf_op jit(solution)/shard_map/ppermute | solution.py:268
  65.4 12.1 %collective-permute-start.2 = (bf16[128,1024]{1,0:T(8,128)(2,1)S(1)}, bf16[128,1024]{1,0:T(8,128)(2,1)S(1)}, u32[]{:S(2)}, u32[]{:S(2)}) collective-permute-start(bf16[128,1024]{1,0:T(8,128)(2,1)S(1)} %collective-permute-done.xm1), channel_id=1, source_target_pairs={{0,1},{1,2},{2,3},{3,4},{4,5},{5,6},{6,7},{7,0},{8,9},{9,10},{10,1... | collective-permute-start | bytes 786440 | tf_op jit(solution)/shard_map/ppermute | solution.py:268
  69.0 12.6 %collective-permute-start.4 = (bf16[128,1024]{1,0:T(8,128)(2,1)S(1)}, bf16[128,1024]{1,0:T(8,128)(2,1)S(1)}, u32[]{:S(2)}, u32[]{:S(2)}) collective-permute-start(bf16[128,1024]{1,0:T(8,128)(2,1)S(1)} %shard_map.125), channel_id=1, source_target_pairs={{0,1},{1,2},{2,3},{3,4},{4,5},{5,6},{6,7},{7,0},{8,9},{9,10},{10,1... | collective-permute-start | bytes 786440 | tf_op jit(solution)/shard_map/ppermute | solution.py:268
  71.3 11.1 %collective-permute-start.5 = (bf16[128,1024]{1,0:T(8,128)(2,1)S(1)}, bf16[128,1024]{1,0:T(8,128)(2,1)S(1)}, u32[]{:S(2)}, u32[]{:S(2)}) collective-permute-start(bf16[128,1024]{1,0:T(8,128)(2,1)S(1)} %collective-permute-done.3.earlier.dp1), channel_id=1, source_target_pairs={{0,7},{1,0},{2,1},{3,2},{4,3},{5,4},{6,5},{7,6},{8,15},{9,8},{10,9... | collective-permute-start | bytes 786440 | tf_op jit(solution)/shard_map/ppermute | solution.py:268
  78.7 8.4 %collective-permute-start.6 = (bf16[128,1024]{1,0:T(8,128)(2,1)S(1)}, bf16[128,1024]{1,0:T(8,128)(2,1)S(1)}, u32[]{:S(2)}, u32[]{:S(2)}) collective-permute-start(bf16[128,1024]{1,0:T(8,128)(2,1)S(1)} %get-tuple-element.35), channel_id=1, source_target_pairs={{0,7},{1,0},{2,1},{3,2},{4,3},{5,4},{6,5},{7,6},{8,15},{9,8},{10,9... | collective-permute-start | bytes 786440 | tf_op jit(solution)/shard_map/ppermute | solution.py:268
  83.3 10.3 %collective-permute-start.9 = (bf16[128,1024]{1,0:T(8,128)(2,1)S(1)}, bf16[128,1024]{1,0:T(8,128)(2,1)S(1)}, u32[]{:S(2)}, u32[]{:S(2)}) collective-permute-start(bf16[128,1024]{1,0:T(8,128)(2,1)S(1)} %get-tuple-element.39), channel_id=1, source_target_pairs={{0,1},{1,2},{2,3},{3,4},{4,5},{5,6},{6,7},{7,0},{8,9},{9,10},{10,1... | collective-permute-start | bytes 786440 | tf_op jit(solution)/shard_map/ppermute | solution.py:268
  87.1 17.4 %collective-permute-start.7 = (bf16[256,1024]{1,0:T(8,128)(2,1)S(1)}, bf16[256,1024]{1,0:T(8,128)(2,1)S(1)}, u32[]{:S(2)}, u32[]{:S(2)}) collective-permute-start(bf16[256,1024]{1,0:T(8,128)(2,1)S(1)} %pad_maximum_fusion), channel_id=1, source_target_pairs={{0,7},{1,0},{2,1},{3,2},{4,3},{5,4},{6,5},{7,6},{8,15},{9,8},{10,9... | collective-permute-start | bytes 1572872 | tf_op jit(solution)/shard_map/ppermute | solution.py:268
  91.6 10.1 %collective-permute-start.8 = (bf16[128,1024]{1,0:T(8,128)(2,1)S(1)}, bf16[128,1024]{1,0:T(8,128)(2,1)S(1)}, u32[]{:S(2)}, u32[]{:S(2)}) collective-permute-start(bf16[128,1024]{1,0:T(8,128)(2,1)S(1)} %get-tuple-element.37), channel_id=1, source_target_pairs={{0,1},{1,2},{2,3},{3,4},{4,5},{5,6},{6,7},{7,0},{8,9},{9,10},{10,1... | collective-permute-start | bytes 786440 | tf_op jit(solution)/shard_map/ppermute | solution.py:268
  93.7 10.8 %collective-permute-start.10 = (bf16[128,1024]{1,0:T(8,128)(2,1)S(1)}, bf16[128,1024]{1,0:T(8,128)(2,1)S(1)}, u32[]{:S(2)}, u32[]{:S(2)}) collective-permute-start(bf16[128,1024]{1,0:T(8,128)(2,1)S(1)} %add_convert_fusion), channel_id=1, source_target_pairs={{0,1},{1,2},{2,3},{3,4},{4,5},{5,6},{6,7},{7,0},{8,9},{9,10},{10,1... | collective-permute-start | bytes 786440 | tf_op jit(solution)/shard_map/ppermute | solution.py:268
